TPU v7x, 32 devices: a whole 2x2x4 slice. The times are simulated.
32 devices in a mesh: grp: 4 (over x, core), dev: 8 (over z, y).
Axes of the slice: x: 2, y: 2, z: 4, core: 2. Of those that a mesh axis runs over, the one named last changes fastest.
Arguments:
- amplitudes: bfloat16 [32, 128, 128], P(('grp', 'dev')), may hold values from -2 to 2
- bases: bfloat16 [32, 256, 128], P(('grp', 'dev')), may hold values from -0.375 to 0.375
- factors: bfloat16 [32, 32, 256, 256], P(('grp', 'dev')), may hold values from -0.1875 to 0.1875
- intersections: bfloat16 [32, 4, 128, 128], P(('grp', 'dev')), may hold values from -0.25 to 0.25
- pair_integrals: float32 [32, 128, 128], P(('grp', 'dev')), may hold values from -6 to 6
- pno_energies: float32 [32, 128], P(('grp', 'dev')), may hold values from 0.3 to 3
- pair_shift: float32 [32], P(('grp', 'dev')), may hold values from 0.5 to 4
- pair_atoms: int32 [32, 2], P('grp'), may hold values from 0 to 7, all different within a row; in each aligned block of 8 rows (0 to 7, 8 to 15, ...) at most 3 rows name the same one
- pair_next: int32 [32, 4], P(('grp', 'dev')), may hold values from 0 to 15, as said below
Outputs:
- new_amplitudes: float32 [32, 128, 128], P(('grp', 'dev'))
Inputs may be any that keep to these rules, and one draw needn't show every extreme that they name: `pair_atoms`: each pair lists 2 different atoms of its own group. Within a group no atom is listed by more than 3 pairs, and some atom is listed by exactly 3 pairs of its group. `pair_next`: each pair lists 4 different pairs other than itself; a number below 8 is a pair of its own group, a number m from 8 on is pair m - 8 of the next group. Pairs of the last group list only pairs of their own group.
All inputs are finite; a program needn't handle non-finite values.
Results may differ from a plain program's by a relative error of at most 0.008.
Values may be sent and summed in bfloat16 or wider, within the bound.
No kernel may reach another device: no remote copies, remote signals or barrier semaphores. Data moves between devices by JAX's collectives and lax.ppermute only.
A program may use at most 128 MiB of HBM per device.

v0:
```python
import jax
import jax.numpy as jnp
from jax import lax
from jax.experimental import pallas as pl
from jax.experimental.pallas import tpu as pltpu
from jax.sharding import PartitionSpec as P

CAP = 3
ITERS = 2
F32 = jnp.float32
BF16 = jnp.bfloat16
CONTRACT_LAST = (((1,), (1,)), ((), ()))


def vmem_spec():
    return pl.BlockSpec(memory_space=pltpu.VMEM)


def smem_spec():
    return pl.BlockSpec(memory_space=pltpu.SMEM)


def in_hbm(value):
    return pltpu.with_memory_space_constraint(value, pltpu.HBM)


def params(mib):
    return pltpu.CompilerParams(vmem_limit_bytes=mib * 2**20)


def exchange(value, axis, offset):
    count = lax.axis_size(axis)
    return lax.ppermute(value, axis, [(d, d ^ offset) for d in range(count)])


def opposite(axis):
    return lax.axis_size(axis) // 2


def gather_across(value, axis):
    return jnp.concatenate([value, exchange(value, axis, opposite(axis))], axis=0)


def exchange_near(entries, axis):
    found = list(entries)
    for j in range(len(entries) - 1, 0, -1):
        found[j] = exchange(entries[j], axis, j)
    return found


def gather_near(pair, axis):
    return exchange_near([pair] * (lax.axis_size(axis) // 2), axis)


def place_of(device, axis):
    half = lax.axis_size(axis) // 2
    offset = device ^ lax.axis_index(axis)
    return jnp.where(offset < half, offset, half + (offset ^ opposite(axis)))


def from_next(value, axis):
    count = lax.axis_size(axis)
    return lax.ppermute(value, axis, [(d, d - 1) for d in range(1, count)])


def stack_kernel(*refs):
    entries, out_ref = refs[:-1], refs[-1]
    for j, entry in enumerate(entries):
        for r in range(2):
            out_ref[r * len(entries) + j] = entry[r]


def stack(entries):
    _, rows, columns = entries[0].shape
    return pl.pallas_call(
        stack_kernel,
        in_specs=[vmem_spec()] * len(entries),
        out_specs=vmem_spec(),
        out_shape=pltpu.VMEM((2 * len(entries), rows, columns), entries[0].dtype),
        compiler_params=params(16),
        name="stack",
    )(*entries)


def project_kernel(given, slots, *refs):
    base_refs, (factors_ref, out_ref, wide, narrow, half) = refs[:given], refs[given:]
    aux, npno = factors_ref.shape[0], narrow.shape[2]

    @pl.when(pl.program_id(0) == 0)
    def _():
        for s in range(CAP):
            for j in range(given):

                @pl.when(lax.rem(slots[s], given) == j)
                def _():
                    narrow[s] = base_refs[j][slots[s] // given]

            wide[pl.ds(s * npno, npno), :] = narrow[s].astype(F32).T.astype(BF16)

    first = pl.program_id(0) * (aux // 2)
    for k in range(aux):
        left = jnp.dot(wide[...], factors_ref[k], preferred_element_type=F32).astype(BF16)
        for s in range(CAP):
            half[s, pl.ds(k * npno, npno), :] = left[s * npno : (s + 1) * npno]
    for s in range(CAP):
        both = jnp.dot(half[s], narrow[s], preferred_element_type=F32).astype(BF16)
        for k in range(aux):
            out_ref[s, first + k // 2, :, pl.ds((k % 2) * npno, npno)] = both[
                k * npno : (k + 1) * npno
            ]


def project(slots, group_bases, factor_block, step=8):
    aux, width, _ = factor_block.shape
    given = len(group_bases)
    npno = group_bases[0].shape[2]
    step = min(step, aux)

    def kernel(*refs):
        project_kernel(given, *refs)

    return pl.pallas_call(
        kernel,
        grid=(aux // step,),
        in_specs=[smem_spec()]
        + [vmem_spec()] * given
        + [pl.BlockSpec((step, width, width), lambda i: (i, 0, 0))],
        out_specs=vmem_spec(),
        out_shape=pltpu.VMEM((CAP, aux // 2, npno, 2 * npno), BF16),
        scratch_shapes=[
            pltpu.VMEM((CAP * npno, width), BF16),
            pltpu.VMEM((CAP, width, npno), BF16),
            pltpu.VMEM((CAP, step * npno, width), BF16),
        ],
        compiler_params=params(24),
        cost_estimate=pl.CostEstimate(
            flops=4 * CAP * aux * npno * width * (width + npno) // 2,
            bytes_accessed=2 * aux * width * width,
            transcendentals=0,
        ),
        name="project",
    )(slots, *group_bases, in_hbm(factor_block))


def ladder_kernel(given, slots, pairs, *refs):
    amp_refs, proj_ref, out_refs = refs[:given], refs[given], refs[given + 1 : 2 * given + 1]
    twice, mixed = refs[2 * given + 1 :]
    half, npno = proj_ref.shape[1], proj_ref.shape[2]
    twice[...] = jnp.zeros_like(twice)
    for out_ref in out_refs:
        out_ref[...] = jnp.zeros_like(out_ref)
    for s in range(CAP):
        for j in range(given):

            @pl.when(lax.rem(slots[s], given) == j)
            def _():
                amp = amp_refs[j][slots[s] // given]
                twice[pl.ds(0, npno), pl.ds(0, npno)] = amp
                twice[pl.ds(npno, npno), pl.ds(npno, npno)] = amp

        flat = proj_ref[s].reshape(half * npno, 2 * npno)
        mixed[...] = jnp.dot(flat, twice[...], preferred_element_type=F32).astype(BF16)
        total = jnp.zeros((npno, npno), F32)
        for m in range(half):
            total = total + lax.dot_general(
                mixed[pl.ds(m * npno, npno), :],
                proj_ref[s, m],
                CONTRACT_LAST,
                preferred_element_type=F32,
            )
        narrow = total.astype(BF16)
        for j in range(given):

            @pl.when((pairs[s] >= 0) & (lax.rem(slots[s], given) == j))
            def _():
                out_refs[j][slots[s] // given] = narrow


def ladder(slots, pairs, group_amps, projected):
    given = len(group_amps)
    half, npno = projected.shape[1:3]

    def kernel(*refs):
        ladder_kernel(given, *refs)

    return pl.pallas_call(
        kernel,
        in_specs=[smem_spec()] * 2 + [vmem_spec()] * (given + 1),
        out_specs=[vmem_spec()] * given,
        out_shape=[pltpu.VMEM((2, npno, npno), BF16)] * given,
        scratch_shapes=[
            pltpu.VMEM((2 * npno, 2 * npno), BF16),
            pltpu.VMEM((half * npno, 2 * npno), BF16),
        ],
        compiler_params=params(24),
        cost_estimate=pl.CostEstimate(
            flops=0,
            bytes_accessed=16 * CAP * half * npno**2,
            transcendentals=0,
        ),
        name="ladder",
    )(slots, pairs, *group_amps, projected)


def coupling_kernel(near, own_ref, next_ref, inter_ref, ints_ref, out_ref):
    count = own_ref.shape[0]
    total = ints_ref[0]
    for n in range(inter_ref.shape[1]):
        at = near[0, n]
        place = place_of(lax.rem(at, count), "dev")
        amp = jnp.where(at < count, own_ref[place], next_ref[place])
        inter = inter_ref[0, n]
        mixed = jnp.dot(inter, amp, preferred_element_type=F32).astype(BF16)
        total = total + lax.dot_general(
            mixed, inter, CONTRACT_LAST, preferred_element_type=F32
        )
    out_ref[...] = total


def coupling(near, own, following, inter, ints):
    return pl.pallas_call(
        coupling_kernel,
        in_specs=[smem_spec()] + [pl.BlockSpec()] * 4,
        out_specs=vmem_spec(),
        out_shape=pltpu.VMEM(ints.shape[1:], F32),
        compiler_params=params(16),
        cost_estimate=pl.CostEstimate(
            flops=4 * inter.shape[1] * inter.shape[2] ** 3, bytes_accessed=0, transcendentals=0
        ),
        name="coupling",
    )(near, own, following, in_hbm(inter), in_hbm(ints))


def fold_kernel(given, last, *refs):
    term_refs, (rest, down, across, far_down, far_across), (send, keep) = (
        refs[:given],
        refs[given : given + 5],
        refs[given + 5 :],
    )
    mine, other = (sum(ref[r].astype(F32) for ref in term_refs) for r in range(2))
    mine = mine + rest[...]
    keep[0] = mine
    if last:
        send[0] = other.astype(BF16)
    else:
        send[0] = other.astype(BF16)
        send[1] = (-mine / (down[...] + across[...])).astype(BF16)
        keep[1] = -other / (far_down[...] + far_across[...])


def fold(last, terms, rest, energies):
    given = len(terms)
    rows = 1 if last else 2

    def kernel(*refs):
        fold_kernel(given, last, *refs)

    return pl.pallas_call(
        kernel,
        in_specs=[vmem_spec()] * (given + 5),
        out_specs=[vmem_spec()] * 2,
        out_shape=[
            pltpu.VMEM((rows,) + rest.shape, BF16),
            pltpu.VMEM((rows,) + rest.shape, F32),
        ],
        compiler_params=params(16),
        name="fold",
    )(*terms, rest, *energies)


def finish_kernel(last, keep, got, down, across, out_ref):
    update = -(keep[0] + got[0].astype(F32)) / (down[...] + across[...])
    out_ref[0] = update.astype(out_ref.dtype)
    if not last:
        out_ref[1] = (keep[1] + got[1].astype(F32)).astype(out_ref.dtype)


def finish(last, keep, got, down, across):
    def kernel(*refs):
        finish_kernel(last, *refs)

    return pl.pallas_call(
        kernel,
        in_specs=[vmem_spec()] * 4,
        out_specs=vmem_spec(),
        out_shape=jax.ShapeDtypeStruct(keep.shape, F32) if last else pltpu.VMEM(keep.shape, BF16),
        compiler_params=params(16),
        name="finish",
    )(keep, got, down, across)


def on_device(
    amplitudes,
    bases,
    factors,
    intersections,
    pair_integrals,
    pno_energies,
    pair_shift,
    pair_atoms,
    pair_next,
):
    me = lax.axis_index("dev")
    count = lax.axis_size("dev")
    places = jnp.arange(count, dtype=jnp.int32)
    listed = jnp.any(pair_atoms == me, axis=1)
    before = places[None, :] < places[:, None]
    rank = jnp.sum(before & listed[None, :], axis=1)
    chosen = listed[None, :] & (rank[None, :] == jnp.arange(CAP)[:, None])
    pairs = jnp.sum(jnp.where(chosen, places[None, :] + 1, 0), axis=1) - 1
    slots = jnp.where(pairs >= 0, place_of(pairs, "dev"), 0)

    far_energies = exchange(pno_energies, "dev", opposite("dev"))
    far_shift = exchange(pair_shift, "dev", opposite("dev"))
    pair_bases = gather_across(bases, "dev")
    amps, far_energies = lax.optimization_barrier((amplitudes, far_energies))
    far_amps = exchange(amps, "dev", opposite("dev"))
    amps, pair_bases = lax.optimization_barrier((amps, pair_bases))
    group_bases = gather_near(pair_bases, "dev")
    group_amps = gather_near(jnp.concatenate([amps, far_amps], axis=0), "dev")
    shifted = pno_energies + 0.5 * pair_shift[:, None]
    far_shifted = far_energies + 0.5 * far_shift[:, None]
    energies = (shifted.reshape(-1, 1), shifted, far_shifted.reshape(-1, 1), far_shifted)
    projected = project(slots, group_bases, factors[0])
    group_amps, projected = lax.optimization_barrier((group_amps, projected))
    for iteration in range(ITERS):
        last = iteration + 1 == ITERS
        stacked = stack(group_amps)
        group_amps, stacked = lax.optimization_barrier((group_amps, stacked))
        following = from_next(stacked, "grp")
        terms = ladder(slots, pairs, group_amps, projected)
        rest = coupling(pair_next, stacked, following, intersections, pair_integrals)
        send, keep = fold(last, exchange_near(terms, "dev"), rest, energies)
        update = finish(last, keep, exchange(send, "dev", opposite("dev")), *energies[:2])
        if not last:
            group_amps = gather_near(update, "dev")
    return update


def solution(mesh):
    return jax.shard_map(
        on_device,
        mesh=mesh,
        in_specs=(
            P(("grp", "dev"), None, None),
            P(("grp", "dev"), None, None),
            P(("grp", "dev"), None, None, None),
            P(("grp", "dev"), None, None, None),
            P(("grp", "dev"), None, None),
            P(("grp", "dev"), None),
            P(("grp", "dev")),
            P("grp", None),
            P(("grp", "dev"), None),
        ),
        out_specs=P(("grp", "dev"), None, None),
        check_vma=False,
    )
```

profile of v0, /device:TPU:0, one launch (start us, length us, event | category | flops | bytes accessed | tf_op | source)
XLA Modules:
  0.0 77.3 jit_solution(1895680885262858019)
XLA Ops:
  0.0 4.0 %collective-permute-start = (f32[1,128]{1,0:T(1,128)}, f32[1,128]{1,0:T(1,128)S(1)}, u32[]{:S(2)}, u32[]{:S(2)}) collective-permute-start(f32[1,128]{1,0:T(1,128)} %param.14), channel_id=1, source_target_pairs={{0,4},{1,5},{2,6},{3,7},{4,0},{5,1},{6,2},{7,3},{8,12},{9,13},{10,... | collective-permute-start | bytes 1544 | tf_op jit(solution)/shard_map/ppermute | solution.py:33
  4.1 2.9 %collective-permute-start.13 = (f32[1]{0:T(128)}, f32[1]{0:T(128)}, u32[]{:S(2)}, u32[]{:S(2)}) collective-permute-start(f32[1]{0:T(128)} %param.15), channel_id=1, source_target_pairs={{0,4},{1,5},{2,6},{3,7},{4,0},{5,1},{6,2},{7,3},{8,12},{9,13},{10,... | collective-permute-start | bytes 20 | tf_op jit(solution)/shard_map/ppermute | solution.py:33
  10.7 1.5 %collective-permute-start.2 = (bf16[1,128,128]{2,1,0:T(8,128)(2,1)}, bf16[1,128,128]{2,1,0:T(8,128)(2,1)S(1)}, u32[]{:S(2)}, u32[]{:S(2)}) collective-permute-start(bf16[1,128,128]{2,1,0:T(8,128)(2,1)} %param.9), channel_id=1, source_target_pairs={{0,4},{1,5},{2,6},{3,7},{4,0},{5,1},{6,2},{7,3},{8,12},{9,13},{10,... | collective-permute-start | bytes 98312 | tf_op jit(solution)/shard_map/ppermute | solution.py:33
  12.2 0.9 %pad_maximum_fusion.refs_1_ = bf16[2,256,128]{2,1,0:T(8,128)(2,1)S(1)} fusion(bf16[1,256,128]{2,1,0:T(8,128)(2,1)S(1)} %collective-permute-done.1, bf16[1,256,128]{2,1,0:T(8,128)(2,1)} %param.10), kind=kLoop, calls=%fused_computation | loop fusion | flops 65536 | bytes 262144 | tf_op jit(solution)/shard_map/concatenate | solution.py:41
  13.1 1.6 %collective-permute-start.6 = (bf16[2,256,128]{2,1,0:T(8,128)(2,1)S(1)}, bf16[2,256,128]{2,1,0:T(8,128)(2,1)S(1)}, u32[]{:S(2)}, u32[]{:S(2)}) collective-permute-start(bf16[2,256,128]{2,1,0:T(8,128)(2,1)S(1)} %pad_maximum_fusion.refs_1_), channel_id=1, source_target_pairs={{0,1},{1,0},{2,3},{3,2},{4,5},{5,4},{6,7},{7,6},{8,9},{9,8},{10,11... | collective-permute-start | bytes 393224 | tf_op jit(solution)/shard_map/ppermute | solution.py:33
  14.6 1.6 %collective-permute-start.7 = (bf16[2,256,128]{2,1,0:T(8,128)(2,1)S(1)}, bf16[2,256,128]{2,1,0:T(8,128)(2,1)S(1)}, u32[]{:S(2)}, u32[]{:S(2)}) collective-permute-start(bf16[2,256,128]{2,1,0:T(8,128)(2,1)S(1)} %pad_maximum_fusion.refs_1_), channel_id=1, source_target_pairs={{0,2},{1,3},{2,0},{3,1},{4,6},{5,7},{6,4},{7,5},{8,10},{9,11},{10,... | collective-permute-start | bytes 393224 | tf_op jit(solution)/shard_map/ppermute | solution.py:33
  17.4 1.6 %collective-permute-start.3 = (bf16[2,128,128]{2,1,0:T(8,128)(2,1)S(1)}, bf16[2,128,128]{2,1,0:T(8,128)(2,1)S(1)}, u32[]{:S(2)}, u32[]{:S(2)}) collective-permute-start(bf16[2,128,128]{2,1,0:T(8,128)(2,1)S(1)} %constant_dynamic-update-slice_fusion.refs_0_.refs_2_), channel_id=1, source_target_pairs={{0,1},{1,0},{2,3},{3,2},{4,5},{5,4},{6,7},{7,6},{8,9},{9,8},{10,11... | collective-permute-start | bytes 196616 | tf_op jit(solution)/shard_map/ppermute | solution.py:33
  19.0 1.6 %collective-permute-start.4 = (bf16[2,128,128]{2,1,0:T(8,128)(2,1)S(1)}, bf16[2,128,128]{2,1,0:T(8,128)(2,1)S(1)}, u32[]{:S(2)}, u32[]{:S(2)}) collective-permute-start(bf16[2,128,128]{2,1,0:T(8,128)(2,1)S(1)} %constant_dynamic-update-slice_fusion.refs_0_.refs_2_), channel_id=1, source_target_pairs={{0,2},{1,3},{2,0},{3,1},{4,6},{5,7},{6,4},{7,5},{8,10},{9,11},{10,... | collective-permute-start | bytes 196616 | tf_op jit(solution)/shard_map/ppermute | solution.py:33
  20.5 2.1 %collective-permute-start.5 = (bf16[2,128,128]{2,1,0:T(8,128)(2,1)S(1)}, bf16[2,128,128]{2,1,0:T(8,128)(2,1)S(1)}, u32[]{:S(2)}, u32[]{:S(2)}) collective-permute-start(bf16[2,128,128]{2,1,0:T(8,128)(2,1)S(1)} %constant_dynamic-update-slice_fusion.refs_0_.refs_2_), channel_id=1, source_target_pairs={{0,3},{1,2},{2,1},{3,0},{4,7},{5,6},{6,5},{7,4},{8,11},{9,10},{10,... | collective-permute-start | bytes 196616 | tf_op jit(solution)/shard_map/ppermute | solution.py:33
  23.1 6.0 %project.1.refs_6_ = bf16[3,16,128,256]{3,2,1,0:T(8,128)(2,1)S(1)} custom-call(s32[3]{0:T(128)S(1)} %get-tuple-element.68.refs_0_, bf16[2,256,128]{2,1,0:T(8,128)(2,1)S(1)} %pad_maximum_fusion.refs_1_, bf16[2,256,128]{2,1,0:T(8,128)(2,1)S(1)} %collective-permute-done.6.refs_2_, bf16[2,256,128]{2,1,0:T(8,128)(2,1)S(1)} %collective-permute-done.7.refs_3_, ...), custom_call_target="tpu_custom_call" | custom-call | flops 2415919104 | bytes 4194304 | tf_op jit(solution)/shard_map/project/pallas_call | solution.py:122
  29.1 1.3 %collective-permute-start.12 = (bf16[8,128,128]{2,1,0:T(8,128)(2,1)S(1)}, bf16[8,128,128]{2,1,0:T(8,128)(2,1)}, u32[]{:S(2)}, u32[]{:S(2)}) collective-permute-start(bf16[8,128,128]{2,1,0:T(8,128)(2,1)S(1)} %stack.2.own_ref), channel_id=1, source_target_pairs={{8,0},{16,8},{24,16},{9,1},{17,9},{25,17},{10,2},{18,10},{26,18},{... | collective-permute-start | bytes 786440 | tf_op jit(solution)/shard_map/ppermute | solution.py:63
  30.9 4.0 %ladder.2 = (bf16[2,128,128]{2,1,0:T(8,128)(2,1)S(1)}, bf16[2,128,128]{2,1,0:T(8,128)(2,1)}, bf16[2,128,128]{2,1,0:T(8,128)(2,1)}, bf16[2,128,128]{2,1,0:T(8,128)(2,1)}) custom-call(s32[3]{0:T(128)S(1)} %get-tuple-element.68.refs_0_, s32[3]{0:T(128)S(1)} %get-tuple-element.67.refs_1_, ...), custom_call_target="tpu_custom_call" | custom-call | bytes 12582912 | tf_op jit(solution)/shard_map/ladder/pallas_call | solution.py:186
  35.6 1.0 %collective-permute-start.9 = (bf16[2,128,128]{2,1,0:T(8,128)(2,1)}, bf16[2,128,128]{2,1,0:T(8,128)(2,1)}, u32[]{:S(2)}, u32[]{:S(2)}) collective-permute-start(bf16[2,128,128]{2,1,0:T(8,128)(2,1)} %get-tuple-element.49), channel_id=1, source_target_pairs={{0,1},{1,0},{2,3},{3,2},{4,5},{5,4},{6,7},{7,6},{8,9},{9,8},{10,11... | collective-permute-start | bytes 196616 | tf_op jit(solution)/shard_map/ppermute | solution.py:33
  36.5 1.5 %collective-permute-start.10 = (bf16[2,128,128]{2,1,0:T(8,128)(2,1)}, bf16[2,128,128]{2,1,0:T(8,128)(2,1)}, u32[]{:S(2)}, u32[]{:S(2)}) collective-permute-start(bf16[2,128,128]{2,1,0:T(8,128)(2,1)} %get-tuple-element.50), channel_id=1, source_target_pairs={{0,2},{1,3},{2,0},{3,1},{4,6},{5,7},{6,4},{7,5},{8,10},{9,11},{10,... | collective-permute-start | bytes 196616 | tf_op jit(solution)/shard_map/ppermute | solution.py:33
  38.1 1.0 %collective-permute-start.11 = (bf16[2,128,128]{2,1,0:T(8,128)(2,1)}, bf16[2,128,128]{2,1,0:T(8,128)(2,1)}, u32[]{:S(2)}, u32[]{:S(2)}) collective-permute-start(bf16[2,128,128]{2,1,0:T(8,128)(2,1)} %get-tuple-element.51), channel_id=1, source_target_pairs={{0,3},{1,2},{2,1},{3,0},{4,7},{5,6},{6,5},{7,4},{8,11},{9,10},{10,... | collective-permute-start | bytes 196616 | tf_op jit(solution)/shard_map/ppermute | solution.py:33
  40.4 1.5 %coupling.2.refs_4_ = f32[128,128]{1,0:T(8,128)S(1)} custom-call(s32[1,4]{1,0:T(1,128)S(1)} %copy-done.2, bf16[8,128,128]{2,1,0:T(8,128)(2,1)S(1)} %stack.2.own_ref, bf16[8,128,128]{2,1,0:T(8,128)(2,1)} %collective-permute-done.12.next_ref, bf16[1,4,128,128]{3,2,1,0:T(8,128)(2,1)} %inter_ref.3, f32[1,128,128]{2,1,0:T(8,128)} %ints_ref.3), custom_call_target="tpu_custom_call" | custom-call | flops 33554432 | tf_op jit(solution)/shard_map/coupling/pallas_call | solution.py:221
  42.0 1.9 %collective-permute-done.11.refs_3_ = bf16[2,128,128]{2,1,0:T(8,128)(2,1)} collective-permute-done((bf16[2,128,128]{2,1,0:T(8,128)(2,1)}, bf16[2,128,128]{2,1,0:T(8,128)(2,1)}, u32[]{:S(2)}, u32[]{:S(2)}) %collective-permute-start.11) | collective-permute-done | bytes 65568 | tf_op jit(solution)/shard_map/ppermute | solution.py:33
  44.7 1.0 %fold.2 = (bf16[2,128,128]{2,1,0:T(8,128)(2,1)S(1)}, f32[2,128,128]{2,1,0:T(8,128)S(1)}) custom-call(bf16[2,128,128]{2,1,0:T(8,128)(2,1)S(1)} %copy-done.1, bf16[2,128,128]{2,1,0:T(8,128)(2,1)} %collective-permute-done.9.refs_1_, bf16[2,128,128]{2,1,0:T(8,128)(2,1)} %collective-permute-done.10.refs_2_, bf16[2,128,128]{2,1,0:T(8,128)(2,1)} %collective-permute-done.11.refs_3_, ...), custom_call_target="tpu_custom_call" | custom-call | tf_op jit(solution)/shard_map/fold/pallas_call | solution.py:258
  45.7 2.1 %collective-permute-start.14 = (bf16[2,128,128]{2,1,0:T(8,128)(2,1)S(1)}, bf16[2,128,128]{2,1,0:T(8,128)(2,1)S(1)}, u32[]{:S(2)}, u32[]{:S(2)}) collective-permute-start(bf16[2,128,128]{2,1,0:T(8,128)(2,1)S(1)} %get-tuple-element.55), channel_id=1, source_target_pairs={{0,4},{1,5},{2,6},{3,7},{4,0},{5,1},{6,2},{7,3},{8,12},{9,13},{10,... | collective-permute-start | bytes 196616 | tf_op jit(solution)/shard_map/ppermute | solution.py:33
  47.8 4.0 %collective-permute-done.14.refs_1_ = bf16[2,128,128]{2,1,0:T(8,128)(2,1)S(1)} collective-permute-done((bf16[2,128,128]{2,1,0:T(8,128)(2,1)S(1)}, bf16[2,128,128]{2,1,0:T(8,128)(2,1)S(1)}, u32[]{:S(2)}, u32[]{:S(2)}) %collective-permute-start.14) | collective-permute-done | bytes 65568 | tf_op jit(solution)/shard_map/ppermute | solution.py:33
  52.0 1.2 %collective-permute-start.15 = (bf16[2,128,128]{2,1,0:T(8,128)(2,1)S(1)}, bf16[2,128,128]{2,1,0:T(8,128)(2,1)S(1)}, u32[]{:S(2)}, u32[]{:S(2)}) collective-permute-start(bf16[2,128,128]{2,1,0:T(8,128)(2,1)S(1)} %finish.2.refs_0_.refs_2_), channel_id=1, source_target_pairs={{0,1},{1,0},{2,3},{3,2},{4,5},{5,4},{6,7},{7,6},{8,9},{9,8},{10,11... | collective-permute-start | bytes 196616 | tf_op jit(solution)/shard_map/ppermute | solution.py:33
  53.4 2.2 %collective-permute-start.17 = (bf16[2,128,128]{2,1,0:T(8,128)(2,1)S(1)}, bf16[2,128,128]{2,1,0:T(8,128)(2,1)S(1)}, u32[]{:S(2)}, u32[]{:S(2)}) collective-permute-start(bf16[2,128,128]{2,1,0:T(8,128)(2,1)S(1)} %finish.2.refs_0_.refs_2_), channel_id=1, source_target_pairs={{0,3},{1,2},{2,1},{3,0},{4,7},{5,6},{6,5},{7,4},{8,11},{9,10},{10,... | collective-permute-start | bytes 196616 | tf_op jit(solution)/shard_map/ppermute | solution.py:33
  55.5 1.1 %collective-permute-done.15.refs_1_.refs_3_ = bf16[2,128,128]{2,1,0:T(8,128)(2,1)S(1)} collective-permute-done((bf16[2,128,128]{2,1,0:T(8,128)(2,1)S(1)}, bf16[2,128,128]{2,1,0:T(8,128)(2,1)S(1)}, u32[]{:S(2)}, u32[]{:S(2)}) %collective-permute-start.15) | collective-permute-done | bytes 65568 | tf_op jit(solution)/shard_map/ppermute | solution.py:33
  57.5 1.0 %collective-permute-done.17.refs_3_.refs_5_ = bf16[2,128,128]{2,1,0:T(8,128)(2,1)S(1)} collective-permute-done((bf16[2,128,128]{2,1,0:T(8,128)(2,1)S(1)}, bf16[2,128,128]{2,1,0:T(8,128)(2,1)S(1)}, u32[]{:S(2)}, u32[]{:S(2)}) %collective-permute-start.17) | collective-permute-done | bytes 65568 | tf_op jit(solution)/shard_map/ppermute | solution.py:33
  58.5 1.3 %collective-permute-start.21 = (bf16[8,128,128]{2,1,0:T(8,128)(2,1)S(1)}, bf16[8,128,128]{2,1,0:T(8,128)(2,1)S(1)}, u32[]{:S(2)}, u32[]{:S(2)}) collective-permute-start(bf16[8,128,128]{2,1,0:T(8,128)(2,1)S(1)} %stack.3.own_ref), channel_id=1, source_target_pairs={{8,0},{16,8},{24,16},{9,1},{17,9},{25,17},{10,2},{18,10},{26,18},{... | collective-permute-start | bytes 786440 | tf_op jit(solution)/shard_map/ppermute | solution.py:63
  59.8 3.4 %ladder.3 = (bf16[2,128,128]{2,1,0:T(8,128)(2,1)S(1)}, bf16[2,128,128]{2,1,0:T(8,128)(2,1)S(1)}, bf16[2,128,128]{2,1,0:T(8,128)(2,1)S(1)}, bf16[2,128,128]{2,1,0:T(8,128)(2,1)S(1)}) custom-call(s32[3]{0:T(128)S(1)} %get-tuple-element.68.refs_0_, s32[3]{0:T(128)S(1)} %get-tuple-element.67.refs_1_, bf16[2,128,128]{2,1,0:T(8,128)(2,1)S(1)} %finish.2.refs_0_.refs_2_, ...), custom_call_target="tpu_custom_call" | custom-call | bytes 12582912 | tf_op jit(solution)/shard_map/ladder/pallas_call | solution.py:186
  63.2 1.2 %collective-permute-start.18 = (bf16[2,128,128]{2,1,0:T(8,128)(2,1)S(1)}, bf16[2,128,128]{2,1,0:T(8,128)(2,1)S(1)}, u32[]{:S(2)}, u32[]{:S(2)}) collective-permute-start(bf16[2,128,128]{2,1,0:T(8,128)(2,1)S(1)} %get-tuple-element.61), channel_id=1, source_target_pairs={{0,1},{1,0},{2,3},{3,2},{4,5},{5,4},{6,7},{7,6},{8,9},{9,8},{10,11... | collective-permute-start | bytes 196616 | tf_op jit(solution)/shard_map/ppermute | solution.py:33
  64.4 1.6 %collective-permute-start.19 = (bf16[2,128,128]{2,1,0:T(8,128)(2,1)S(1)}, bf16[2,128,128]{2,1,0:T(8,128)(2,1)S(1)}, u32[]{:S(2)}, u32[]{:S(2)}) collective-permute-start(bf16[2,128,128]{2,1,0:T(8,128)(2,1)S(1)} %get-tuple-element.62), channel_id=1, source_target_pairs={{0,2},{1,3},{2,0},{3,1},{4,6},{5,7},{6,4},{7,5},{8,10},{9,11},{10,... | collective-permute-start | bytes 196616 | tf_op jit(solution)/shard_map/ppermute | solution.py:33
  67.4 1.4 %coupling.3.refs_4_ = f32[128,128]{1,0:T(8,128)S(1)} custom-call(s32[1,4]{1,0:T(1,128)S(1)} %copy-done.3, bf16[8,128,128]{2,1,0:T(8,128)(2,1)S(1)} %stack.3.own_ref, bf16[8,128,128]{2,1,0:T(8,128)(2,1)S(1)} %collective-permute-done.21.next_ref, bf16[1,4,128,128]{3,2,1,0:T(8,128)(2,1)} %inter_ref.3, f32[1,128,128]{2,1,0:T(8,128)} %ints_ref.3), custom_call_target="tpu_custom_call" | custom-call | flops 33554432 | tf_op jit(solution)/shard_map/coupling/pallas_call | solution.py:221
  69.3 2.2 %collective-permute-done.20.refs_3_ = bf16[2,128,128]{2,1,0:T(8,128)(2,1)S(1)} collective-permute-done((bf16[2,128,128]{2,1,0:T(8,128)(2,1)S(1)}, bf16[2,128,128]{2,1,0:T(8,128)(2,1)S(1)}, u32[]{:S(2)}, u32[]{:S(2)}) %collective-permute-start.20) | collective-permute-done | bytes 65568 | tf_op jit(solution)/shard_map/ppermute | solution.py:33
  71.5 2.4 %collective-permute-start.22 = (bf16[1,128,128]{2,1,0:T(8,128)(2,1)S(1)}, bf16[1,128,128]{2,1,0:T(8,128)(2,1)S(1)}, u32[]{:S(2)}, u32[]{:S(2)}) collective-permute-start(bf16[1,128,128]{2,1,0:T(8,128)(2,1)S(1)} %get-tuple-element.66), channel_id=1, source_target_pairs={{0,4},{1,5},{2,6},{3,7},{4,0},{5,1},{6,2},{7,3},{8,12},{9,13},{10,... | collective-permute-start | bytes 98312 | tf_op jit(solution)/shard_map/ppermute | solution.py:33
  73.9 2.7 %collective-permute-done.22.refs_1_ = bf16[1,128,128]{2,1,0:T(8,128)(2,1)S(1)} collective-permute-done((bf16[1,128,128]{2,1,0:T(8,128)(2,1)S(1)}, bf16[1,128,128]{2,1,0:T(8,128)(2,1)S(1)}, u32[]{:S(2)}, u32[]{:S(2)}) %collective-permute-start.22) | collective-permute-done | bytes 32800 | tf_op jit(solution)/shard_map/ppermute | solution.py:33
  (47 shorter events, 11.1 us)
Async XLA Ops:
  0.0 10.7 %collective-permute-start = (f32[1,128]{1,0:T(1,128)}, f32[1,128]{1,0:T(1,128)S(1)}, u32[]{:S(2)}, u32[]{:S(2)}) collective-permute-start(f32[1,128]{1,0:T(1,128)} %param.14), channel_id=1, source_target_pairs={{0,4},{1,5},{2,6},{3,7},{4,0},{5,1},{6,2},{7,3},{8,12},{9,13},{10,... | collective-permute-start | bytes 1544 | tf_op jit(solution)/shard_map/ppermute | solution.py:33
  4.0 8.2 %collective-permute-start.1 = (bf16[1,256,128]{2,1,0:T(8,128)(2,1)}, bf16[1,256,128]{2,1,0:T(8,128)(2,1)S(1)}, u32[]{:S(2)}, u32[]{:S(2)}) collective-permute-start(bf16[1,256,128]{2,1,0:T(8,128)(2,1)} %param.10), channel_id=1, source_target_pairs={{0,4},{1,5},{2,6},{3,7},{4,0},{5,1},{6,2},{7,3},{8,12},{9,13},{10,... | collective-permute-start | bytes 196616 | tf_op jit(solution)/shard_map/ppermute | solution.py:33
  4.1 6.0 %collective-permute-start.13 = (f32[1]{0:T(128)}, f32[1]{0:T(128)}, u32[]{:S(2)}, u32[]{:S(2)}) collective-permute-start(f32[1]{0:T(128)} %param.15), channel_id=1, source_target_pairs={{0,4},{1,5},{2,6},{3,7},{4,0},{5,1},{6,2},{7,3},{8,12},{9,13},{10,... | collective-permute-start | bytes 20 | tf_op jit(solution)/shard_map/ppermute | solution.py:33
  10.7 6.7 %collective-permute-start.2 = (bf16[1,128,128]{2,1,0:T(8,128)(2,1)}, bf16[1,128,128]{2,1,0:T(8,128)(2,1)S(1)}, u32[]{:S(2)}, u32[]{:S(2)}) collective-permute-start(bf16[1,128,128]{2,1,0:T(8,128)(2,1)} %param.9), channel_id=1, source_target_pairs={{0,4},{1,5},{2,6},{3,7},{4,0},{5,1},{6,2},{7,3},{8,12},{9,13},{10,... | collective-permute-start | bytes 98312 | tf_op jit(solution)/shard_map/ppermute | solution.py:33
  13.1 7.5 %collective-permute-start.6 = (bf16[2,256,128]{2,1,0:T(8,128)(2,1)S(1)}, bf16[2,256,128]{2,1,0:T(8,128)(2,1)S(1)}, u32[]{:S(2)}, u32[]{:S(2)}) collective-permute-start(bf16[2,256,128]{2,1,0:T(8,128)(2,1)S(1)} %pad_maximum_fusion.refs_1_), channel_id=1, source_target_pairs={{0,1},{1,0},{2,3},{3,2},{4,5},{5,4},{6,7},{7,6},{8,9},{9,8},{10,11... | collective-permute-start | bytes 393224 | tf_op jit(solution)/shard_map/ppermute | solution.py:33
  14.6 8.0 %collective-permute-start.7 = (bf16[2,256,128]{2,1,0:T(8,128)(2,1)S(1)}, bf16[2,256,128]{2,1,0:T(8,128)(2,1)S(1)}, u32[]{:S(2)}, u32[]{:S(2)}) collective-permute-start(bf16[2,256,128]{2,1,0:T(8,128)(2,1)S(1)} %pad_maximum_fusion.refs_1_), channel_id=1, source_target_pairs={{0,2},{1,3},{2,0},{3,1},{4,6},{5,7},{6,4},{7,5},{8,10},{9,11},{10,... | collective-permute-start | bytes 393224 | tf_op jit(solution)/shard_map/ppermute | solution.py:33
  16.2 6.8 %collective-permute-start.8 = (bf16[2,256,128]{2,1,0:T(8,128)(2,1)S(1)}, bf16[2,256,128]{2,1,0:T(8,128)(2,1)S(1)}, u32[]{:S(2)}, u32[]{:S(2)}) collective-permute-start(bf16[2,256,128]{2,1,0:T(8,128)(2,1)S(1)} %pad_maximum_fusion.refs_1_), channel_id=1, source_target_pairs={{0,3},{1,2},{2,1},{3,0},{4,7},{5,6},{6,5},{7,4},{8,11},{9,10},{10,... | collective-permute-start | bytes 393224 | tf_op jit(solution)/shard_map/ppermute | solution.py:33
  17.4 11.7 %collective-permute-start.3 = (bf16[2,128,128]{2,1,0:T(8,128)(2,1)S(1)}, bf16[2,128,128]{2,1,0:T(8,128)(2,1)S(1)}, u32[]{:S(2)}, u32[]{:S(2)}) collective-permute-start(bf16[2,128,128]{2,1,0:T(8,128)(2,1)S(1)} %constant_dynamic-update-slice_fusion.refs_0_.refs_2_), channel_id=1, source_target_pairs={{0,1},{1,0},{2,3},{3,2},{4,5},{5,4},{6,7},{7,6},{8,9},{9,8},{10,11... | collective-permute-start | bytes 196616 | tf_op jit(solution)/shard_map/ppermute | solution.py:33
  19.0 10.1 %collective-permute-start.4 = (bf16[2,128,128]{2,1,0:T(8,128)(2,1)S(1)}, bf16[2,128,128]{2,1,0:T(8,128)(2,1)S(1)}, u32[]{:S(2)}, u32[]{:S(2)}) collective-permute-start(bf16[2,128,128]{2,1,0:T(8,128)(2,1)S(1)} %constant_dynamic-update-slice_fusion.refs_0_.refs_2_), channel_id=1, source_target_pairs={{0,2},{1,3},{2,0},{3,1},{4,6},{5,7},{6,4},{7,5},{8,10},{9,11},{10,... | collective-permute-start | bytes 196616 | tf_op jit(solution)/shard_map/ppermute | solution.py:33
  20.5 8.5 %collective-permute-start.5 = (bf16[2,128,128]{2,1,0:T(8,128)(2,1)S(1)}, bf16[2,128,128]{2,1,0:T(8,128)(2,1)S(1)}, u32[]{:S(2)}, u32[]{:S(2)}) collective-permute-start(bf16[2,128,128]{2,1,0:T(8,128)(2,1)S(1)} %constant_dynamic-update-slice_fusion.refs_0_.refs_2_), channel_id=1, source_target_pairs={{0,3},{1,2},{2,1},{3,0},{4,7},{5,6},{6,5},{7,4},{8,11},{9,10},{10,... | collective-permute-start | bytes 196616 | tf_op jit(solution)/shard_map/ppermute | solution.py:33
  29.1 10.7 %collective-permute-start.12 = (bf16[8,128,128]{2,1,0:T(8,128)(2,1)S(1)}, bf16[8,128,128]{2,1,0:T(8,128)(2,1)}, u32[]{:S(2)}, u32[]{:S(2)}) collective-permute-start(bf16[8,128,128]{2,1,0:T(8,128)(2,1)S(1)} %stack.2.own_ref), channel_id=1, source_target_pairs={{8,0},{16,8},{24,16},{9,1},{17,9},{25,17},{10,2},{18,10},{26,18},{... | collective-permute-start | bytes 786440 | tf_op jit(solution)/shard_map/ppermute | solution.py:63
  35.0 0.6 copy-start
  35.6 6.4 %collective-permute-start.9 = (bf16[2,128,128]{2,1,0:T(8,128)(2,1)}, bf16[2,128,128]{2,1,0:T(8,128)(2,1)}, u32[]{:S(2)}, u32[]{:S(2)}) collective-permute-start(bf16[2,128,128]{2,1,0:T(8,128)(2,1)} %get-tuple-element.49), channel_id=1, source_target_pairs={{0,1},{1,0},{2,3},{3,2},{4,5},{5,4},{6,7},{7,6},{8,9},{9,8},{10,11... | collective-permute-start | bytes 196616 | tf_op jit(solution)/shard_map/ppermute | solution.py:33
  36.5 5.4 %collective-permute-start.10 = (bf16[2,128,128]{2,1,0:T(8,128)(2,1)}, bf16[2,128,128]{2,1,0:T(8,128)(2,1)}, u32[]{:S(2)}, u32[]{:S(2)}) collective-permute-start(bf16[2,128,128]{2,1,0:T(8,128)(2,1)} %get-tuple-element.50), channel_id=1, source_target_pairs={{0,2},{1,3},{2,0},{3,1},{4,6},{5,7},{6,4},{7,5},{8,10},{9,11},{10,... | collective-permute-start | bytes 196616 | tf_op jit(solution)/shard_map/ppermute | solution.py:33
  38.1 5.8 %collective-permute-start.11 = (bf16[2,128,128]{2,1,0:T(8,128)(2,1)}, bf16[2,128,128]{2,1,0:T(8,128)(2,1)}, u32[]{:S(2)}, u32[]{:S(2)}) collective-permute-start(bf16[2,128,128]{2,1,0:T(8,128)(2,1)} %get-tuple-element.51), channel_id=1, source_target_pairs={{0,3},{1,2},{2,1},{3,0},{4,7},{5,6},{6,5},{7,4},{8,11},{9,10},{10,... | collective-permute-start | bytes 196616 | tf_op jit(solution)/shard_map/ppermute | solution.py:33
  39.8 0.7 copy-start.2
  43.8 0.8 %copy-start.1 = (bf16[2,128,128]{2,1,0:T(8,128)(2,1)S(1)}, bf16[2,128,128]{2,1,0:T(8,128)(2,1)}, u32[]{:S(2)}) copy-start(bf16[2,128,128]{2,1,0:T(8,128)(2,1)} %copy-done) | copy-start | bytes 196612
  45.7 6.2 %collective-permute-start.14 = (bf16[2,128,128]{2,1,0:T(8,128)(2,1)S(1)}, bf16[2,128,128]{2,1,0:T(8,128)(2,1)S(1)}, u32[]{:S(2)}, u32[]{:S(2)}) collective-permute-start(bf16[2,128,128]{2,1,0:T(8,128)(2,1)S(1)} %get-tuple-element.55), channel_id=1, source_target_pairs={{0,4},{1,5},{2,6},{3,7},{4,0},{5,1},{6,2},{7,3},{8,12},{9,13},{10,... | collective-permute-start | bytes 196616 | tf_op jit(solution)/shard_map/ppermute | solution.py:33
  52.0 4.7 %collective-permute-start.15 = (bf16[2,128,128]{2,1,0:T(8,128)(2,1)S(1)}, bf16[2,128,128]{2,1,0:T(8,128)(2,1)S(1)}, u32[]{:S(2)}, u32[]{:S(2)}) collective-permute-start(bf16[2,128,128]{2,1,0:T(8,128)(2,1)S(1)} %finish.2.refs_0_.refs_2_), channel_id=1, source_target_pairs={{0,1},{1,0},{2,3},{3,2},{4,5},{5,4},{6,7},{7,6},{8,9},{9,8},{10,11... | collective-permute-start | bytes 196616 | tf_op jit(solution)/shard_map/ppermute | solution.py:33
  53.2 4.3 %collective-permute-start.16 = (bf16[2,128,128]{2,1,0:T(8,128)(2,1)S(1)}, bf16[2,128,128]{2,1,0:T(8,128)(2,1)S(1)}, u32[]{:S(2)}, u32[]{:S(2)}) collective-permute-start(bf16[2,128,128]{2,1,0:T(8,128)(2,1)S(1)} %finish.2.refs_0_.refs_2_), channel_id=1, source_target_pairs={{0,2},{1,3},{2,0},{3,1},{4,6},{5,7},{6,4},{7,5},{8,10},{9,11},{10,... | collective-permute-start | bytes 196616 | tf_op jit(solution)/shard_map/ppermute | solution.py:33
  53.4 5.2 %collective-permute-start.17 = (bf16[2,128,128]{2,1,0:T(8,128)(2,1)S(1)}, bf16[2,128,128]{2,1,0:T(8,128)(2,1)S(1)}, u32[]{:S(2)}, u32[]{:S(2)}) collective-permute-start(bf16[2,128,128]{2,1,0:T(8,128)(2,1)S(1)} %finish.2.refs_0_.refs_2_), channel_id=1, source_target_pairs={{0,3},{1,2},{2,1},{3,0},{4,7},{5,6},{6,5},{7,4},{8,11},{9,10},{10,... | collective-permute-start | bytes 196616 | tf_op jit(solution)/shard_map/ppermute | solution.py:33
  58.5 8.2 %collective-permute-start.21 = (bf16[8,128,128]{2,1,0:T(8,128)(2,1)S(1)}, bf16[8,128,128]{2,1,0:T(8,128)(2,1)S(1)}, u32[]{:S(2)}, u32[]{:S(2)}) collective-permute-start(bf16[8,128,128]{2,1,0:T(8,128)(2,1)S(1)} %stack.3.own_ref), channel_id=1, source_target_pairs={{8,0},{16,8},{24,16},{9,1},{17,9},{25,17},{10,2},{18,10},{26,18},{... | collective-permute-start | bytes 786440 | tf_op jit(solution)/shard_map/ppermute | solution.py:63
  63.2 5.6 %collective-permute-start.18 = (bf16[2,128,128]{2,1,0:T(8,128)(2,1)S(1)}, bf16[2,128,128]{2,1,0:T(8,128)(2,1)S(1)}, u32[]{:S(2)}, u32[]{:S(2)}) collective-permute-start(bf16[2,128,128]{2,1,0:T(8,128)(2,1)S(1)} %get-tuple-element.61), channel_id=1, source_target_pairs={{0,1},{1,0},{2,3},{3,2},{4,5},{5,4},{6,7},{7,6},{8,9},{9,8},{10,11... | collective-permute-start | bytes 196616 | tf_op jit(solution)/shard_map/ppermute | solution.py:33
  64.4 4.9 %collective-permute-start.19 = (bf16[2,128,128]{2,1,0:T(8,128)(2,1)S(1)}, bf16[2,128,128]{2,1,0:T(8,128)(2,1)S(1)}, u32[]{:S(2)}, u32[]{:S(2)}) collective-permute-start(bf16[2,128,128]{2,1,0:T(8,128)(2,1)S(1)} %get-tuple-element.62), channel_id=1, source_target_pairs={{0,2},{1,3},{2,0},{3,1},{4,6},{5,7},{6,4},{7,5},{8,10},{9,11},{10,... | collective-permute-start | bytes 196616 | tf_op jit(solution)/shard_map/ppermute | solution.py:33
  66.0 5.5 %collective-permute-start.20 = (bf16[2,128,128]{2,1,0:T(8,128)(2,1)S(1)}, bf16[2,128,128]{2,1,0:T(8,128)(2,1)S(1)}, u32[]{:S(2)}, u32[]{:S(2)}) collective-permute-start(bf16[2,128,128]{2,1,0:T(8,128)(2,1)S(1)} %get-tuple-element.63), channel_id=1, source_target_pairs={{0,3},{1,2},{2,1},{3,0},{4,7},{5,6},{6,5},{7,4},{8,11},{9,10},{10,... | collective-permute-start | bytes 196616 | tf_op jit(solution)/shard_map/ppermute | solution.py:33
  66.8 0.7 copy-start.3
  71.5 5.1 %collective-permute-start.22 = (bf16[1,128,128]{2,1,0:T(8,128)(2,1)S(1)}, bf16[1,128,128]{2,1,0:T(8,128)(2,1)S(1)}, u32[]{:S(2)}, u32[]{:S(2)}) collective-permute-start(bf16[1,128,128]{2,1,0:T(8,128)(2,1)S(1)} %get-tuple-element.66), channel_id=1, source_target_pairs={{0,4},{1,5},{2,6},{3,7},{4,0},{5,1},{6,2},{7,3},{8,12},{9,13},{10,... | collective-permute-start | bytes 98312 | tf_op jit(solution)/shard_map/ppermute | solution.py:33
where the time goes:
time: 77.9 us; the launch traced here: 77.3 us
  starting transfers between devices  35 us (45%)
  Pallas kernels  18.2 us (23%)
  waiting for transfers between devices  14.7 us (19%)
  local copies, waits for them, and re-layouts  4.35 us (6%)
  other arithmetic  3.64 us (5%)
  between operations  1.48 us (2%)
    ppermute x21, starting transfers between devices, exchange(): return lax.ppermute(value, axis, [(d, d ^ offset) for d in range(count)])  32.4 us
    ppermute x21, waiting for transfers between devices, exchange(): return lax.ppermute(value, axis, [(d, d ^ offset) for d in range(count)])  14.7 us
    pallas_call x2, Pallas kernels, ladder(): pl.pallas_call(kernel, in_specs=[smem_spec()] * 2 + [vmem_spec()] * (give...  7.41 us
    pallas_call x1, Pallas kernels, project(): pl.pallas_call(kernel, grid=(aux // step,), in_specs=[smem_spec()] + [vme...  5.98 us
    unnamed x9, local copies, waits for them, and re-layouts  3.52 us
    pallas_call x2, Pallas kernels, coupling(): pl.pallas_call(coupling_kernel, in_specs=[smem_spec()] + [pl.BlockSpec()]...  2.9 us
    ppermute x2, starting transfers between devices, from_next(): return lax.ppermute(value, axis, [(d, d - 1) for d in range(1, count)])  2.58 us
  transfers between devices with their start and end apart: 23, of which 9 were waited for; matrix products, arithmetic and copies ran while one was open for 7% of the time, Pallas kernels for 21%

commit v1 on v0

--- a/solution.py
+++ b/solution.py
@@ -83,7 +83,7 @@
 
 
 def project_kernel(given, slots, *refs):
-    base_refs, (factors_ref, out_ref, wide, narrow, half) = refs[:given], refs[given:]
+    base_refs, (factors_ref, out_ref, tail_ref, wide, narrow, half) = refs[:given], refs[given:]
     aux, npno = factors_ref.shape[0], narrow.shape[2]
 
     @pl.when(pl.program_id(0) == 0)
@@ -105,9 +105,11 @@
     for s in range(CAP):
         both = jnp.dot(half[s], narrow[s], preferred_element_type=F32).astype(BF16)
         for k in range(aux):
-            out_ref[s, first + k // 2, :, pl.ds((k % 2) * npno, npno)] = both[
-                k * npno : (k + 1) * npno
-            ]
+            block = both[k * npno : (k + 1) * npno]
+            if s < CAP - 1:
+                out_ref[s, first + k // 2, :, pl.ds((k % 2) * npno, npno)] = block
+            else:
+                tail_ref[k // 2, :, pl.ds((k % 2) * npno, npno)] = block
 
 
 def project(slots, group_bases, factor_block, step=8):
@@ -125,8 +127,14 @@
         in_specs=[smem_spec()]
         + [vmem_spec()] * given
         + [pl.BlockSpec((step, width, width), lambda i: (i, 0, 0))],
-        out_specs=vmem_spec(),
-        out_shape=pltpu.VMEM((CAP, aux // 2, npno, 2 * npno), BF16),
+        out_specs=[
+            vmem_spec(),
+            pl.BlockSpec((step // 2, npno, 2 * npno), lambda i: (i, 0, 0)),
+        ],
+        out_shape=[
+            pltpu.VMEM((CAP - 1, aux // 2, npno, 2 * npno), BF16),
+            pltpu.HBM((aux // 2, npno, 2 * npno), BF16),
+        ],
         scratch_shapes=[
             pltpu.VMEM((CAP * npno, width), BF16),
             pltpu.VMEM((CAP, width, npno), BF16),
@@ -143,9 +151,11 @@
 
 
 def ladder_kernel(given, slots, pairs, *refs):
-    amp_refs, proj_ref, out_refs = refs[:given], refs[given], refs[given + 1 : 2 * given + 1]
-    twice, mixed = refs[2 * given + 1 :]
+    amp_refs, (proj_ref, tail_ref) = refs[:given], refs[given : given + 2]
+    out_refs, (twice, mixed, tail, sem) = refs[given + 2 : 2 * given + 2], refs[2 * given + 2 :]
     half, npno = proj_ref.shape[1], proj_ref.shape[2]
+    fetch = pltpu.make_async_copy(tail_ref, tail, sem)
+    fetch.start()
     twice[...] = jnp.zeros_like(twice)
     for out_ref in out_refs:
         out_ref[...] = jnp.zeros_like(out_ref)
@@ -158,13 +168,18 @@
                 twice[pl.ds(0, npno), pl.ds(0, npno)] = amp
                 twice[pl.ds(npno, npno), pl.ds(npno, npno)] = amp
 
-        flat = proj_ref[s].reshape(half * npno, 2 * npno)
+        if s == CAP - 1:
+            fetch.wait()
+            source = tail
+        else:
+            source = proj_ref.at[s]
+        flat = source[...].reshape(half * npno, 2 * npno)
         mixed[...] = jnp.dot(flat, twice[...], preferred_element_type=F32).astype(BF16)
         total = jnp.zeros((npno, npno), F32)
         for m in range(half):
             total = total + lax.dot_general(
                 mixed[pl.ds(m * npno, npno), :],
-                proj_ref[s, m],
+                source[m],
                 CONTRACT_LAST,
                 preferred_element_type=F32,
             )
@@ -178,19 +193,24 @@
 
 def ladder(slots, pairs, group_amps, projected):
     given = len(group_amps)
-    half, npno = projected.shape[1:3]
+    main, tail = projected
+    half, npno = tail.shape[:2]
 
     def kernel(*refs):
         ladder_kernel(given, *refs)
 
     return pl.pallas_call(
         kernel,
-        in_specs=[smem_spec()] * 2 + [vmem_spec()] * (given + 1),
+        in_specs=[smem_spec()] * 2
+        + [vmem_spec()] * (given + 1)
+        + [pl.BlockSpec(memory_space=pl.ANY)],
         out_specs=[vmem_spec()] * given,
         out_shape=[pltpu.VMEM((2, npno, npno), BF16)] * given,
         scratch_shapes=[
             pltpu.VMEM((2 * npno, 2 * npno), BF16),
             pltpu.VMEM((half * npno, 2 * npno), BF16),
+            pltpu.VMEM(tail.shape, BF16),
+            pltpu.SemaphoreType.DMA,
         ],
         compiler_params=params(24),
         cost_estimate=pl.CostEstimate(
@@ -199,7 +219,7 @@
             transcendentals=0,
         ),
         name="ladder",
-    )(slots, pairs, *group_amps, projected)
+    )(slots, pairs, *group_amps, main, in_hbm(tail))
 
 
 def coupling_kernel(near, own_ref, next_ref, inter_ref, ints_ref, out_ref):
@@ -310,16 +330,14 @@
     pairs = jnp.sum(jnp.where(chosen, places[None, :] + 1, 0), axis=1) - 1
     slots = jnp.where(pairs >= 0, place_of(pairs, "dev"), 0)
 
-    far_energies = exchange(pno_energies, "dev", opposite("dev"))
-    far_shift = exchange(pair_shift, "dev", opposite("dev"))
+    shifted = pno_energies + 0.5 * pair_shift[:, None]
+    far_shifted = exchange(shifted, "dev", opposite("dev"))
     pair_bases = gather_across(bases, "dev")
-    amps, far_energies = lax.optimization_barrier((amplitudes, far_energies))
+    amps, far_shifted = lax.optimization_barrier((amplitudes, far_shifted))
     far_amps = exchange(amps, "dev", opposite("dev"))
     amps, pair_bases = lax.optimization_barrier((amps, pair_bases))
     group_bases = gather_near(pair_bases, "dev")
     group_amps = gather_near(jnp.concatenate([amps, far_amps], axis=0), "dev")
-    shifted = pno_energies + 0.5 * pair_shift[:, None]
-    far_shifted = far_energies + 0.5 * far_shift[:, None]
     energies = (shifted.reshape(-1, 1), shifted, far_shifted.reshape(-1, 1), far_shifted)
     projected = project(slots, group_bases, factors[0])
     group_amps, projected = lax.optimization_barrier((group_amps, projected))

time: 77.9 us -> 73.3 us (0.941)
  waiting for transfers between devices: 14.7 us -> 21.4 us
  starting transfers between devices: 35 us -> 29.8 us
  local copies, waits for them, and re-layouts: 4.35 us -> 1 us
  other arithmetic: 3.64 us -> 2.47 us
  Pallas kernels: 18.2 us -> 17.4 us
    ppermute x21 -> x20, waiting for transfers between devices: 14.7 us -> 21.4 us  [exchange(): return lax.ppermute(value, axis, [(d, d ^ offset) for d in range(count)])]
    ppermute x21 -> x20, starting transfers between devices: 32.4 us -> 27.3 us  [exchange(): return lax.ppermute(value, axis, [(d, d ^ offset) for d in range(count)])]
    unnamed x9 -> x5, local copies, waits for them, and re-layouts: 3.52 us -> 0.77 us
    pallas_call x2, Pallas kernels: 1.06 us -> 0.15 us  [fold(): pl.pallas_call(kernel, in_specs=[vmem_spec()] * (given + 5), out_specs=[v...]
    pallas_call x1, Pallas kernels: 5.98 us -> 6.8 us  [project(): pl.pallas_call(kernel, grid=(aux // step,), in_specs=[smem_spec()] + [vme...]
  transfers between devices with their start and end apart: 23 -> 22, of which waited for: 9 -> 13; matrix products, arithmetic and copies ran while one was open for 7% -> 4% of each run, Pallas kernels for 21% -> 22%
where the time goes in v1:
time: 73.3 us; the launch traced here: 72.9 us
  starting transfers between devices  29.8 us (41%)
  waiting for transfers between devices  21.4 us (29%)
  Pallas kernels  17.4 us (24%)
  other arithmetic  2.47 us (3%)
  local copies, waits for them, and re-layouts  1 us (1%)
  between operations  0.79 us (1%)
    ppermute x20, starting transfers between devices, exchange(): return lax.ppermute(value, axis, [(d, d ^ offset) for d in range(count)])  27.3 us
    ppermute x20, waiting for transfers between devices, exchange(): return lax.ppermute(value, axis, [(d, d ^ offset) for d in range(count)])  21.4 us
    pallas_call x1, Pallas kernels, project(): pl.pallas_call(kernel, grid=(aux // step,), in_specs=[smem_spec()] + [vme...  6.8 us
    pallas_call x2, Pallas kernels, ladder(): pl.pallas_call(kernel, in_specs=[smem_spec()] * 2 + [vmem_spec()] * (give...  6.77 us
    pallas_call x2, Pallas kernels, coupling(): pl.pallas_call(coupling_kernel, in_specs=[smem_spec()] + [pl.BlockSpec()]...  2.79 us
    ppermute x2, starting transfers between devices, from_next(): return lax.ppermute(value, axis, [(d, d - 1) for d in range(1, count)])  2.58 us
  transfers between devices with their start and end apart: 22, of which 13 were waited for; matrix products, arithmetic and copies ran while one was open for 4% of the time, Pallas kernels for 22%

profile of v1, /device:TPU:0, one launch (start us, length us, event | category | flops | bytes accessed | tf_op | source)
XLA Modules:
  0.0 72.9 jit_solution(17876759952221807832)
XLA Ops:
  1.3 4.0 %collective-permute-start = (f32[1,128]{1,0:T(1,128)S(1)}, f32[1,128]{1,0:T(1,128)S(1)}, u32[]{:S(2)}, u32[]{:S(2)}) collective-permute-start(f32[1,128]{1,0:T(1,128)S(1)} %broadcast_add_fusion.refs_6_.refs_3_), channel_id=1, source_target_pairs={{0,4},{1,5},{2,6},{3,7},{4,0},{5,1},{6,2},{7,3},{8,12},{9,13},{10,... | collective-permute-start | bytes 1544 | tf_op jit(solution)/shard_map/ppermute | solution.py:33
  6.9 2.9 %collective-permute-start.2 = (bf16[1,128,128]{2,1,0:T(8,128)(2,1)}, bf16[1,128,128]{2,1,0:T(8,128)(2,1)S(1)}, u32[]{:S(2)}, u32[]{:S(2)}) collective-permute-start(bf16[1,128,128]{2,1,0:T(8,128)(2,1)} %param.9), channel_id=1, source_target_pairs={{0,4},{1,5},{2,6},{3,7},{4,0},{5,1},{6,2},{7,3},{8,12},{9,13},{10,... | collective-permute-start | bytes 98312 | tf_op jit(solution)/shard_map/ppermute | solution.py:33
  9.8 2.6 %collective-permute-done.1 = bf16[1,256,128]{2,1,0:T(8,128)(2,1)S(1)} collective-permute-done((bf16[1,256,128]{2,1,0:T(8,128)(2,1)}, bf16[1,256,128]{2,1,0:T(8,128)(2,1)S(1)}, u32[]{:S(2)}, u32[]{:S(2)}) %collective-permute-start.1) | collective-permute-done | bytes 65568 | tf_op jit(solution)/shard_map/ppermute | solution.py:33
  12.4 0.9 %pad_maximum_fusion.refs_1_ = bf16[2,256,128]{2,1,0:T(8,128)(2,1)S(1)} fusion(bf16[1,256,128]{2,1,0:T(8,128)(2,1)S(1)} %collective-permute-done.1, bf16[1,256,128]{2,1,0:T(8,128)(2,1)} %param.10), kind=kLoop, calls=%fused_computation | loop fusion | flops 65536 | bytes 262144 | tf_op jit(solution)/shard_map/concatenate | solution.py:41
  13.3 1.6 %collective-permute-start.6 = (bf16[2,256,128]{2,1,0:T(8,128)(2,1)S(1)}, bf16[2,256,128]{2,1,0:T(8,128)(2,1)S(1)}, u32[]{:S(2)}, u32[]{:S(2)}) collective-permute-start(bf16[2,256,128]{2,1,0:T(8,128)(2,1)S(1)} %pad_maximum_fusion.refs_1_), channel_id=1, source_target_pairs={{0,1},{1,0},{2,3},{3,2},{4,5},{5,4},{6,7},{7,6},{8,9},{9,8},{10,11... | collective-permute-start | bytes 393224 | tf_op jit(solution)/shard_map/ppermute | solution.py:33
  14.9 2.0 %collective-permute-start.8 = (bf16[2,256,128]{2,1,0:T(8,128)(2,1)S(1)}, bf16[2,256,128]{2,1,0:T(8,128)(2,1)S(1)}, u32[]{:S(2)}, u32[]{:S(2)}) collective-permute-start(bf16[2,256,128]{2,1,0:T(8,128)(2,1)S(1)} %pad_maximum_fusion.refs_1_), channel_id=1, source_target_pairs={{0,3},{1,2},{2,1},{3,0},{4,7},{5,6},{6,5},{7,4},{8,11},{9,10},{10,... | collective-permute-start | bytes 393224 | tf_op jit(solution)/shard_map/ppermute | solution.py:33
  17.6 1.6 %collective-permute-start.3 = (bf16[2,128,128]{2,1,0:T(8,128)(2,1)S(1)}, bf16[2,128,128]{2,1,0:T(8,128)(2,1)S(1)}, u32[]{:S(2)}, u32[]{:S(2)}) collective-permute-start(bf16[2,128,128]{2,1,0:T(8,128)(2,1)S(1)} %constant_dynamic-update-slice_fusion.refs_0_.refs_2_), channel_id=1, source_target_pairs={{0,1},{1,0},{2,3},{3,2},{4,5},{5,4},{6,7},{7,6},{8,9},{9,8},{10,11... | collective-permute-start | bytes 196616 | tf_op jit(solution)/shard_map/ppermute | solution.py:33
  19.6 1.6 %collective-permute-start.5 = (bf16[2,128,128]{2,1,0:T(8,128)(2,1)S(1)}, bf16[2,128,128]{2,1,0:T(8,128)(2,1)S(1)}, u32[]{:S(2)}, u32[]{:S(2)}) collective-permute-start(bf16[2,128,128]{2,1,0:T(8,128)(2,1)S(1)} %constant_dynamic-update-slice_fusion.refs_0_.refs_2_), channel_id=1, source_target_pairs={{0,3},{1,2},{2,1},{3,0},{4,7},{5,6},{6,5},{7,4},{8,11},{9,10},{10,... | collective-permute-start | bytes 196616 | tf_op jit(solution)/shard_map/ppermute | solution.py:33
  22.0 6.8 %project.1 = (bf16[2,16,128,256]{3,2,1,0:T(8,128)(2,1)S(1)}, bf16[16,128,256]{2,1,0:T(8,128)(2,1)}) custom-call(s32[3]{0:T(128)S(1)} %get-tuple-element.74.refs_0_, bf16[2,256,128]{2,1,0:T(8,128)(2,1)S(1)} %pad_maximum_fusion.refs_1_, bf16[2,256,128]{2,1,0:T(8,128)(2,1)S(1)} %collective-permute-done.6.refs_2_, ...), custom_call_target="tpu_custom_call" | custom-call | flops 2415919104 | bytes 4194304 | tf_op jit(solution)/shard_map/project/pallas_call | solution.py:124
  28.8 1.3 %collective-permute-start.12 = (bf16[8,128,128]{2,1,0:T(8,128)(2,1)S(1)}, bf16[8,128,128]{2,1,0:T(8,128)(2,1)S(1)}, u32[]{:S(2)}, u32[]{:S(2)}) collective-permute-start(bf16[8,128,128]{2,1,0:T(8,128)(2,1)S(1)} %stack.2.own_ref), channel_id=1, source_target_pairs={{8,0},{16,8},{24,16},{9,1},{17,9},{25,17},{10,2},{18,10},{26,18},{... | collective-permute-start | bytes 786440 | tf_op jit(solution)/shard_map/ppermute | solution.py:63
  30.1 3.4 %ladder.2 = (bf16[2,128,128]{2,1,0:T(8,128)(2,1)S(1)}, bf16[2,128,128]{2,1,0:T(8,128)(2,1)S(1)}, bf16[2,128,128]{2,1,0:T(8,128)(2,1)S(1)}, bf16[2,128,128]{2,1,0:T(8,128)(2,1)S(1)}) custom-call(s32[3]{0:T(128)S(1)} %get-tuple-element.74.refs_0_, s32[3]{0:T(128)S(1)} %get-tuple-element.73.refs_1_, ...), custom_call_target="tpu_custom_call" | custom-call | bytes 12582912 | tf_op jit(solution)/shard_map/ladder/pallas_call | solution.py:202
  33.5 1.6 %collective-permute-start.9 = (bf16[2,128,128]{2,1,0:T(8,128)(2,1)S(1)}, bf16[2,128,128]{2,1,0:T(8,128)(2,1)S(1)}, u32[]{:S(2)}, u32[]{:S(2)}) collective-permute-start(bf16[2,128,128]{2,1,0:T(8,128)(2,1)S(1)} %get-tuple-element.55), channel_id=1, source_target_pairs={{0,1},{1,0},{2,3},{3,2},{4,5},{5,4},{6,7},{7,6},{8,9},{9,8},{10,11... | collective-permute-start | bytes 196616 | tf_op jit(solution)/shard_map/ppermute | solution.py:33
  35.8 1.2 %collective-permute-start.11 = (bf16[2,128,128]{2,1,0:T(8,128)(2,1)S(1)}, bf16[2,128,128]{2,1,0:T(8,128)(2,1)S(1)}, u32[]{:S(2)}, u32[]{:S(2)}) collective-permute-start(bf16[2,128,128]{2,1,0:T(8,128)(2,1)S(1)} %get-tuple-element.57), channel_id=1, source_target_pairs={{0,3},{1,2},{2,1},{3,0},{4,7},{5,6},{6,5},{7,4},{8,11},{9,10},{10,... | collective-permute-start | bytes 196616 | tf_op jit(solution)/shard_map/ppermute | solution.py:33
  37.3 1.4 %coupling.2.refs_4_ = f32[128,128]{1,0:T(8,128)S(1)} custom-call(s32[1,4]{1,0:T(1,128)S(1)} %copy-done, bf16[8,128,128]{2,1,0:T(8,128)(2,1)S(1)} %stack.2.own_ref, bf16[8,128,128]{2,1,0:T(8,128)(2,1)S(1)} %collective-permute-done.12.next_ref, bf16[1,4,128,128]{3,2,1,0:T(8,128)(2,1)} %inter_ref.3, f32[1,128,128]{2,1,0:T(8,128)} %ints_ref.3), custom_call_target="tpu_custom_call" | custom-call | flops 33554432 | tf_op jit(solution)/shard_map/coupling/pallas_call | solution.py:241
  38.7 1.3 %collective-permute-done.10.refs_2_ = bf16[2,128,128]{2,1,0:T(8,128)(2,1)S(1)} collective-permute-done((bf16[2,128,128]{2,1,0:T(8,128)(2,1)S(1)}, bf16[2,128,128]{2,1,0:T(8,128)(2,1)S(1)}, u32[]{:S(2)}, u32[]{:S(2)}) %collective-permute-start.10) | collective-permute-done | bytes 65568 | tf_op jit(solution)/shard_map/ppermute | solution.py:33
  40.1 1.2 %collective-permute-done.11.refs_3_ = bf16[2,128,128]{2,1,0:T(8,128)(2,1)S(1)} collective-permute-done((bf16[2,128,128]{2,1,0:T(8,128)(2,1)S(1)}, bf16[2,128,128]{2,1,0:T(8,128)(2,1)S(1)}, u32[]{:S(2)}, u32[]{:S(2)}) %collective-permute-start.11) | collective-permute-done | bytes 65568 | tf_op jit(solution)/shard_map/ppermute | solution.py:33
  41.4 1.1 %collective-permute-start.13 = (bf16[2,128,128]{2,1,0:T(8,128)(2,1)S(1)}, bf16[2,128,128]{2,1,0:T(8,128)(2,1)S(1)}, u32[]{:S(2)}, u32[]{:S(2)}) collective-permute-start(bf16[2,128,128]{2,1,0:T(8,128)(2,1)S(1)} %get-tuple-element.61), channel_id=1, source_target_pairs={{0,4},{1,5},{2,6},{3,7},{4,0},{5,1},{6,2},{7,3},{8,12},{9,13},{10,... | collective-permute-start | bytes 196616 | tf_op jit(solution)/shard_map/ppermute | solution.py:33
  42.5 5.1 %collective-permute-done.13.refs_1_ = bf16[2,128,128]{2,1,0:T(8,128)(2,1)S(1)} collective-permute-done((bf16[2,128,128]{2,1,0:T(8,128)(2,1)S(1)}, bf16[2,128,128]{2,1,0:T(8,128)(2,1)S(1)}, u32[]{:S(2)}, u32[]{:S(2)}) %collective-permute-start.13) | collective-permute-done | bytes 65568 | tf_op jit(solution)/shard_map/ppermute | solution.py:33
  47.7 1.7 %collective-permute-start.14 = (bf16[2,128,128]{2,1,0:T(8,128)(2,1)S(1)}, bf16[2,128,128]{2,1,0:T(8,128)(2,1)S(1)}, u32[]{:S(2)}, u32[]{:S(2)}) collective-permute-start(bf16[2,128,128]{2,1,0:T(8,128)(2,1)S(1)} %finish.2.refs_0_.refs_2_), channel_id=1, source_target_pairs={{0,1},{1,0},{2,3},{3,2},{4,5},{5,4},{6,7},{7,6},{8,9},{9,8},{10,11... | collective-permute-start | bytes 196616 | tf_op jit(solution)/shard_map/ppermute | solution.py:33
  49.4 1.8 %collective-permute-start.16 = (bf16[2,128,128]{2,1,0:T(8,128)(2,1)S(1)}, bf16[2,128,128]{2,1,0:T(8,128)(2,1)S(1)}, u32[]{:S(2)}, u32[]{:S(2)}) collective-permute-start(bf16[2,128,128]{2,1,0:T(8,128)(2,1)S(1)} %finish.2.refs_0_.refs_2_), channel_id=1, source_target_pairs={{0,3},{1,2},{2,1},{3,0},{4,7},{5,6},{6,5},{7,4},{8,11},{9,10},{10,... | collective-permute-start | bytes 196616 | tf_op jit(solution)/shard_map/ppermute | solution.py:33
  52.0 1.7 %collective-permute-done.15.refs_2_.refs_4_ = bf16[2,128,128]{2,1,0:T(8,128)(2,1)S(1)} collective-permute-done((bf16[2,128,128]{2,1,0:T(8,128)(2,1)S(1)}, bf16[2,128,128]{2,1,0:T(8,128)(2,1)S(1)}, u32[]{:S(2)}, u32[]{:S(2)}) %collective-permute-start.15) | collective-permute-done | bytes 65568 | tf_op jit(solution)/shard_map/ppermute | solution.py:33
  53.7 0.9 %collective-permute-done.16.refs_3_.refs_5_ = bf16[2,128,128]{2,1,0:T(8,128)(2,1)S(1)} collective-permute-done((bf16[2,128,128]{2,1,0:T(8,128)(2,1)S(1)}, bf16[2,128,128]{2,1,0:T(8,128)(2,1)S(1)}, u32[]{:S(2)}, u32[]{:S(2)}) %collective-permute-start.16) | collective-permute-done | bytes 65568 | tf_op jit(solution)/shard_map/ppermute | solution.py:33
  54.6 1.3 %collective-permute-start.20 = (bf16[8,128,128]{2,1,0:T(8,128)(2,1)S(1)}, bf16[8,128,128]{2,1,0:T(8,128)(2,1)S(1)}, u32[]{:S(2)}, u32[]{:S(2)}) collective-permute-start(bf16[8,128,128]{2,1,0:T(8,128)(2,1)S(1)} %stack.3.own_ref), channel_id=1, source_target_pairs={{8,0},{16,8},{24,16},{9,1},{17,9},{25,17},{10,2},{18,10},{26,18},{... | collective-permute-start | bytes 786440 | tf_op jit(solution)/shard_map/ppermute | solution.py:63
  55.9 3.4 %ladder.3 = (bf16[2,128,128]{2,1,0:T(8,128)(2,1)S(1)}, bf16[2,128,128]{2,1,0:T(8,128)(2,1)S(1)}, bf16[2,128,128]{2,1,0:T(8,128)(2,1)S(1)}, bf16[2,128,128]{2,1,0:T(8,128)(2,1)S(1)}) custom-call(s32[3]{0:T(128)S(1)} %get-tuple-element.74.refs_0_, s32[3]{0:T(128)S(1)} %get-tuple-element.73.refs_1_, bf16[2,128,128]{2,1,0:T(8,128)(2,1)S(1)} %finish.2.refs_0_.refs_2_, ...), custom_call_target="tpu_custom_call" | custom-call | bytes 12582912 | tf_op jit(solution)/shard_map/ladder/pallas_call | solution.py:202
  59.3 1.3 %collective-permute-start.17 = (bf16[2,128,128]{2,1,0:T(8,128)(2,1)S(1)}, bf16[2,128,128]{2,1,0:T(8,128)(2,1)S(1)}, u32[]{:S(2)}, u32[]{:S(2)}) collective-permute-start(bf16[2,128,128]{2,1,0:T(8,128)(2,1)S(1)} %get-tuple-element.67), channel_id=1, source_target_pairs={{0,1},{1,0},{2,3},{3,2},{4,5},{5,4},{6,7},{7,6},{8,9},{9,8},{10,11... | collective-permute-start | bytes 196616 | tf_op jit(solution)/shard_map/ppermute | solution.py:33
  60.7 1.1 %collective-permute-start.18 = (bf16[2,128,128]{2,1,0:T(8,128)(2,1)S(1)}, bf16[2,128,128]{2,1,0:T(8,128)(2,1)S(1)}, u32[]{:S(2)}, u32[]{:S(2)}) collective-permute-start(bf16[2,128,128]{2,1,0:T(8,128)(2,1)S(1)} %get-tuple-element.68), channel_id=1, source_target_pairs={{0,2},{1,3},{2,0},{3,1},{4,6},{5,7},{6,4},{7,5},{8,10},{9,11},{10,... | collective-permute-start | bytes 196616 | tf_op jit(solution)/shard_map/ppermute | solution.py:33
  61.8 1.1 %collective-permute-start.19 = (bf16[2,128,128]{2,1,0:T(8,128)(2,1)S(1)}, bf16[2,128,128]{2,1,0:T(8,128)(2,1)S(1)}, u32[]{:S(2)}, u32[]{:S(2)}) collective-permute-start(bf16[2,128,128]{2,1,0:T(8,128)(2,1)S(1)} %get-tuple-element.69), channel_id=1, source_target_pairs={{0,3},{1,2},{2,1},{3,0},{4,7},{5,6},{6,5},{7,4},{8,11},{9,10},{10,... | collective-permute-start | bytes 196616 | tf_op jit(solution)/shard_map/ppermute | solution.py:33
  62.9 1.4 %coupling.3.refs_4_ = f32[128,128]{1,0:T(8,128)S(1)} custom-call(s32[1,4]{1,0:T(1,128)S(1)} %copy-done, bf16[8,128,128]{2,1,0:T(8,128)(2,1)S(1)} %stack.3.own_ref, bf16[8,128,128]{2,1,0:T(8,128)(2,1)S(1)} %collective-permute-done.20.next_ref, bf16[1,4,128,128]{3,2,1,0:T(8,128)(2,1)} %inter_ref.3, f32[1,128,128]{2,1,0:T(8,128)} %ints_ref.3), custom_call_target="tpu_custom_call" | custom-call | flops 33554432 | tf_op jit(solution)/shard_map/coupling/pallas_call | solution.py:241
  64.3 1.2 %collective-permute-done.18.refs_2_ = bf16[2,128,128]{2,1,0:T(8,128)(2,1)S(1)} collective-permute-done((bf16[2,128,128]{2,1,0:T(8,128)(2,1)S(1)}, bf16[2,128,128]{2,1,0:T(8,128)(2,1)S(1)}, u32[]{:S(2)}, u32[]{:S(2)}) %collective-permute-start.18) | collective-permute-done | bytes 65568 | tf_op jit(solution)/shard_map/ppermute | solution.py:33
  65.5 1.7 %collective-permute-done.19.refs_3_ = bf16[2,128,128]{2,1,0:T(8,128)(2,1)S(1)} collective-permute-done((bf16[2,128,128]{2,1,0:T(8,128)(2,1)S(1)}, bf16[2,128,128]{2,1,0:T(8,128)(2,1)S(1)}, u32[]{:S(2)}, u32[]{:S(2)}) %collective-permute-start.19) | collective-permute-done | bytes 65568 | tf_op jit(solution)/shard_map/ppermute | solution.py:33
  67.3 1.7 %collective-permute-start.21 = (bf16[1,128,128]{2,1,0:T(8,128)(2,1)S(1)}, bf16[1,128,128]{2,1,0:T(8,128)(2,1)S(1)}, u32[]{:S(2)}, u32[]{:S(2)}) collective-permute-start(bf16[1,128,128]{2,1,0:T(8,128)(2,1)S(1)} %get-tuple-element.72), channel_id=1, source_target_pairs={{0,4},{1,5},{2,6},{3,7},{4,0},{5,1},{6,2},{7,3},{8,12},{9,13},{10,... | collective-permute-start | bytes 98312 | tf_op jit(solution)/shard_map/ppermute | solution.py:33
  69.0 3.2 %collective-permute-done.21.refs_1_ = bf16[1,128,128]{2,1,0:T(8,128)(2,1)S(1)} collective-permute-done((bf16[1,128,128]{2,1,0:T(8,128)(2,1)S(1)}, bf16[1,128,128]{2,1,0:T(8,128)(2,1)S(1)}, u32[]{:S(2)}, u32[]{:S(2)}) %collective-permute-start.21) | collective-permute-done | bytes 32800 | tf_op jit(solution)/shard_map/ppermute | solution.py:33
  (39 shorter events, 6.8 us)
Async XLA Ops:
  1.3 5.6 %collective-permute-start = (f32[1,128]{1,0:T(1,128)S(1)}, f32[1,128]{1,0:T(1,128)S(1)}, u32[]{:S(2)}, u32[]{:S(2)}) collective-permute-start(f32[1,128]{1,0:T(1,128)S(1)} %broadcast_add_fusion.refs_6_.refs_3_), channel_id=1, source_target_pairs={{0,4},{1,5},{2,6},{3,7},{4,0},{5,1},{6,2},{7,3},{8,12},{9,13},{10,... | collective-permute-start | bytes 1544 | tf_op jit(solution)/shard_map/ppermute | solution.py:33
  5.3 7.1 %collective-permute-start.1 = (bf16[1,256,128]{2,1,0:T(8,128)(2,1)}, bf16[1,256,128]{2,1,0:T(8,128)(2,1)S(1)}, u32[]{:S(2)}, u32[]{:S(2)}) collective-permute-start(bf16[1,256,128]{2,1,0:T(8,128)(2,1)} %param.10), channel_id=1, source_target_pairs={{0,4},{1,5},{2,6},{3,7},{4,0},{5,1},{6,2},{7,3},{8,12},{9,13},{10,... | collective-permute-start | bytes 196616 | tf_op jit(solution)/shard_map/ppermute | solution.py:33
  6.9 10.7 %collective-permute-start.2 = (bf16[1,128,128]{2,1,0:T(8,128)(2,1)}, bf16[1,128,128]{2,1,0:T(8,128)(2,1)S(1)}, u32[]{:S(2)}, u32[]{:S(2)}) collective-permute-start(bf16[1,128,128]{2,1,0:T(8,128)(2,1)} %param.9), channel_id=1, source_target_pairs={{0,4},{1,5},{2,6},{3,7},{4,0},{5,1},{6,2},{7,3},{8,12},{9,13},{10,... | collective-permute-start | bytes 98312 | tf_op jit(solution)/shard_map/ppermute | solution.py:33
  13.3 6.4 %collective-permute-start.6 = (bf16[2,256,128]{2,1,0:T(8,128)(2,1)S(1)}, bf16[2,256,128]{2,1,0:T(8,128)(2,1)S(1)}, u32[]{:S(2)}, u32[]{:S(2)}) collective-permute-start(bf16[2,256,128]{2,1,0:T(8,128)(2,1)S(1)} %pad_maximum_fusion.refs_1_), channel_id=1, source_target_pairs={{0,1},{1,0},{2,3},{3,2},{4,5},{5,4},{6,7},{7,6},{8,9},{9,8},{10,11... | collective-permute-start | bytes 393224 | tf_op jit(solution)/shard_map/ppermute | solution.py:33
  14.9 6.4 %collective-permute-start.7 = (bf16[2,256,128]{2,1,0:T(8,128)(2,1)S(1)}, bf16[2,256,128]{2,1,0:T(8,128)(2,1)S(1)}, u32[]{:S(2)}, u32[]{:S(2)}) collective-permute-start(bf16[2,256,128]{2,1,0:T(8,128)(2,1)S(1)} %pad_maximum_fusion.refs_1_), channel_id=1, source_target_pairs={{0,2},{1,3},{2,0},{3,1},{4,6},{5,7},{6,4},{7,5},{8,10},{9,11},{10,... | collective-permute-start | bytes 393224 | tf_op jit(solution)/shard_map/ppermute | solution.py:33
  14.9 7.1 %collective-permute-start.8 = (bf16[2,256,128]{2,1,0:T(8,128)(2,1)S(1)}, bf16[2,256,128]{2,1,0:T(8,128)(2,1)S(1)}, u32[]{:S(2)}, u32[]{:S(2)}) collective-permute-start(bf16[2,256,128]{2,1,0:T(8,128)(2,1)S(1)} %pad_maximum_fusion.refs_1_), channel_id=1, source_target_pairs={{0,3},{1,2},{2,1},{3,0},{4,7},{5,6},{6,5},{7,4},{8,11},{9,10},{10,... | collective-permute-start | bytes 393224 | tf_op jit(solution)/shard_map/ppermute | solution.py:33
  17.6 11.2 %collective-permute-start.3 = (bf16[2,128,128]{2,1,0:T(8,128)(2,1)S(1)}, bf16[2,128,128]{2,1,0:T(8,128)(2,1)S(1)}, u32[]{:S(2)}, u32[]{:S(2)}) collective-permute-start(bf16[2,128,128]{2,1,0:T(8,128)(2,1)S(1)} %constant_dynamic-update-slice_fusion.refs_0_.refs_2_), channel_id=1, source_target_pairs={{0,1},{1,0},{2,3},{3,2},{4,5},{5,4},{6,7},{7,6},{8,9},{9,8},{10,11... | collective-permute-start | bytes 196616 | tf_op jit(solution)/shard_map/ppermute | solution.py:33
  19.2 9.6 %collective-permute-start.4 = (bf16[2,128,128]{2,1,0:T(8,128)(2,1)S(1)}, bf16[2,128,128]{2,1,0:T(8,128)(2,1)S(1)}, u32[]{:S(2)}, u32[]{:S(2)}) collective-permute-start(bf16[2,128,128]{2,1,0:T(8,128)(2,1)S(1)} %constant_dynamic-update-slice_fusion.refs_0_.refs_2_), channel_id=1, source_target_pairs={{0,2},{1,3},{2,0},{3,1},{4,6},{5,7},{6,4},{7,5},{8,10},{9,11},{10,... | collective-permute-start | bytes 196616 | tf_op jit(solution)/shard_map/ppermute | solution.py:33
  19.6 9.1 %collective-permute-start.5 = (bf16[2,128,128]{2,1,0:T(8,128)(2,1)S(1)}, bf16[2,128,128]{2,1,0:T(8,128)(2,1)S(1)}, u32[]{:S(2)}, u32[]{:S(2)}) collective-permute-start(bf16[2,128,128]{2,1,0:T(8,128)(2,1)S(1)} %constant_dynamic-update-slice_fusion.refs_0_.refs_2_), channel_id=1, source_target_pairs={{0,3},{1,2},{2,1},{3,0},{4,7},{5,6},{6,5},{7,4},{8,11},{9,10},{10,... | collective-permute-start | bytes 196616 | tf_op jit(solution)/shard_map/ppermute | solution.py:33
  22.0 15.1 %copy-start.1 = (f32[1,128]{1,0:T(1,128)S(1)}, f32[1,128]{1,0:T(1,128)}, u32[]{:S(2)}) copy-start(f32[1,128]{1,0:T(1,128)} %param.14) | copy-start | bytes 1540
  22.0 15.3 %copy-start = (s32[1,4]{1,0:T(1,128)S(1)}, s32[1,4]{1,0:T(1,128)}, u32[]{:S(2)}) copy-start(s32[1,4]{1,0:T(1,128)} %near.3) | copy-start | bytes 52
  28.8 8.5 %collective-permute-start.12 = (bf16[8,128,128]{2,1,0:T(8,128)(2,1)S(1)}, bf16[8,128,128]{2,1,0:T(8,128)(2,1)S(1)}, u32[]{:S(2)}, u32[]{:S(2)}) collective-permute-start(bf16[8,128,128]{2,1,0:T(8,128)(2,1)S(1)} %stack.2.own_ref), channel_id=1, source_target_pairs={{8,0},{16,8},{24,16},{9,1},{17,9},{25,17},{10,2},{18,10},{26,18},{... | collective-permute-start | bytes 786440 | tf_op jit(solution)/shard_map/ppermute | solution.py:63
  33.5 5.2 %collective-permute-start.9 = (bf16[2,128,128]{2,1,0:T(8,128)(2,1)S(1)}, bf16[2,128,128]{2,1,0:T(8,128)(2,1)S(1)}, u32[]{:S(2)}, u32[]{:S(2)}) collective-permute-start(bf16[2,128,128]{2,1,0:T(8,128)(2,1)S(1)} %get-tuple-element.55), channel_id=1, source_target_pairs={{0,1},{1,0},{2,3},{3,2},{4,5},{5,4},{6,7},{7,6},{8,9},{9,8},{10,11... | collective-permute-start | bytes 196616 | tf_op jit(solution)/shard_map/ppermute | solution.py:33
  35.1 5.0 %collective-permute-start.10 = (bf16[2,128,128]{2,1,0:T(8,128)(2,1)S(1)}, bf16[2,128,128]{2,1,0:T(8,128)(2,1)S(1)}, u32[]{:S(2)}, u32[]{:S(2)}) collective-permute-start(bf16[2,128,128]{2,1,0:T(8,128)(2,1)S(1)} %get-tuple-element.56), channel_id=1, source_target_pairs={{0,2},{1,3},{2,0},{3,1},{4,6},{5,7},{6,4},{7,5},{8,10},{9,11},{10,... | collective-permute-start | bytes 196616 | tf_op jit(solution)/shard_map/ppermute | solution.py:33
  35.8 5.5 %collective-permute-start.11 = (bf16[2,128,128]{2,1,0:T(8,128)(2,1)S(1)}, bf16[2,128,128]{2,1,0:T(8,128)(2,1)S(1)}, u32[]{:S(2)}, u32[]{:S(2)}) collective-permute-start(bf16[2,128,128]{2,1,0:T(8,128)(2,1)S(1)} %get-tuple-element.57), channel_id=1, source_target_pairs={{0,3},{1,2},{2,1},{3,0},{4,7},{5,6},{6,5},{7,4},{8,11},{9,10},{10,... | collective-permute-start | bytes 196616 | tf_op jit(solution)/shard_map/ppermute | solution.py:33
  41.4 6.2 %collective-permute-start.13 = (bf16[2,128,128]{2,1,0:T(8,128)(2,1)S(1)}, bf16[2,128,128]{2,1,0:T(8,128)(2,1)S(1)}, u32[]{:S(2)}, u32[]{:S(2)}) collective-permute-start(bf16[2,128,128]{2,1,0:T(8,128)(2,1)S(1)} %get-tuple-element.61), channel_id=1, source_target_pairs={{0,4},{1,5},{2,6},{3,7},{4,0},{5,1},{6,2},{7,3},{8,12},{9,13},{10,... | collective-permute-start | bytes 196616 | tf_op jit(solution)/shard_map/ppermute | solution.py:33
  47.7 4.3 %collective-permute-start.14 = (bf16[2,128,128]{2,1,0:T(8,128)(2,1)S(1)}, bf16[2,128,128]{2,1,0:T(8,128)(2,1)S(1)}, u32[]{:S(2)}, u32[]{:S(2)}) collective-permute-start(bf16[2,128,128]{2,1,0:T(8,128)(2,1)S(1)} %finish.2.refs_0_.refs_2_), channel_id=1, source_target_pairs={{0,1},{1,0},{2,3},{3,2},{4,5},{5,4},{6,7},{7,6},{8,9},{9,8},{10,11... | collective-permute-start | bytes 196616 | tf_op jit(solution)/shard_map/ppermute | solution.py:33
  49.4 4.3 %collective-permute-start.15 = (bf16[2,128,128]{2,1,0:T(8,128)(2,1)S(1)}, bf16[2,128,128]{2,1,0:T(8,128)(2,1)S(1)}, u32[]{:S(2)}, u32[]{:S(2)}) collective-permute-start(bf16[2,128,128]{2,1,0:T(8,128)(2,1)S(1)} %finish.2.refs_0_.refs_2_), channel_id=1, source_target_pairs={{0,2},{1,3},{2,0},{3,1},{4,6},{5,7},{6,4},{7,5},{8,10},{9,11},{10,... | collective-permute-start | bytes 196616 | tf_op jit(solution)/shard_map/ppermute | solution.py:33
  49.4 5.2 %collective-permute-start.16 = (bf16[2,128,128]{2,1,0:T(8,128)(2,1)S(1)}, bf16[2,128,128]{2,1,0:T(8,128)(2,1)S(1)}, u32[]{:S(2)}, u32[]{:S(2)}) collective-permute-start(bf16[2,128,128]{2,1,0:T(8,128)(2,1)S(1)} %finish.2.refs_0_.refs_2_), channel_id=1, source_target_pairs={{0,3},{1,2},{2,1},{3,0},{4,7},{5,6},{6,5},{7,4},{8,11},{9,10},{10,... | collective-permute-start | bytes 196616 | tf_op jit(solution)/shard_map/ppermute | solution.py:33
  54.6 8.2 %collective-permute-start.20 = (bf16[8,128,128]{2,1,0:T(8,128)(2,1)S(1)}, bf16[8,128,128]{2,1,0:T(8,128)(2,1)S(1)}, u32[]{:S(2)}, u32[]{:S(2)}) collective-permute-start(bf16[8,128,128]{2,1,0:T(8,128)(2,1)S(1)} %stack.3.own_ref), channel_id=1, source_target_pairs={{8,0},{16,8},{24,16},{9,1},{17,9},{25,17},{10,2},{18,10},{26,18},{... | collective-permute-start | bytes 786440 | tf_op jit(solution)/shard_map/ppermute | solution.py:63
  59.3 5.0 %collective-permute-start.17 = (bf16[2,128,128]{2,1,0:T(8,128)(2,1)S(1)}, bf16[2,128,128]{2,1,0:T(8,128)(2,1)S(1)}, u32[]{:S(2)}, u32[]{:S(2)}) collective-permute-start(bf16[2,128,128]{2,1,0:T(8,128)(2,1)S(1)} %get-tuple-element.67), channel_id=1, source_target_pairs={{0,1},{1,0},{2,3},{3,2},{4,5},{5,4},{6,7},{7,6},{8,9},{9,8},{10,11... | collective-permute-start | bytes 196616 | tf_op jit(solution)/shard_map/ppermute | solution.py:33
  60.7 4.9 %collective-permute-start.18 = (bf16[2,128,128]{2,1,0:T(8,128)(2,1)S(1)}, bf16[2,128,128]{2,1,0:T(8,128)(2,1)S(1)}, u32[]{:S(2)}, u32[]{:S(2)}) collective-permute-start(bf16[2,128,128]{2,1,0:T(8,128)(2,1)S(1)} %get-tuple-element.68), channel_id=1, source_target_pairs={{0,2},{1,3},{2,0},{3,1},{4,6},{5,7},{6,4},{7,5},{8,10},{9,11},{10,... | collective-permute-start | bytes 196616 | tf_op jit(solution)/shard_map/ppermute | solution.py:33
  61.8 5.5 %collective-permute-start.19 = (bf16[2,128,128]{2,1,0:T(8,128)(2,1)S(1)}, bf16[2,128,128]{2,1,0:T(8,128)(2,1)S(1)}, u32[]{:S(2)}, u32[]{:S(2)}) collective-permute-start(bf16[2,128,128]{2,1,0:T(8,128)(2,1)S(1)} %get-tuple-element.69), channel_id=1, source_target_pairs={{0,3},{1,2},{2,1},{3,0},{4,7},{5,6},{6,5},{7,4},{8,11},{9,10},{10,... | collective-permute-start | bytes 196616 | tf_op jit(solution)/shard_map/ppermute | solution.py:33
  67.3 4.9 %collective-permute-start.21 = (bf16[1,128,128]{2,1,0:T(8,128)(2,1)S(1)}, bf16[1,128,128]{2,1,0:T(8,128)(2,1)S(1)}, u32[]{:S(2)}, u32[]{:S(2)}) collective-permute-start(bf16[1,128,128]{2,1,0:T(8,128)(2,1)S(1)} %get-tuple-element.72), channel_id=1, source_target_pairs={{0,4},{1,5},{2,6},{3,7},{4,0},{5,1},{6,2},{7,3},{8,12},{9,13},{10,... | collective-permute-start | bytes 98312 | tf_op jit(solution)/shard_map/ppermute | solution.py:33

commit v2 on v1

--- a/solution.py
+++ b/solution.py
@@ -37,8 +37,35 @@
     return lax.axis_size(axis) // 2
 
 
-def gather_across(value, axis):
-    return jnp.concatenate([value, exchange(value, axis, opposite(axis))], axis=0)
+def copy_kernel(value_ref, out_ref):
+    out_ref[...] = value_ref[...]
+
+
+def in_vmem(value):
+    return pl.pallas_call(
+        copy_kernel,
+        in_specs=[vmem_spec()],
+        out_specs=vmem_spec(),
+        out_shape=pltpu.VMEM(value.shape, value.dtype),
+        compiler_params=params(16),
+        name="in_vmem",
+    )(value)
+
+
+def join_kernel(value_ref, other_ref, out_ref):
+    out_ref[0] = value_ref[0]
+    out_ref[1] = other_ref[0]
+
+
+def join(value, other):
+    return pl.pallas_call(
+        join_kernel,
+        in_specs=[vmem_spec()] * 2,
+        out_specs=vmem_spec(),
+        out_shape=pltpu.VMEM((2,) + value.shape[1:], value.dtype),
+        compiler_params=params(16),
+        name="join",
+    )(value, other)
 
 
 def exchange_near(entries, axis):
@@ -82,34 +109,53 @@
     )(*entries)
 
 
-def project_kernel(given, slots, *refs):
-    base_refs, (factors_ref, out_ref, tail_ref, wide, narrow, half) = refs[:given], refs[given:]
-    aux, npno = factors_ref.shape[0], narrow.shape[2]
-
-    @pl.when(pl.program_id(0) == 0)
-    def _():
-        for s in range(CAP):
-            for j in range(given):
-
-                @pl.when(lax.rem(slots[s], given) == j)
-                def _():
-                    narrow[s] = base_refs[j][slots[s] // given]
-
-            wide[pl.ds(s * npno, npno), :] = narrow[s].astype(F32).T.astype(BF16)
-
-    first = pl.program_id(0) * (aux // 2)
-    for k in range(aux):
-        left = jnp.dot(wide[...], factors_ref[k], preferred_element_type=F32).astype(BF16)
-        for s in range(CAP):
-            half[s, pl.ds(k * npno, npno), :] = left[s * npno : (s + 1) * npno]
+def project_kernel(given, step, slots, *refs):
+    base_refs, (factors_ref, out_ref, tail_ref) = refs[:given], refs[given : given + 3]
+    held, wide, narrow, half, tail, in_sems, out_sems = refs[given + 3 :]
+    aux, npno = held.shape[0], narrow.shape[2]
+    blocks = step // 2
+
+    def fetch(i):
+        part = pl.ds(i * step, step)
+        return pltpu.make_async_copy(factors_ref.at[part], held.at[part], in_sems.at[i])
+
+    def put(i):
+        part = pl.ds(i * blocks, blocks)
+        return pltpu.make_async_copy(tail.at[part], tail_ref.at[part], out_sems.at[i])
+
+    for i in range(aux // step):
+        fetch(i).start()
     for s in range(CAP):
-        both = jnp.dot(half[s], narrow[s], preferred_element_type=F32).astype(BF16)
-        for k in range(aux):
-            block = both[k * npno : (k + 1) * npno]
-            if s < CAP - 1:
-                out_ref[s, first + k // 2, :, pl.ds((k % 2) * npno, npno)] = block
-            else:
-                tail_ref[k // 2, :, pl.ds((k % 2) * npno, npno)] = block
+        for j in range(given):
+
+            @pl.when(lax.rem(slots[s], given) == j)
+            def _():
+                narrow[s] = base_refs[j][slots[s] // given]
+
+        wide[pl.ds(s * npno, npno), :] = narrow[s].astype(F32).T.astype(BF16)
+
+    def body(i, carry):
+        fetch(i).wait()
+        for k in range(step):
+            left = jnp.dot(wide[...], held[i * step + k], preferred_element_type=F32).astype(BF16)
+            for s in range(CAP):
+                half[s, pl.ds(k * npno, npno), :] = left[s * npno : (s + 1) * npno]
+        for s in range(CAP - 1, -1, -1):
+            both = jnp.dot(half[s], narrow[s], preferred_element_type=F32).astype(BF16)
+            for k in range(step):
+                block = both[k * npno : (k + 1) * npno]
+                place = i * blocks + k // 2
+                if s < CAP - 1:
+                    out_ref[s, place, :, pl.ds((k % 2) * npno, npno)] = block
+                else:
+                    tail[place, :, pl.ds((k % 2) * npno, npno)] = block
+            if s == CAP - 1:
+                put(i).start()
+        return carry
+
+    lax.fori_loop(0, aux // step, body, 0)
+    for i in range(aux // step):
+        put(i).wait()
 
 
 def project(slots, group_bases, factor_block, step=8):
@@ -119,26 +165,24 @@
     step = min(step, aux)
 
     def kernel(*refs):
-        project_kernel(given, *refs)
+        project_kernel(given, step, *refs)
 
     return pl.pallas_call(
         kernel,
-        grid=(aux // step,),
-        in_specs=[smem_spec()]
-        + [vmem_spec()] * given
-        + [pl.BlockSpec((step, width, width), lambda i: (i, 0, 0))],
-        out_specs=[
-            vmem_spec(),
-            pl.BlockSpec((step // 2, npno, 2 * npno), lambda i: (i, 0, 0)),
-        ],
+        in_specs=[smem_spec()] + [vmem_spec()] * given + [pl.BlockSpec(memory_space=pl.ANY)],
+        out_specs=[vmem_spec(), pl.BlockSpec(memory_space=pl.ANY)],
         out_shape=[
             pltpu.VMEM((CAP - 1, aux // 2, npno, 2 * npno), BF16),
             pltpu.HBM((aux // 2, npno, 2 * npno), BF16),
         ],
         scratch_shapes=[
+            pltpu.VMEM(factor_block.shape, BF16),
             pltpu.VMEM((CAP * npno, width), BF16),
             pltpu.VMEM((CAP, width, npno), BF16),
             pltpu.VMEM((CAP, step * npno, width), BF16),
+            pltpu.VMEM((aux // 2, npno, 2 * npno), BF16),
+            pltpu.SemaphoreType.DMA((aux // step,)),
+            pltpu.SemaphoreType.DMA((aux // step,)),
         ],
         compiler_params=params(24),
         cost_estimate=pl.CostEstimate(
@@ -332,7 +376,7 @@
 
     shifted = pno_energies + 0.5 * pair_shift[:, None]
     far_shifted = exchange(shifted, "dev", opposite("dev"))
-    pair_bases = gather_across(bases, "dev")
+    pair_bases = join(in_vmem(bases), exchange(bases, "dev", opposite("dev")))
     amps, far_shifted = lax.optimization_barrier((amplitudes, far_shifted))
     far_amps = exchange(amps, "dev", opposite("dev"))
     amps, pair_bases = lax.optimization_barrier((amps, pair_bases))

time: 73.3 us -> 72.2 us (0.985)
  other arithmetic: 2.47 us -> 1.61 us
  local copies, waits for them, and re-layouts: 1 us -> 1.84 us
    concatenate x1 -> x0, other arithmetic: 0.85 us -> none  [gather_across(): jnp.concatenate([value, exchange(value, axis, opposite(axis))], axis=0)]
    unnamed x5 -> x7, local copies, waits for them, and re-layouts: 0.77 us -> 1.6 us
    pallas_call x1 -> x3, Pallas kernels: 6.8 us -> 6.29 us  [the longest x1 6.28 us: project(): pl.pallas_call(kernel, in_specs=[smem_spec()] + [vmem_spec()] * given + [...]
  transfers between devices with their start and end apart: 22 -> 22, of which waited for: 13 -> 12; matrix products, arithmetic and copies ran while one was open for 4% -> 3% of each run, Pallas kernels for 22% -> 22%
where the time goes in v2:
time: 72.2 us; the launch traced here: 72.1 us
  starting transfers between devices  30.1 us (42%)
  waiting for transfers between devices  20.9 us (29%)
  Pallas kernels  16.8 us (23%)
  local copies, waits for them, and re-layouts  1.84 us (3%)
  other arithmetic  1.61 us (2%)
  between operations  0.82 us (1%)
    ppermute x20, starting transfers between devices, exchange(): return lax.ppermute(value, axis, [(d, d ^ offset) for d in range(count)])  27.5 us
    ppermute x20, waiting for transfers between devices, exchange(): return lax.ppermute(value, axis, [(d, d ^ offset) for d in range(count)])  20.9 us
    pallas_call x2, Pallas kernels, ladder(): pl.pallas_call(kernel, in_specs=[smem_spec()] * 2 + [vmem_spec()] * (give...  6.76 us
    pallas_call x1, Pallas kernels, project(): pl.pallas_call(kernel, in_specs=[smem_spec()] + [vmem_spec()] * given + [...  6.28 us
    pallas_call x2, Pallas kernels, coupling(): pl.pallas_call(coupling_kernel, in_specs=[smem_spec()] + [pl.BlockSpec()]...  2.79 us
    ppermute x2, starting transfers between devices, from_next(): return lax.ppermute(value, axis, [(d, d - 1) for d in range(1, count)])  2.58 us
    unnamed x7, local copies, waits for them, and re-layouts  1.6 us
  transfers between devices with their start and end apart: 22, of which 12 were waited for; matrix products, arithmetic and copies ran while one was open for 3% of the time, Pallas kernels for 22%

profile of v2, /device:TPU:0, one launch (start us, length us, event | category | flops | bytes accessed | tf_op | source)
XLA Modules:
  0.0 72.1 jit_solution(13923662825748868921)
XLA Ops:
  1.3 4.0 %collective-permute-start = (f32[1,128]{1,0:T(1,128)S(1)}, f32[1,128]{1,0:T(1,128)S(1)}, u32[]{:S(2)}, u32[]{:S(2)}) collective-permute-start(f32[1,128]{1,0:T(1,128)S(1)} %broadcast_add_fusion.refs_6_.refs_3_), channel_id=1, source_target_pairs={{0,4},{1,5},{2,6},{3,7},{4,0},{5,1},{6,2},{7,3},{8,12},{9,13},{10,... | collective-permute-start | bytes 1544 | tf_op jit(solution)/shard_map/ppermute | solution.py:33
  7.2 3.0 %collective-permute-start.2 = (bf16[1,128,128]{2,1,0:T(8,128)(2,1)}, bf16[1,128,128]{2,1,0:T(8,128)(2,1)S(1)}, u32[]{:S(2)}, u32[]{:S(2)}) collective-permute-start(bf16[1,128,128]{2,1,0:T(8,128)(2,1)} %param.9), channel_id=1, source_target_pairs={{0,4},{1,5},{2,6},{3,7},{4,0},{5,1},{6,2},{7,3},{8,12},{9,13},{10,... | collective-permute-start | bytes 98312 | tf_op jit(solution)/shard_map/ppermute | solution.py:33
  10.2 2.3 %collective-permute-done.1.other_ref = bf16[1,256,128]{2,1,0:T(8,128)(2,1)S(1)} collective-permute-done((bf16[1,256,128]{2,1,0:T(8,128)(2,1)}, bf16[1,256,128]{2,1,0:T(8,128)(2,1)S(1)}, u32[]{:S(2)}, u32[]{:S(2)}) %collective-permute-start.1) | collective-permute-done | bytes 65568 | tf_op jit(solution)/shard_map/ppermute | solution.py:33
  12.4 1.7 %collective-permute-start.6 = (bf16[2,256,128]{2,1,0:T(8,128)(2,1)S(1)}, bf16[2,256,128]{2,1,0:T(8,128)(2,1)S(1)}, u32[]{:S(2)}, u32[]{:S(2)}) collective-permute-start(bf16[2,256,128]{2,1,0:T(8,128)(2,1)S(1)} %join.1.refs_1_), channel_id=1, source_target_pairs={{0,1},{1,0},{2,3},{3,2},{4,5},{5,4},{6,7},{7,6},{8,9},{9,8},{10,11... | collective-permute-start | bytes 393224 | tf_op jit(solution)/shard_map/ppermute | solution.py:33
  14.3 1.7 %collective-permute-start.8 = (bf16[2,256,128]{2,1,0:T(8,128)(2,1)S(1)}, bf16[2,256,128]{2,1,0:T(8,128)(2,1)S(1)}, u32[]{:S(2)}, u32[]{:S(2)}) collective-permute-start(bf16[2,256,128]{2,1,0:T(8,128)(2,1)S(1)} %join.1.refs_1_), channel_id=1, source_target_pairs={{0,3},{1,2},{2,1},{3,0},{4,7},{5,6},{6,5},{7,4},{8,11},{9,10},{10,... | collective-permute-start | bytes 393224 | tf_op jit(solution)/shard_map/ppermute | solution.py:33
  16.8 1.7 %collective-permute-start.3 = (bf16[2,128,128]{2,1,0:T(8,128)(2,1)S(1)}, bf16[2,128,128]{2,1,0:T(8,128)(2,1)S(1)}, u32[]{:S(2)}, u32[]{:S(2)}) collective-permute-start(bf16[2,128,128]{2,1,0:T(8,128)(2,1)S(1)} %constant_dynamic-update-slice_fusion.refs_0_.refs_2_), channel_id=1, source_target_pairs={{0,1},{1,0},{2,3},{3,2},{4,5},{5,4},{6,7},{7,6},{8,9},{9,8},{10,11... | collective-permute-start | bytes 196616 | tf_op jit(solution)/shard_map/ppermute | solution.py:33
  18.8 1.7 %collective-permute-start.5 = (bf16[2,128,128]{2,1,0:T(8,128)(2,1)S(1)}, bf16[2,128,128]{2,1,0:T(8,128)(2,1)S(1)}, u32[]{:S(2)}, u32[]{:S(2)}) collective-permute-start(bf16[2,128,128]{2,1,0:T(8,128)(2,1)S(1)} %constant_dynamic-update-slice_fusion.refs_0_.refs_2_), channel_id=1, source_target_pairs={{0,3},{1,2},{2,1},{3,0},{4,7},{5,6},{6,5},{7,4},{8,11},{9,10},{10,... | collective-permute-start | bytes 196616 | tf_op jit(solution)/shard_map/ppermute | solution.py:33
  21.1 6.3 %project.1 = (bf16[2,16,128,256]{3,2,1,0:T(8,128)(2,1)S(1)}, bf16[16,128,256]{2,1,0:T(8,128)(2,1)}) custom-call(s32[3]{0:T(128)S(1)} %get-tuple-element.74.refs_0_, bf16[2,256,128]{2,1,0:T(8,128)(2,1)S(1)} %join.1.refs_1_, bf16[2,256,128]{2,1,0:T(8,128)(2,1)S(1)} %collective-permute-done.6.refs_2_, bf16[2,256,128]{2,1,0:T(8,128)(2,1)S(1)} %collective-permute-done.7.refs_3_, ...), custom_call_target="tpu_custom_call" | custom-call | flops 2415919104 | bytes 4194304 | tf_op jit(solution)/shard_map/project/pallas_call | solution.py:170
  27.5 1.3 %collective-permute-start.12 = (bf16[8,128,128]{2,1,0:T(8,128)(2,1)S(1)}, bf16[8,128,128]{2,1,0:T(8,128)(2,1)S(1)}, u32[]{:S(2)}, u32[]{:S(2)}) collective-permute-start(bf16[8,128,128]{2,1,0:T(8,128)(2,1)S(1)} %stack.2.own_ref), channel_id=1, source_target_pairs={{8,0},{16,8},{24,16},{9,1},{17,9},{25,17},{10,2},{18,10},{26,18},{... | collective-permute-start | bytes 786440 | tf_op jit(solution)/shard_map/ppermute | solution.py:90
  28.8 3.4 %ladder.2 = (bf16[2,128,128]{2,1,0:T(8,128)(2,1)S(1)}, bf16[2,128,128]{2,1,0:T(8,128)(2,1)S(1)}, bf16[2,128,128]{2,1,0:T(8,128)(2,1)S(1)}, bf16[2,128,128]{2,1,0:T(8,128)(2,1)S(1)}) custom-call(s32[3]{0:T(128)S(1)} %get-tuple-element.74.refs_0_, s32[3]{0:T(128)S(1)} %get-tuple-element.73.refs_1_, ...), custom_call_target="tpu_custom_call" | custom-call | bytes 12582912 | tf_op jit(solution)/shard_map/ladder/pallas_call | solution.py:246
  32.1 1.7 %collective-permute-start.9 = (bf16[2,128,128]{2,1,0:T(8,128)(2,1)S(1)}, bf16[2,128,128]{2,1,0:T(8,128)(2,1)S(1)}, u32[]{:S(2)}, u32[]{:S(2)}) collective-permute-start(bf16[2,128,128]{2,1,0:T(8,128)(2,1)S(1)} %get-tuple-element.55), channel_id=1, source_target_pairs={{0,1},{1,0},{2,3},{3,2},{4,5},{5,4},{6,7},{7,6},{8,9},{9,8},{10,11... | collective-permute-start | bytes 196616 | tf_op jit(solution)/shard_map/ppermute | solution.py:33
  33.8 0.9 %collective-permute-start.10 = (bf16[2,128,128]{2,1,0:T(8,128)(2,1)S(1)}, bf16[2,128,128]{2,1,0:T(8,128)(2,1)S(1)}, u32[]{:S(2)}, u32[]{:S(2)}) collective-permute-start(bf16[2,128,128]{2,1,0:T(8,128)(2,1)S(1)} %get-tuple-element.56), channel_id=1, source_target_pairs={{0,2},{1,3},{2,0},{3,1},{4,6},{5,7},{6,4},{7,5},{8,10},{9,11},{10,... | collective-permute-start | bytes 196616 | tf_op jit(solution)/shard_map/ppermute | solution.py:33
  34.7 1.0 %collective-permute-start.11 = (bf16[2,128,128]{2,1,0:T(8,128)(2,1)S(1)}, bf16[2,128,128]{2,1,0:T(8,128)(2,1)S(1)}, u32[]{:S(2)}, u32[]{:S(2)}) collective-permute-start(bf16[2,128,128]{2,1,0:T(8,128)(2,1)S(1)} %get-tuple-element.57), channel_id=1, source_target_pairs={{0,3},{1,2},{2,1},{3,0},{4,7},{5,6},{6,5},{7,4},{8,11},{9,10},{10,... | collective-permute-start | bytes 196616 | tf_op jit(solution)/shard_map/ppermute | solution.py:33
  36.0 1.4 %coupling.2.refs_4_ = f32[128,128]{1,0:T(8,128)S(1)} custom-call(s32[1,4]{1,0:T(1,128)S(1)} %copy-done.1, bf16[8,128,128]{2,1,0:T(8,128)(2,1)S(1)} %stack.2.own_ref, bf16[8,128,128]{2,1,0:T(8,128)(2,1)S(1)} %collective-permute-done.12.next_ref, bf16[1,4,128,128]{3,2,1,0:T(8,128)(2,1)} %inter_ref.3, f32[1,128,128]{2,1,0:T(8,128)} %ints_ref.3), custom_call_target="tpu_custom_call" | custom-call | flops 33554432 | tf_op jit(solution)/shard_map/coupling/pallas_call | solution.py:285
  37.4 1.4 %collective-permute-done.10.refs_2_ = bf16[2,128,128]{2,1,0:T(8,128)(2,1)S(1)} collective-permute-done((bf16[2,128,128]{2,1,0:T(8,128)(2,1)S(1)}, bf16[2,128,128]{2,1,0:T(8,128)(2,1)S(1)}, u32[]{:S(2)}, u32[]{:S(2)}) %collective-permute-start.10) | collective-permute-done | bytes 65568 | tf_op jit(solution)/shard_map/ppermute | solution.py:33
  38.8 1.4 %collective-permute-done.11.refs_3_ = bf16[2,128,128]{2,1,0:T(8,128)(2,1)S(1)} collective-permute-done((bf16[2,128,128]{2,1,0:T(8,128)(2,1)S(1)}, bf16[2,128,128]{2,1,0:T(8,128)(2,1)S(1)}, u32[]{:S(2)}, u32[]{:S(2)}) %collective-permute-start.11) | collective-permute-done | bytes 65568 | tf_op jit(solution)/shard_map/ppermute | solution.py:33
  40.3 1.0 %collective-permute-start.13 = (bf16[2,128,128]{2,1,0:T(8,128)(2,1)S(1)}, bf16[2,128,128]{2,1,0:T(8,128)(2,1)S(1)}, u32[]{:S(2)}, u32[]{:S(2)}) collective-permute-start(bf16[2,128,128]{2,1,0:T(8,128)(2,1)S(1)} %get-tuple-element.61), channel_id=1, source_target_pairs={{0,4},{1,5},{2,6},{3,7},{4,0},{5,1},{6,2},{7,3},{8,12},{9,13},{10,... | collective-permute-start | bytes 196616 | tf_op jit(solution)/shard_map/ppermute | solution.py:33
  41.3 5.1 %collective-permute-done.13.refs_1_ = bf16[2,128,128]{2,1,0:T(8,128)(2,1)S(1)} collective-permute-done((bf16[2,128,128]{2,1,0:T(8,128)(2,1)S(1)}, bf16[2,128,128]{2,1,0:T(8,128)(2,1)S(1)}, u32[]{:S(2)}, u32[]{:S(2)}) %collective-permute-start.13) | collective-permute-done | bytes 65568 | tf_op jit(solution)/shard_map/ppermute | solution.py:33
  46.5 1.6 %collective-permute-start.14 = (bf16[2,128,128]{2,1,0:T(8,128)(2,1)S(1)}, bf16[2,128,128]{2,1,0:T(8,128)(2,1)S(1)}, u32[]{:S(2)}, u32[]{:S(2)}) collective-permute-start(bf16[2,128,128]{2,1,0:T(8,128)(2,1)S(1)} %finish.2.refs_0_.refs_2_), channel_id=1, source_target_pairs={{0,1},{1,0},{2,3},{3,2},{4,5},{5,4},{6,7},{7,6},{8,9},{9,8},{10,11... | collective-permute-start | bytes 196616 | tf_op jit(solution)/shard_map/ppermute | solution.py:33
  48.2 1.9 %collective-permute-start.16 = (bf16[2,128,128]{2,1,0:T(8,128)(2,1)S(1)}, bf16[2,128,128]{2,1,0:T(8,128)(2,1)S(1)}, u32[]{:S(2)}, u32[]{:S(2)}) collective-permute-start(bf16[2,128,128]{2,1,0:T(8,128)(2,1)S(1)} %finish.2.refs_0_.refs_2_), channel_id=1, source_target_pairs={{0,3},{1,2},{2,1},{3,0},{4,7},{5,6},{6,5},{7,4},{8,11},{9,10},{10,... | collective-permute-start | bytes 196616 | tf_op jit(solution)/shard_map/ppermute | solution.py:33
  50.9 1.6 %collective-permute-done.15.refs_2_.refs_4_ = bf16[2,128,128]{2,1,0:T(8,128)(2,1)S(1)} collective-permute-done((bf16[2,128,128]{2,1,0:T(8,128)(2,1)S(1)}, bf16[2,128,128]{2,1,0:T(8,128)(2,1)S(1)}, u32[]{:S(2)}, u32[]{:S(2)}) %collective-permute-start.15) | collective-permute-done | bytes 65568 | tf_op jit(solution)/shard_map/ppermute | solution.py:33
  52.4 0.9 %collective-permute-done.16.refs_3_.refs_5_ = bf16[2,128,128]{2,1,0:T(8,128)(2,1)S(1)} collective-permute-done((bf16[2,128,128]{2,1,0:T(8,128)(2,1)S(1)}, bf16[2,128,128]{2,1,0:T(8,128)(2,1)S(1)}, u32[]{:S(2)}, u32[]{:S(2)}) %collective-permute-start.16) | collective-permute-done | bytes 65568 | tf_op jit(solution)/shard_map/ppermute | solution.py:33
  53.4 1.3 %collective-permute-start.20 = (bf16[8,128,128]{2,1,0:T(8,128)(2,1)S(1)}, bf16[8,128,128]{2,1,0:T(8,128)(2,1)S(1)}, u32[]{:S(2)}, u32[]{:S(2)}) collective-permute-start(bf16[8,128,128]{2,1,0:T(8,128)(2,1)S(1)} %stack.3.own_ref), channel_id=1, source_target_pairs={{8,0},{16,8},{24,16},{9,1},{17,9},{25,17},{10,2},{18,10},{26,18},{... | collective-permute-start | bytes 786440 | tf_op jit(solution)/shard_map/ppermute | solution.py:90
  54.7 3.4 %ladder.3 = (bf16[2,128,128]{2,1,0:T(8,128)(2,1)S(1)}, bf16[2,128,128]{2,1,0:T(8,128)(2,1)S(1)}, bf16[2,128,128]{2,1,0:T(8,128)(2,1)S(1)}, bf16[2,128,128]{2,1,0:T(8,128)(2,1)S(1)}) custom-call(s32[3]{0:T(128)S(1)} %get-tuple-element.74.refs_0_, s32[3]{0:T(128)S(1)} %get-tuple-element.73.refs_1_, bf16[2,128,128]{2,1,0:T(8,128)(2,1)S(1)} %finish.2.refs_0_.refs_2_, ...), custom_call_target="tpu_custom_call" | custom-call | bytes 12582912 | tf_op jit(solution)/shard_map/ladder/pallas_call | solution.py:246
  58.0 1.3 %collective-permute-start.17 = (bf16[2,128,128]{2,1,0:T(8,128)(2,1)S(1)}, bf16[2,128,128]{2,1,0:T(8,128)(2,1)S(1)}, u32[]{:S(2)}, u32[]{:S(2)}) collective-permute-start(bf16[2,128,128]{2,1,0:T(8,128)(2,1)S(1)} %get-tuple-element.67), channel_id=1, source_target_pairs={{0,1},{1,0},{2,3},{3,2},{4,5},{5,4},{6,7},{7,6},{8,9},{9,8},{10,11... | collective-permute-start | bytes 196616 | tf_op jit(solution)/shard_map/ppermute | solution.py:33
  59.4 1.2 %collective-permute-start.18 = (bf16[2,128,128]{2,1,0:T(8,128)(2,1)S(1)}, bf16[2,128,128]{2,1,0:T(8,128)(2,1)S(1)}, u32[]{:S(2)}, u32[]{:S(2)}) collective-permute-start(bf16[2,128,128]{2,1,0:T(8,128)(2,1)S(1)} %get-tuple-element.68), channel_id=1, source_target_pairs={{0,2},{1,3},{2,0},{3,1},{4,6},{5,7},{6,4},{7,5},{8,10},{9,11},{10,... | collective-permute-start | bytes 196616 | tf_op jit(solution)/shard_map/ppermute | solution.py:33
  60.6 1.0 %collective-permute-start.19 = (bf16[2,128,128]{2,1,0:T(8,128)(2,1)S(1)}, bf16[2,128,128]{2,1,0:T(8,128)(2,1)S(1)}, u32[]{:S(2)}, u32[]{:S(2)}) collective-permute-start(bf16[2,128,128]{2,1,0:T(8,128)(2,1)S(1)} %get-tuple-element.69), channel_id=1, source_target_pairs={{0,3},{1,2},{2,1},{3,0},{4,7},{5,6},{6,5},{7,4},{8,11},{9,10},{10,... | collective-permute-start | bytes 196616 | tf_op jit(solution)/shard_map/ppermute | solution.py:33
  61.6 1.4 %coupling.3.refs_4_ = f32[128,128]{1,0:T(8,128)S(1)} custom-call(s32[1,4]{1,0:T(1,128)S(1)} %copy-done.1, bf16[8,128,128]{2,1,0:T(8,128)(2,1)S(1)} %stack.3.own_ref, bf16[8,128,128]{2,1,0:T(8,128)(2,1)S(1)} %collective-permute-done.20.next_ref, bf16[1,4,128,128]{3,2,1,0:T(8,128)(2,1)} %inter_ref.3, f32[1,128,128]{2,1,0:T(8,128)} %ints_ref.3), custom_call_target="tpu_custom_call" | custom-call | flops 33554432 | tf_op jit(solution)/shard_map/coupling/pallas_call | solution.py:285
  63.0 1.2 %collective-permute-done.18.refs_2_ = bf16[2,128,128]{2,1,0:T(8,128)(2,1)S(1)} collective-permute-done((bf16[2,128,128]{2,1,0:T(8,128)(2,1)S(1)}, bf16[2,128,128]{2,1,0:T(8,128)(2,1)S(1)}, u32[]{:S(2)}, u32[]{:S(2)}) %collective-permute-start.18) | collective-permute-done | bytes 65568 | tf_op jit(solution)/shard_map/ppermute | solution.py:33
  64.2 1.9 %collective-permute-done.19.refs_3_ = bf16[2,128,128]{2,1,0:T(8,128)(2,1)S(1)} collective-permute-done((bf16[2,128,128]{2,1,0:T(8,128)(2,1)S(1)}, bf16[2,128,128]{2,1,0:T(8,128)(2,1)S(1)}, u32[]{:S(2)}, u32[]{:S(2)}) %collective-permute-start.19) | collective-permute-done | bytes 65568 | tf_op jit(solution)/shard_map/ppermute | solution.py:33
  66.1 1.7 %collective-permute-start.21 = (bf16[1,128,128]{2,1,0:T(8,128)(2,1)S(1)}, bf16[1,128,128]{2,1,0:T(8,128)(2,1)S(1)}, u32[]{:S(2)}, u32[]{:S(2)}) collective-permute-start(bf16[1,128,128]{2,1,0:T(8,128)(2,1)S(1)} %get-tuple-element.72), channel_id=1, source_target_pairs={{0,4},{1,5},{2,6},{3,7},{4,0},{5,1},{6,2},{7,3},{8,12},{9,13},{10,... | collective-permute-start | bytes 98312 | tf_op jit(solution)/shard_map/ppermute | solution.py:33
  67.8 3.6 %collective-permute-done.21.refs_1_ = bf16[1,128,128]{2,1,0:T(8,128)(2,1)S(1)} collective-permute-done((bf16[1,128,128]{2,1,0:T(8,128)(2,1)S(1)}, bf16[1,128,128]{2,1,0:T(8,128)(2,1)S(1)}, u32[]{:S(2)}, u32[]{:S(2)}) %collective-permute-start.21) | collective-permute-done | bytes 32800 | tf_op jit(solution)/shard_map/ppermute | solution.py:33
  (42 shorter events, 6.4 us)
Async XLA Ops:
  1.3 5.9 %collective-permute-start = (f32[1,128]{1,0:T(1,128)S(1)}, f32[1,128]{1,0:T(1,128)S(1)}, u32[]{:S(2)}, u32[]{:S(2)}) collective-permute-start(f32[1,128]{1,0:T(1,128)S(1)} %broadcast_add_fusion.refs_6_.refs_3_), channel_id=1, source_target_pairs={{0,4},{1,5},{2,6},{3,7},{4,0},{5,1},{6,2},{7,3},{8,12},{9,13},{10,... | collective-permute-start | bytes 1544 | tf_op jit(solution)/shard_map/ppermute | solution.py:33
  5.3 7.1 %collective-permute-start.1 = (bf16[1,256,128]{2,1,0:T(8,128)(2,1)}, bf16[1,256,128]{2,1,0:T(8,128)(2,1)S(1)}, u32[]{:S(2)}, u32[]{:S(2)}) collective-permute-start(bf16[1,256,128]{2,1,0:T(8,128)(2,1)} %value_ref.1), channel_id=1, source_target_pairs={{0,4},{1,5},{2,6},{3,7},{4,0},{5,1},{6,2},{7,3},{8,12},{9,13},{10,... | collective-permute-start | bytes 196616 | tf_op jit(solution)/shard_map/ppermute | solution.py:33
  6.3 0.8 %copy-start = (bf16[1,256,128]{2,1,0:T(8,128)(2,1)S(1)}, bf16[1,256,128]{2,1,0:T(8,128)(2,1)}, u32[]{:S(2)}) copy-start(bf16[1,256,128]{2,1,0:T(8,128)(2,1)} %value_ref.1) | copy-start | bytes 196612
  7.2 9.6 %collective-permute-start.2 = (bf16[1,128,128]{2,1,0:T(8,128)(2,1)}, bf16[1,128,128]{2,1,0:T(8,128)(2,1)S(1)}, u32[]{:S(2)}, u32[]{:S(2)}) collective-permute-start(bf16[1,128,128]{2,1,0:T(8,128)(2,1)} %param.9), channel_id=1, source_target_pairs={{0,4},{1,5},{2,6},{3,7},{4,0},{5,1},{6,2},{7,3},{8,12},{9,13},{10,... | collective-permute-start | bytes 98312 | tf_op jit(solution)/shard_map/ppermute | solution.py:33
  12.4 6.3 %collective-permute-start.6 = (bf16[2,256,128]{2,1,0:T(8,128)(2,1)S(1)}, bf16[2,256,128]{2,1,0:T(8,128)(2,1)S(1)}, u32[]{:S(2)}, u32[]{:S(2)}) collective-permute-start(bf16[2,256,128]{2,1,0:T(8,128)(2,1)S(1)} %join.1.refs_1_), channel_id=1, source_target_pairs={{0,1},{1,0},{2,3},{3,2},{4,5},{5,4},{6,7},{7,6},{8,9},{9,8},{10,11... | collective-permute-start | bytes 393224 | tf_op jit(solution)/shard_map/ppermute | solution.py:33
  14.1 6.4 %collective-permute-start.7 = (bf16[2,256,128]{2,1,0:T(8,128)(2,1)S(1)}, bf16[2,256,128]{2,1,0:T(8,128)(2,1)S(1)}, u32[]{:S(2)}, u32[]{:S(2)}) collective-permute-start(bf16[2,256,128]{2,1,0:T(8,128)(2,1)S(1)} %join.1.refs_1_), channel_id=1, source_target_pairs={{0,2},{1,3},{2,0},{3,1},{4,6},{5,7},{6,4},{7,5},{8,10},{9,11},{10,... | collective-permute-start | bytes 393224 | tf_op jit(solution)/shard_map/ppermute | solution.py:33
  14.3 6.9 %collective-permute-start.8 = (bf16[2,256,128]{2,1,0:T(8,128)(2,1)S(1)}, bf16[2,256,128]{2,1,0:T(8,128)(2,1)S(1)}, u32[]{:S(2)}, u32[]{:S(2)}) collective-permute-start(bf16[2,256,128]{2,1,0:T(8,128)(2,1)S(1)} %join.1.refs_1_), channel_id=1, source_target_pairs={{0,3},{1,2},{2,1},{3,0},{4,7},{5,6},{6,5},{7,4},{8,11},{9,10},{10,... | collective-permute-start | bytes 393224 | tf_op jit(solution)/shard_map/ppermute | solution.py:33
  16.8 10.6 %collective-permute-start.3 = (bf16[2,128,128]{2,1,0:T(8,128)(2,1)S(1)}, bf16[2,128,128]{2,1,0:T(8,128)(2,1)S(1)}, u32[]{:S(2)}, u32[]{:S(2)}) collective-permute-start(bf16[2,128,128]{2,1,0:T(8,128)(2,1)S(1)} %constant_dynamic-update-slice_fusion.refs_0_.refs_2_), channel_id=1, source_target_pairs={{0,1},{1,0},{2,3},{3,2},{4,5},{5,4},{6,7},{7,6},{8,9},{9,8},{10,11... | collective-permute-start | bytes 196616 | tf_op jit(solution)/shard_map/ppermute | solution.py:33
  18.5 9.0 %collective-permute-start.4 = (bf16[2,128,128]{2,1,0:T(8,128)(2,1)S(1)}, bf16[2,128,128]{2,1,0:T(8,128)(2,1)S(1)}, u32[]{:S(2)}, u32[]{:S(2)}) collective-permute-start(bf16[2,128,128]{2,1,0:T(8,128)(2,1)S(1)} %constant_dynamic-update-slice_fusion.refs_0_.refs_2_), channel_id=1, source_target_pairs={{0,2},{1,3},{2,0},{3,1},{4,6},{5,7},{6,4},{7,5},{8,10},{9,11},{10,... | collective-permute-start | bytes 196616 | tf_op jit(solution)/shard_map/ppermute | solution.py:33
  18.8 8.6 %collective-permute-start.5 = (bf16[2,128,128]{2,1,0:T(8,128)(2,1)S(1)}, bf16[2,128,128]{2,1,0:T(8,128)(2,1)S(1)}, u32[]{:S(2)}, u32[]{:S(2)}) collective-permute-start(bf16[2,128,128]{2,1,0:T(8,128)(2,1)S(1)} %constant_dynamic-update-slice_fusion.refs_0_.refs_2_), channel_id=1, source_target_pairs={{0,3},{1,2},{2,1},{3,0},{4,7},{5,6},{6,5},{7,4},{8,11},{9,10},{10,... | collective-permute-start | bytes 196616 | tf_op jit(solution)/shard_map/ppermute | solution.py:33
  21.1 14.6 %copy-start.2 = (f32[1,128]{1,0:T(1,128)S(1)}, f32[1,128]{1,0:T(1,128)}, u32[]{:S(2)}) copy-start(f32[1,128]{1,0:T(1,128)} %param.14) | copy-start | bytes 1540
  21.1 14.8 %copy-start.1 = (s32[1,4]{1,0:T(1,128)S(1)}, s32[1,4]{1,0:T(1,128)}, u32[]{:S(2)}) copy-start(s32[1,4]{1,0:T(1,128)} %near.3) | copy-start | bytes 52
  27.5 8.5 %collective-permute-start.12 = (bf16[8,128,128]{2,1,0:T(8,128)(2,1)S(1)}, bf16[8,128,128]{2,1,0:T(8,128)(2,1)S(1)}, u32[]{:S(2)}, u32[]{:S(2)}) collective-permute-start(bf16[8,128,128]{2,1,0:T(8,128)(2,1)S(1)} %stack.2.own_ref), channel_id=1, source_target_pairs={{8,0},{16,8},{24,16},{9,1},{17,9},{25,17},{10,2},{18,10},{26,18},{... | collective-permute-start | bytes 786440 | tf_op jit(solution)/shard_map/ppermute | solution.py:90
  32.1 5.2 %collective-permute-start.9 = (bf16[2,128,128]{2,1,0:T(8,128)(2,1)S(1)}, bf16[2,128,128]{2,1,0:T(8,128)(2,1)S(1)}, u32[]{:S(2)}, u32[]{:S(2)}) collective-permute-start(bf16[2,128,128]{2,1,0:T(8,128)(2,1)S(1)} %get-tuple-element.55), channel_id=1, source_target_pairs={{0,1},{1,0},{2,3},{3,2},{4,5},{5,4},{6,7},{7,6},{8,9},{9,8},{10,11... | collective-permute-start | bytes 196616 | tf_op jit(solution)/shard_map/ppermute | solution.py:33
  33.8 5.0 %collective-permute-start.10 = (bf16[2,128,128]{2,1,0:T(8,128)(2,1)S(1)}, bf16[2,128,128]{2,1,0:T(8,128)(2,1)S(1)}, u32[]{:S(2)}, u32[]{:S(2)}) collective-permute-start(bf16[2,128,128]{2,1,0:T(8,128)(2,1)S(1)} %get-tuple-element.56), channel_id=1, source_target_pairs={{0,2},{1,3},{2,0},{3,1},{4,6},{5,7},{6,4},{7,5},{8,10},{9,11},{10,... | collective-permute-start | bytes 196616 | tf_op jit(solution)/shard_map/ppermute | solution.py:33
  34.7 5.5 %collective-permute-start.11 = (bf16[2,128,128]{2,1,0:T(8,128)(2,1)S(1)}, bf16[2,128,128]{2,1,0:T(8,128)(2,1)S(1)}, u32[]{:S(2)}, u32[]{:S(2)}) collective-permute-start(bf16[2,128,128]{2,1,0:T(8,128)(2,1)S(1)} %get-tuple-element.57), channel_id=1, source_target_pairs={{0,3},{1,2},{2,1},{3,0},{4,7},{5,6},{6,5},{7,4},{8,11},{9,10},{10,... | collective-permute-start | bytes 196616 | tf_op jit(solution)/shard_map/ppermute | solution.py:33
  40.3 6.2 %collective-permute-start.13 = (bf16[2,128,128]{2,1,0:T(8,128)(2,1)S(1)}, bf16[2,128,128]{2,1,0:T(8,128)(2,1)S(1)}, u32[]{:S(2)}, u32[]{:S(2)}) collective-permute-start(bf16[2,128,128]{2,1,0:T(8,128)(2,1)S(1)} %get-tuple-element.61), channel_id=1, source_target_pairs={{0,4},{1,5},{2,6},{3,7},{4,0},{5,1},{6,2},{7,3},{8,12},{9,13},{10,... | collective-permute-start | bytes 196616 | tf_op jit(solution)/shard_map/ppermute | solution.py:33
  46.5 4.3 %collective-permute-start.14 = (bf16[2,128,128]{2,1,0:T(8,128)(2,1)S(1)}, bf16[2,128,128]{2,1,0:T(8,128)(2,1)S(1)}, u32[]{:S(2)}, u32[]{:S(2)}) collective-permute-start(bf16[2,128,128]{2,1,0:T(8,128)(2,1)S(1)} %finish.2.refs_0_.refs_2_), channel_id=1, source_target_pairs={{0,1},{1,0},{2,3},{3,2},{4,5},{5,4},{6,7},{7,6},{8,9},{9,8},{10,11... | collective-permute-start | bytes 196616 | tf_op jit(solution)/shard_map/ppermute | solution.py:33
  48.2 4.3 %collective-permute-start.15 = (bf16[2,128,128]{2,1,0:T(8,128)(2,1)S(1)}, bf16[2,128,128]{2,1,0:T(8,128)(2,1)S(1)}, u32[]{:S(2)}, u32[]{:S(2)}) collective-permute-start(bf16[2,128,128]{2,1,0:T(8,128)(2,1)S(1)} %finish.2.refs_0_.refs_2_), channel_id=1, source_target_pairs={{0,2},{1,3},{2,0},{3,1},{4,6},{5,7},{6,4},{7,5},{8,10},{9,11},{10,... | collective-permute-start | bytes 196616 | tf_op jit(solution)/shard_map/ppermute | solution.py:33
  48.2 5.2 %collective-permute-start.16 = (bf16[2,128,128]{2,1,0:T(8,128)(2,1)S(1)}, bf16[2,128,128]{2,1,0:T(8,128)(2,1)S(1)}, u32[]{:S(2)}, u32[]{:S(2)}) collective-permute-start(bf16[2,128,128]{2,1,0:T(8,128)(2,1)S(1)} %finish.2.refs_0_.refs_2_), channel_id=1, source_target_pairs={{0,3},{1,2},{2,1},{3,0},{4,7},{5,6},{6,5},{7,4},{8,11},{9,10},{10,... | collective-permute-start | bytes 196616 | tf_op jit(solution)/shard_map/ppermute | solution.py:33
  53.4 8.2 %collective-permute-start.20 = (bf16[8,128,128]{2,1,0:T(8,128)(2,1)S(1)}, bf16[8,128,128]{2,1,0:T(8,128)(2,1)S(1)}, u32[]{:S(2)}, u32[]{:S(2)}) collective-permute-start(bf16[8,128,128]{2,1,0:T(8,128)(2,1)S(1)} %stack.3.own_ref), channel_id=1, source_target_pairs={{8,0},{16,8},{24,16},{9,1},{17,9},{25,17},{10,2},{18,10},{26,18},{... | collective-permute-start | bytes 786440 | tf_op jit(solution)/shard_map/ppermute | solution.py:90
  58.0 5.0 %collective-permute-start.17 = (bf16[2,128,128]{2,1,0:T(8,128)(2,1)S(1)}, bf16[2,128,128]{2,1,0:T(8,128)(2,1)S(1)}, u32[]{:S(2)}, u32[]{:S(2)}) collective-permute-start(bf16[2,128,128]{2,1,0:T(8,128)(2,1)S(1)} %get-tuple-element.67), channel_id=1, source_target_pairs={{0,1},{1,0},{2,3},{3,2},{4,5},{5,4},{6,7},{7,6},{8,9},{9,8},{10,11... | collective-permute-start | bytes 196616 | tf_op jit(solution)/shard_map/ppermute | solution.py:33
  59.4 4.8 %collective-permute-start.18 = (bf16[2,128,128]{2,1,0:T(8,128)(2,1)S(1)}, bf16[2,128,128]{2,1,0:T(8,128)(2,1)S(1)}, u32[]{:S(2)}, u32[]{:S(2)}) collective-permute-start(bf16[2,128,128]{2,1,0:T(8,128)(2,1)S(1)} %get-tuple-element.68), channel_id=1, source_target_pairs={{0,2},{1,3},{2,0},{3,1},{4,6},{5,7},{6,4},{7,5},{8,10},{9,11},{10,... | collective-permute-start | bytes 196616 | tf_op jit(solution)/shard_map/ppermute | solution.py:33
  60.6 5.5 %collective-permute-start.19 = (bf16[2,128,128]{2,1,0:T(8,128)(2,1)S(1)}, bf16[2,128,128]{2,1,0:T(8,128)(2,1)S(1)}, u32[]{:S(2)}, u32[]{:S(2)}) collective-permute-start(bf16[2,128,128]{2,1,0:T(8,128)(2,1)S(1)} %get-tuple-element.69), channel_id=1, source_target_pairs={{0,3},{1,2},{2,1},{3,0},{4,7},{5,6},{6,5},{7,4},{8,11},{9,10},{10,... | collective-permute-start | bytes 196616 | tf_op jit(solution)/shard_map/ppermute | solution.py:33
  66.1 5.2 %collective-permute-start.21 = (bf16[1,128,128]{2,1,0:T(8,128)(2,1)S(1)}, bf16[1,128,128]{2,1,0:T(8,128)(2,1)S(1)}, u32[]{:S(2)}, u32[]{:S(2)}) collective-permute-start(bf16[1,128,128]{2,1,0:T(8,128)(2,1)S(1)} %get-tuple-element.72), channel_id=1, source_target_pairs={{0,4},{1,5},{2,6},{3,7},{4,0},{5,1},{6,2},{7,3},{8,12},{9,13},{10,... | collective-permute-start | bytes 98312 | tf_op jit(solution)/shard_map/ppermute | solution.py:33

commit v3 on v2

--- a/solution.py
+++ b/solution.py
@@ -217,16 +217,19 @@
             source = tail
         else:
             source = proj_ref.at[s]
-        flat = source[...].reshape(half * npno, 2 * npno)
-        mixed[...] = jnp.dot(flat, twice[...], preferred_element_type=F32).astype(BF16)
         total = jnp.zeros((npno, npno), F32)
-        for m in range(half):
-            total = total + lax.dot_general(
-                mixed[pl.ds(m * npno, npno), :],
-                source[m],
-                CONTRACT_LAST,
-                preferred_element_type=F32,
-            )
+        chunk = min(4, half)
+        for c in range(0, half, chunk):
+            part = pl.ds(c * npno, chunk * npno)
+            flat = source[pl.ds(c, chunk)].reshape(chunk * npno, 2 * npno)
+            mixed[part, :] = jnp.dot(flat, twice[...], preferred_element_type=F32).astype(BF16)
+            for m in range(c, c + chunk):
+                total = total + lax.dot_general(
+                    mixed[pl.ds(m * npno, npno), :],
+                    source[m],
+                    CONTRACT_LAST,
+                    preferred_element_type=F32,
+                )
         narrow = total.astype(BF16)
         for j in range(given):
 

time: 72.2 us -> 72.4 us (level)
  no operation moved by 1% of the time
where the time goes in v3:
time: 72.4 us; the launch traced here: 72.1 us
  starting transfers between devices  30.1 us (42%)
  waiting for transfers between devices  20.9 us (29%)
  Pallas kernels  16.9 us (23%)
  local copies, waits for them, and re-layouts  1.84 us (3%)
  other arithmetic  1.61 us (2%)
  between operations  0.82 us (1%)
    ppermute x20, starting transfers between devices, exchange(): return lax.ppermute(value, axis, [(d, d ^ offset) for d in range(count)])  27.5 us
    ppermute x20, waiting for transfers between devices, exchange(): return lax.ppermute(value, axis, [(d, d ^ offset) for d in range(count)])  20.9 us
    pallas_call x2, Pallas kernels, ladder(): pl.pallas_call(kernel, in_specs=[smem_spec()] * 2 + [vmem_spec()] * (give...  6.78 us
    pallas_call x1, Pallas kernels, project(): pl.pallas_call(kernel, in_specs=[smem_spec()] + [vmem_spec()] * given + [...  6.28 us
    pallas_call x2, Pallas kernels, coupling(): pl.pallas_call(coupling_kernel, in_specs=[smem_spec()] + [pl.BlockSpec()]...  2.79 us
    ppermute x2, starting transfers between devices, from_next(): return lax.ppermute(value, axis, [(d, d - 1) for d in range(1, count)])  2.58 us
    unnamed x7, local copies, waits for them, and re-layouts  1.6 us
  transfers between devices with their start and end apart: 22, of which 12 were waited for; matrix products, arithmetic and copies ran while one was open for 3% of the time, Pallas kernels for 22%

profile of v3, /device:TPU:0, one launch (start us, length us, event | category | flops | bytes accessed | tf_op | source)
XLA Modules:
  0.0 72.1 jit_solution(11005924929935194677)
XLA Ops:
  1.3 4.0 %collective-permute-start = (f32[1,128]{1,0:T(1,128)S(1)}, f32[1,128]{1,0:T(1,128)S(1)}, u32[]{:S(2)}, u32[]{:S(2)}) collective-permute-start(f32[1,128]{1,0:T(1,128)S(1)} %broadcast_add_fusion.refs_6_.refs_3_), channel_id=1, source_target_pairs={{0,4},{1,5},{2,6},{3,7},{4,0},{5,1},{6,2},{7,3},{8,12},{9,13},{10,... | collective-permute-start | bytes 1544 | tf_op jit(solution)/shard_map/ppermute | solution.py:33
  7.2 3.0 %collective-permute-start.2 = (bf16[1,128,128]{2,1,0:T(8,128)(2,1)}, bf16[1,128,128]{2,1,0:T(8,128)(2,1)S(1)}, u32[]{:S(2)}, u32[]{:S(2)}) collective-permute-start(bf16[1,128,128]{2,1,0:T(8,128)(2,1)} %param.9), channel_id=1, source_target_pairs={{0,4},{1,5},{2,6},{3,7},{4,0},{5,1},{6,2},{7,3},{8,12},{9,13},{10,... | collective-permute-start | bytes 98312 | tf_op jit(solution)/shard_map/ppermute | solution.py:33
  10.2 2.3 %collective-permute-done.1.other_ref = bf16[1,256,128]{2,1,0:T(8,128)(2,1)S(1)} collective-permute-done((bf16[1,256,128]{2,1,0:T(8,128)(2,1)}, bf16[1,256,128]{2,1,0:T(8,128)(2,1)S(1)}, u32[]{:S(2)}, u32[]{:S(2)}) %collective-permute-start.1) | collective-permute-done | bytes 65568 | tf_op jit(solution)/shard_map/ppermute | solution.py:33
  12.4 1.7 %collective-permute-start.6 = (bf16[2,256,128]{2,1,0:T(8,128)(2,1)S(1)}, bf16[2,256,128]{2,1,0:T(8,128)(2,1)S(1)}, u32[]{:S(2)}, u32[]{:S(2)}) collective-permute-start(bf16[2,256,128]{2,1,0:T(8,128)(2,1)S(1)} %join.1.refs_1_), channel_id=1, source_target_pairs={{0,1},{1,0},{2,3},{3,2},{4,5},{5,4},{6,7},{7,6},{8,9},{9,8},{10,11... | collective-permute-start | bytes 393224 | tf_op jit(solution)/shard_map/ppermute | solution.py:33
  14.3 1.7 %collective-permute-start.8 = (bf16[2,256,128]{2,1,0:T(8,128)(2,1)S(1)}, bf16[2,256,128]{2,1,0:T(8,128)(2,1)S(1)}, u32[]{:S(2)}, u32[]{:S(2)}) collective-permute-start(bf16[2,256,128]{2,1,0:T(8,128)(2,1)S(1)} %join.1.refs_1_), channel_id=1, source_target_pairs={{0,3},{1,2},{2,1},{3,0},{4,7},{5,6},{6,5},{7,4},{8,11},{9,10},{10,... | collective-permute-start | bytes 393224 | tf_op jit(solution)/shard_map/ppermute | solution.py:33
  16.8 1.7 %collective-permute-start.3 = (bf16[2,128,128]{2,1,0:T(8,128)(2,1)S(1)}, bf16[2,128,128]{2,1,0:T(8,128)(2,1)S(1)}, u32[]{:S(2)}, u32[]{:S(2)}) collective-permute-start(bf16[2,128,128]{2,1,0:T(8,128)(2,1)S(1)} %constant_dynamic-update-slice_fusion.refs_0_.refs_2_), channel_id=1, source_target_pairs={{0,1},{1,0},{2,3},{3,2},{4,5},{5,4},{6,7},{7,6},{8,9},{9,8},{10,11... | collective-permute-start | bytes 196616 | tf_op jit(solution)/shard_map/ppermute | solution.py:33
  18.8 1.7 %collective-permute-start.5 = (bf16[2,128,128]{2,1,0:T(8,128)(2,1)S(1)}, bf16[2,128,128]{2,1,0:T(8,128)(2,1)S(1)}, u32[]{:S(2)}, u32[]{:S(2)}) collective-permute-start(bf16[2,128,128]{2,1,0:T(8,128)(2,1)S(1)} %constant_dynamic-update-slice_fusion.refs_0_.refs_2_), channel_id=1, source_target_pairs={{0,3},{1,2},{2,1},{3,0},{4,7},{5,6},{6,5},{7,4},{8,11},{9,10},{10,... | collective-permute-start | bytes 196616 | tf_op jit(solution)/shard_map/ppermute | solution.py:33
  21.1 6.3 %project.1 = (bf16[2,16,128,256]{3,2,1,0:T(8,128)(2,1)S(1)}, bf16[16,128,256]{2,1,0:T(8,128)(2,1)}) custom-call(s32[3]{0:T(128)S(1)} %get-tuple-element.74.refs_0_, bf16[2,256,128]{2,1,0:T(8,128)(2,1)S(1)} %join.1.refs_1_, bf16[2,256,128]{2,1,0:T(8,128)(2,1)S(1)} %collective-permute-done.6.refs_2_, bf16[2,256,128]{2,1,0:T(8,128)(2,1)S(1)} %collective-permute-done.7.refs_3_, ...), custom_call_target="tpu_custom_call" | custom-call | flops 2415919104 | bytes 4194304 | tf_op jit(solution)/shard_map/project/pallas_call | solution.py:170
  27.5 1.3 %collective-permute-start.12 = (bf16[8,128,128]{2,1,0:T(8,128)(2,1)S(1)}, bf16[8,128,128]{2,1,0:T(8,128)(2,1)S(1)}, u32[]{:S(2)}, u32[]{:S(2)}) collective-permute-start(bf16[8,128,128]{2,1,0:T(8,128)(2,1)S(1)} %stack.2.own_ref), channel_id=1, source_target_pairs={{8,0},{16,8},{24,16},{9,1},{17,9},{25,17},{10,2},{18,10},{26,18},{... | collective-permute-start | bytes 786440 | tf_op jit(solution)/shard_map/ppermute | solution.py:90
  28.8 3.4 %ladder.2 = (bf16[2,128,128]{2,1,0:T(8,128)(2,1)S(1)}, bf16[2,128,128]{2,1,0:T(8,128)(2,1)S(1)}, bf16[2,128,128]{2,1,0:T(8,128)(2,1)S(1)}, bf16[2,128,128]{2,1,0:T(8,128)(2,1)S(1)}) custom-call(s32[3]{0:T(128)S(1)} %get-tuple-element.74.refs_0_, s32[3]{0:T(128)S(1)} %get-tuple-element.73.refs_1_, ...), custom_call_target="tpu_custom_call" | custom-call | bytes 12582912 | tf_op jit(solution)/shard_map/ladder/pallas_call | solution.py:249
  32.2 1.7 %collective-permute-start.9 = (bf16[2,128,128]{2,1,0:T(8,128)(2,1)S(1)}, bf16[2,128,128]{2,1,0:T(8,128)(2,1)S(1)}, u32[]{:S(2)}, u32[]{:S(2)}) collective-permute-start(bf16[2,128,128]{2,1,0:T(8,128)(2,1)S(1)} %get-tuple-element.55), channel_id=1, source_target_pairs={{0,1},{1,0},{2,3},{3,2},{4,5},{5,4},{6,7},{7,6},{8,9},{9,8},{10,11... | collective-permute-start | bytes 196616 | tf_op jit(solution)/shard_map/ppermute | solution.py:33
  33.8 0.9 %collective-permute-start.10 = (bf16[2,128,128]{2,1,0:T(8,128)(2,1)S(1)}, bf16[2,128,128]{2,1,0:T(8,128)(2,1)S(1)}, u32[]{:S(2)}, u32[]{:S(2)}) collective-permute-start(bf16[2,128,128]{2,1,0:T(8,128)(2,1)S(1)} %get-tuple-element.56), channel_id=1, source_target_pairs={{0,2},{1,3},{2,0},{3,1},{4,6},{5,7},{6,4},{7,5},{8,10},{9,11},{10,... | collective-permute-start | bytes 196616 | tf_op jit(solution)/shard_map/ppermute | solution.py:33
  34.7 1.0 %collective-permute-start.11 = (bf16[2,128,128]{2,1,0:T(8,128)(2,1)S(1)}, bf16[2,128,128]{2,1,0:T(8,128)(2,1)S(1)}, u32[]{:S(2)}, u32[]{:S(2)}) collective-permute-start(bf16[2,128,128]{2,1,0:T(8,128)(2,1)S(1)} %get-tuple-element.57), channel_id=1, source_target_pairs={{0,3},{1,2},{2,1},{3,0},{4,7},{5,6},{6,5},{7,4},{8,11},{9,10},{10,... | collective-permute-start | bytes 196616 | tf_op jit(solution)/shard_map/ppermute | solution.py:33
  36.0 1.4 %coupling.2.refs_4_ = f32[128,128]{1,0:T(8,128)S(1)} custom-call(s32[1,4]{1,0:T(1,128)S(1)} %copy-done.1, bf16[8,128,128]{2,1,0:T(8,128)(2,1)S(1)} %stack.2.own_ref, bf16[8,128,128]{2,1,0:T(8,128)(2,1)S(1)} %collective-permute-done.12.next_ref, bf16[1,4,128,128]{3,2,1,0:T(8,128)(2,1)} %inter_ref.3, f32[1,128,128]{2,1,0:T(8,128)} %ints_ref.3), custom_call_target="tpu_custom_call" | custom-call | flops 33554432 | tf_op jit(solution)/shard_map/coupling/pallas_call | solution.py:288
  37.4 1.4 %collective-permute-done.10.refs_2_ = bf16[2,128,128]{2,1,0:T(8,128)(2,1)S(1)} collective-permute-done((bf16[2,128,128]{2,1,0:T(8,128)(2,1)S(1)}, bf16[2,128,128]{2,1,0:T(8,128)(2,1)S(1)}, u32[]{:S(2)}, u32[]{:S(2)}) %collective-permute-start.10) | collective-permute-done | bytes 65568 | tf_op jit(solution)/shard_map/ppermute | solution.py:33
  38.8 1.4 %collective-permute-done.11.refs_3_ = bf16[2,128,128]{2,1,0:T(8,128)(2,1)S(1)} collective-permute-done((bf16[2,128,128]{2,1,0:T(8,128)(2,1)S(1)}, bf16[2,128,128]{2,1,0:T(8,128)(2,1)S(1)}, u32[]{:S(2)}, u32[]{:S(2)}) %collective-permute-start.11) | collective-permute-done | bytes 65568 | tf_op jit(solution)/shard_map/ppermute | solution.py:33
  40.3 1.0 %collective-permute-start.13 = (bf16[2,128,128]{2,1,0:T(8,128)(2,1)S(1)}, bf16[2,128,128]{2,1,0:T(8,128)(2,1)S(1)}, u32[]{:S(2)}, u32[]{:S(2)}) collective-permute-start(bf16[2,128,128]{2,1,0:T(8,128)(2,1)S(1)} %get-tuple-element.61), channel_id=1, source_target_pairs={{0,4},{1,5},{2,6},{3,7},{4,0},{5,1},{6,2},{7,3},{8,12},{9,13},{10,... | collective-permute-start | bytes 196616 | tf_op jit(solution)/shard_map/ppermute | solution.py:33
  41.3 5.1 %collective-permute-done.13.refs_1_ = bf16[2,128,128]{2,1,0:T(8,128)(2,1)S(1)} collective-permute-done((bf16[2,128,128]{2,1,0:T(8,128)(2,1)S(1)}, bf16[2,128,128]{2,1,0:T(8,128)(2,1)S(1)}, u32[]{:S(2)}, u32[]{:S(2)}) %collective-permute-start.13) | collective-permute-done | bytes 65568 | tf_op jit(solution)/shard_map/ppermute | solution.py:33
  46.5 1.6 %collective-permute-start.14 = (bf16[2,128,128]{2,1,0:T(8,128)(2,1)S(1)}, bf16[2,128,128]{2,1,0:T(8,128)(2,1)S(1)}, u32[]{:S(2)}, u32[]{:S(2)}) collective-permute-start(bf16[2,128,128]{2,1,0:T(8,128)(2,1)S(1)} %finish.2.refs_0_.refs_2_), channel_id=1, source_target_pairs={{0,1},{1,0},{2,3},{3,2},{4,5},{5,4},{6,7},{7,6},{8,9},{9,8},{10,11... | collective-permute-start | bytes 196616 | tf_op jit(solution)/shard_map/ppermute | solution.py:33
  48.2 1.9 %collective-permute-start.16 = (bf16[2,128,128]{2,1,0:T(8,128)(2,1)S(1)}, bf16[2,128,128]{2,1,0:T(8,128)(2,1)S(1)}, u32[]{:S(2)}, u32[]{:S(2)}) collective-permute-start(bf16[2,128,128]{2,1,0:T(8,128)(2,1)S(1)} %finish.2.refs_0_.refs_2_), channel_id=1, source_target_pairs={{0,3},{1,2},{2,1},{3,0},{4,7},{5,6},{6,5},{7,4},{8,11},{9,10},{10,... | collective-permute-start | bytes 196616 | tf_op jit(solution)/shard_map/ppermute | solution.py:33
  50.9 1.6 %collective-permute-done.15.refs_2_.refs_4_ = bf16[2,128,128]{2,1,0:T(8,128)(2,1)S(1)} collective-permute-done((bf16[2,128,128]{2,1,0:T(8,128)(2,1)S(1)}, bf16[2,128,128]{2,1,0:T(8,128)(2,1)S(1)}, u32[]{:S(2)}, u32[]{:S(2)}) %collective-permute-start.15) | collective-permute-done | bytes 65568 | tf_op jit(solution)/shard_map/ppermute | solution.py:33
  52.5 0.9 %collective-permute-done.16.refs_3_.refs_5_ = bf16[2,128,128]{2,1,0:T(8,128)(2,1)S(1)} collective-permute-done((bf16[2,128,128]{2,1,0:T(8,128)(2,1)S(1)}, bf16[2,128,128]{2,1,0:T(8,128)(2,1)S(1)}, u32[]{:S(2)}, u32[]{:S(2)}) %collective-permute-start.16) | collective-permute-done | bytes 65568 | tf_op jit(solution)/shard_map/ppermute | solution.py:33
  53.4 1.3 %collective-permute-start.20 = (bf16[8,128,128]{2,1,0:T(8,128)(2,1)S(1)}, bf16[8,128,128]{2,1,0:T(8,128)(2,1)S(1)}, u32[]{:S(2)}, u32[]{:S(2)}) collective-permute-start(bf16[8,128,128]{2,1,0:T(8,128)(2,1)S(1)} %stack.3.own_ref), channel_id=1, source_target_pairs={{8,0},{16,8},{24,16},{9,1},{17,9},{25,17},{10,2},{18,10},{26,18},{... | collective-permute-start | bytes 786440 | tf_op jit(solution)/shard_map/ppermute | solution.py:90
  54.7 3.4 %ladder.3 = (bf16[2,128,128]{2,1,0:T(8,128)(2,1)S(1)}, bf16[2,128,128]{2,1,0:T(8,128)(2,1)S(1)}, bf16[2,128,128]{2,1,0:T(8,128)(2,1)S(1)}, bf16[2,128,128]{2,1,0:T(8,128)(2,1)S(1)}) custom-call(s32[3]{0:T(128)S(1)} %get-tuple-element.74.refs_0_, s32[3]{0:T(128)S(1)} %get-tuple-element.73.refs_1_, bf16[2,128,128]{2,1,0:T(8,128)(2,1)S(1)} %finish.2.refs_0_.refs_2_, ...), custom_call_target="tpu_custom_call" | custom-call | bytes 12582912 | tf_op jit(solution)/shard_map/ladder/pallas_call | solution.py:249
  58.1 1.3 %collective-permute-start.17 = (bf16[2,128,128]{2,1,0:T(8,128)(2,1)S(1)}, bf16[2,128,128]{2,1,0:T(8,128)(2,1)S(1)}, u32[]{:S(2)}, u32[]{:S(2)}) collective-permute-start(bf16[2,128,128]{2,1,0:T(8,128)(2,1)S(1)} %get-tuple-element.67), channel_id=1, source_target_pairs={{0,1},{1,0},{2,3},{3,2},{4,5},{5,4},{6,7},{7,6},{8,9},{9,8},{10,11... | collective-permute-start | bytes 196616 | tf_op jit(solution)/shard_map/ppermute | solution.py:33
  59.4 1.2 %collective-permute-start.18 = (bf16[2,128,128]{2,1,0:T(8,128)(2,1)S(1)}, bf16[2,128,128]{2,1,0:T(8,128)(2,1)S(1)}, u32[]{:S(2)}, u32[]{:S(2)}) collective-permute-start(bf16[2,128,128]{2,1,0:T(8,128)(2,1)S(1)} %get-tuple-element.68), channel_id=1, source_target_pairs={{0,2},{1,3},{2,0},{3,1},{4,6},{5,7},{6,4},{7,5},{8,10},{9,11},{10,... | collective-permute-start | bytes 196616 | tf_op jit(solution)/shard_map/ppermute | solution.py:33
  60.6 1.0 %collective-permute-start.19 = (bf16[2,128,128]{2,1,0:T(8,128)(2,1)S(1)}, bf16[2,128,128]{2,1,0:T(8,128)(2,1)S(1)}, u32[]{:S(2)}, u32[]{:S(2)}) collective-permute-start(bf16[2,128,128]{2,1,0:T(8,128)(2,1)S(1)} %get-tuple-element.69), channel_id=1, source_target_pairs={{0,3},{1,2},{2,1},{3,0},{4,7},{5,6},{6,5},{7,4},{8,11},{9,10},{10,... | collective-permute-start | bytes 196616 | tf_op jit(solution)/shard_map/ppermute | solution.py:33
  61.6 1.4 %coupling.3.refs_4_ = f32[128,128]{1,0:T(8,128)S(1)} custom-call(s32[1,4]{1,0:T(1,128)S(1)} %copy-done.1, bf16[8,128,128]{2,1,0:T(8,128)(2,1)S(1)} %stack.3.own_ref, bf16[8,128,128]{2,1,0:T(8,128)(2,1)S(1)} %collective-permute-done.20.next_ref, bf16[1,4,128,128]{3,2,1,0:T(8,128)(2,1)} %inter_ref.3, f32[1,128,128]{2,1,0:T(8,128)} %ints_ref.3), custom_call_target="tpu_custom_call" | custom-call | flops 33554432 | tf_op jit(solution)/shard_map/coupling/pallas_call | solution.py:288
  63.0 1.2 %collective-permute-done.18.refs_2_ = bf16[2,128,128]{2,1,0:T(8,128)(2,1)S(1)} collective-permute-done((bf16[2,128,128]{2,1,0:T(8,128)(2,1)S(1)}, bf16[2,128,128]{2,1,0:T(8,128)(2,1)S(1)}, u32[]{:S(2)}, u32[]{:S(2)}) %collective-permute-start.18) | collective-permute-done | bytes 65568 | tf_op jit(solution)/shard_map/ppermute | solution.py:33
  64.2 1.8 %collective-permute-done.19.refs_3_ = bf16[2,128,128]{2,1,0:T(8,128)(2,1)S(1)} collective-permute-done((bf16[2,128,128]{2,1,0:T(8,128)(2,1)S(1)}, bf16[2,128,128]{2,1,0:T(8,128)(2,1)S(1)}, u32[]{:S(2)}, u32[]{:S(2)}) %collective-permute-start.19) | collective-permute-done | bytes 65568 | tf_op jit(solution)/shard_map/ppermute | solution.py:33
  66.1 1.7 %collective-permute-start.21 = (bf16[1,128,128]{2,1,0:T(8,128)(2,1)S(1)}, bf16[1,128,128]{2,1,0:T(8,128)(2,1)S(1)}, u32[]{:S(2)}, u32[]{:S(2)}) collective-permute-start(bf16[1,128,128]{2,1,0:T(8,128)(2,1)S(1)} %get-tuple-element.72), channel_id=1, source_target_pairs={{0,4},{1,5},{2,6},{3,7},{4,0},{5,1},{6,2},{7,3},{8,12},{9,13},{10,... | collective-permute-start | bytes 98312 | tf_op jit(solution)/shard_map/ppermute | solution.py:33
  67.8 3.5 %collective-permute-done.21.refs_1_ = bf16[1,128,128]{2,1,0:T(8,128)(2,1)S(1)} collective-permute-done((bf16[1,128,128]{2,1,0:T(8,128)(2,1)S(1)}, bf16[1,128,128]{2,1,0:T(8,128)(2,1)S(1)}, u32[]{:S(2)}, u32[]{:S(2)}) %collective-permute-start.21) | collective-permute-done | bytes 32800 | tf_op jit(solution)/shard_map/ppermute | solution.py:33
  (42 shorter events, 6.4 us)
Async XLA Ops:
  1.3 5.9 %collective-permute-start = (f32[1,128]{1,0:T(1,128)S(1)}, f32[1,128]{1,0:T(1,128)S(1)}, u32[]{:S(2)}, u32[]{:S(2)}) collective-permute-start(f32[1,128]{1,0:T(1,128)S(1)} %broadcast_add_fusion.refs_6_.refs_3_), channel_id=1, source_target_pairs={{0,4},{1,5},{2,6},{3,7},{4,0},{5,1},{6,2},{7,3},{8,12},{9,13},{10,... | collective-permute-start | bytes 1544 | tf_op jit(solution)/shard_map/ppermute | solution.py:33
  5.3 7.1 %collective-permute-start.1 = (bf16[1,256,128]{2,1,0:T(8,128)(2,1)}, bf16[1,256,128]{2,1,0:T(8,128)(2,1)S(1)}, u32[]{:S(2)}, u32[]{:S(2)}) collective-permute-start(bf16[1,256,128]{2,1,0:T(8,128)(2,1)} %value_ref.1), channel_id=1, source_target_pairs={{0,4},{1,5},{2,6},{3,7},{4,0},{5,1},{6,2},{7,3},{8,12},{9,13},{10,... | collective-permute-start | bytes 196616 | tf_op jit(solution)/shard_map/ppermute | solution.py:33
  6.3 0.8 %copy-start = (bf16[1,256,128]{2,1,0:T(8,128)(2,1)S(1)}, bf16[1,256,128]{2,1,0:T(8,128)(2,1)}, u32[]{:S(2)}) copy-start(bf16[1,256,128]{2,1,0:T(8,128)(2,1)} %value_ref.1) | copy-start | bytes 196612
  7.2 9.6 %collective-permute-start.2 = (bf16[1,128,128]{2,1,0:T(8,128)(2,1)}, bf16[1,128,128]{2,1,0:T(8,128)(2,1)S(1)}, u32[]{:S(2)}, u32[]{:S(2)}) collective-permute-start(bf16[1,128,128]{2,1,0:T(8,128)(2,1)} %param.9), channel_id=1, source_target_pairs={{0,4},{1,5},{2,6},{3,7},{4,0},{5,1},{6,2},{7,3},{8,12},{9,13},{10,... | collective-permute-start | bytes 98312 | tf_op jit(solution)/shard_map/ppermute | solution.py:33
  12.4 6.3 %collective-permute-start.6 = (bf16[2,256,128]{2,1,0:T(8,128)(2,1)S(1)}, bf16[2,256,128]{2,1,0:T(8,128)(2,1)S(1)}, u32[]{:S(2)}, u32[]{:S(2)}) collective-permute-start(bf16[2,256,128]{2,1,0:T(8,128)(2,1)S(1)} %join.1.refs_1_), channel_id=1, source_target_pairs={{0,1},{1,0},{2,3},{3,2},{4,5},{5,4},{6,7},{7,6},{8,9},{9,8},{10,11... | collective-permute-start | bytes 393224 | tf_op jit(solution)/shard_map/ppermute | solution.py:33
  14.1 6.4 %collective-permute-start.7 = (bf16[2,256,128]{2,1,0:T(8,128)(2,1)S(1)}, bf16[2,256,128]{2,1,0:T(8,128)(2,1)S(1)}, u32[]{:S(2)}, u32[]{:S(2)}) collective-permute-start(bf16[2,256,128]{2,1,0:T(8,128)(2,1)S(1)} %join.1.refs_1_), channel_id=1, source_target_pairs={{0,2},{1,3},{2,0},{3,1},{4,6},{5,7},{6,4},{7,5},{8,10},{9,11},{10,... | collective-permute-start | bytes 393224 | tf_op jit(solution)/shard_map/ppermute | solution.py:33
  14.3 6.9 %collective-permute-start.8 = (bf16[2,256,128]{2,1,0:T(8,128)(2,1)S(1)}, bf16[2,256,128]{2,1,0:T(8,128)(2,1)S(1)}, u32[]{:S(2)}, u32[]{:S(2)}) collective-permute-start(bf16[2,256,128]{2,1,0:T(8,128)(2,1)S(1)} %join.1.refs_1_), channel_id=1, source_target_pairs={{0,3},{1,2},{2,1},{3,0},{4,7},{5,6},{6,5},{7,4},{8,11},{9,10},{10,... | collective-permute-start | bytes 393224 | tf_op jit(solution)/shard_map/ppermute | solution.py:33
  16.8 10.6 %collective-permute-start.3 = (bf16[2,128,128]{2,1,0:T(8,128)(2,1)S(1)}, bf16[2,128,128]{2,1,0:T(8,128)(2,1)S(1)}, u32[]{:S(2)}, u32[]{:S(2)}) collective-permute-start(bf16[2,128,128]{2,1,0:T(8,128)(2,1)S(1)} %constant_dynamic-update-slice_fusion.refs_0_.refs_2_), channel_id=1, source_target_pairs={{0,1},{1,0},{2,3},{3,2},{4,5},{5,4},{6,7},{7,6},{8,9},{9,8},{10,11... | collective-permute-start | bytes 196616 | tf_op jit(solution)/shard_map/ppermute | solution.py:33
  18.5 9.0 %collective-permute-start.4 = (bf16[2,128,128]{2,1,0:T(8,128)(2,1)S(1)}, bf16[2,128,128]{2,1,0:T(8,128)(2,1)S(1)}, u32[]{:S(2)}, u32[]{:S(2)}) collective-permute-start(bf16[2,128,128]{2,1,0:T(8,128)(2,1)S(1)} %constant_dynamic-update-slice_fusion.refs_0_.refs_2_), channel_id=1, source_target_pairs={{0,2},{1,3},{2,0},{3,1},{4,6},{5,7},{6,4},{7,5},{8,10},{9,11},{10,... | collective-permute-start | bytes 196616 | tf_op jit(solution)/shard_map/ppermute | solution.py:33
  18.8 8.6 %collective-permute-start.5 = (bf16[2,128,128]{2,1,0:T(8,128)(2,1)S(1)}, bf16[2,128,128]{2,1,0:T(8,128)(2,1)S(1)}, u32[]{:S(2)}, u32[]{:S(2)}) collective-permute-start(bf16[2,128,128]{2,1,0:T(8,128)(2,1)S(1)} %constant_dynamic-update-slice_fusion.refs_0_.refs_2_), channel_id=1, source_target_pairs={{0,3},{1,2},{2,1},{3,0},{4,7},{5,6},{6,5},{7,4},{8,11},{9,10},{10,... | collective-permute-start | bytes 196616 | tf_op jit(solution)/shard_map/ppermute | solution.py:33
  21.1 14.6 %copy-start.2 = (f32[1,128]{1,0:T(1,128)S(1)}, f32[1,128]{1,0:T(1,128)}, u32[]{:S(2)}) copy-start(f32[1,128]{1,0:T(1,128)} %param.14) | copy-start | bytes 1540
  21.1 14.8 %copy-start.1 = (s32[1,4]{1,0:T(1,128)S(1)}, s32[1,4]{1,0:T(1,128)}, u32[]{:S(2)}) copy-start(s32[1,4]{1,0:T(1,128)} %near.3) | copy-start | bytes 52
  27.5 8.5 %collective-permute-start.12 = (bf16[8,128,128]{2,1,0:T(8,128)(2,1)S(1)}, bf16[8,128,128]{2,1,0:T(8,128)(2,1)S(1)}, u32[]{:S(2)}, u32[]{:S(2)}) collective-permute-start(bf16[8,128,128]{2,1,0:T(8,128)(2,1)S(1)} %stack.2.own_ref), channel_id=1, source_target_pairs={{8,0},{16,8},{24,16},{9,1},{17,9},{25,17},{10,2},{18,10},{26,18},{... | collective-permute-start | bytes 786440 | tf_op jit(solution)/shard_map/ppermute | solution.py:90
  32.2 5.2 %collective-permute-start.9 = (bf16[2,128,128]{2,1,0:T(8,128)(2,1)S(1)}, bf16[2,128,128]{2,1,0:T(8,128)(2,1)S(1)}, u32[]{:S(2)}, u32[]{:S(2)}) collective-permute-start(bf16[2,128,128]{2,1,0:T(8,128)(2,1)S(1)} %get-tuple-element.55), channel_id=1, source_target_pairs={{0,1},{1,0},{2,3},{3,2},{4,5},{5,4},{6,7},{7,6},{8,9},{9,8},{10,11... | collective-permute-start | bytes 196616 | tf_op jit(solution)/shard_map/ppermute | solution.py:33
  33.8 5.0 %collective-permute-start.10 = (bf16[2,128,128]{2,1,0:T(8,128)(2,1)S(1)}, bf16[2,128,128]{2,1,0:T(8,128)(2,1)S(1)}, u32[]{:S(2)}, u32[]{:S(2)}) collective-permute-start(bf16[2,128,128]{2,1,0:T(8,128)(2,1)S(1)} %get-tuple-element.56), channel_id=1, source_target_pairs={{0,2},{1,3},{2,0},{3,1},{4,6},{5,7},{6,4},{7,5},{8,10},{9,11},{10,... | collective-permute-start | bytes 196616 | tf_op jit(solution)/shard_map/ppermute | solution.py:33
  34.7 5.5 %collective-permute-start.11 = (bf16[2,128,128]{2,1,0:T(8,128)(2,1)S(1)}, bf16[2,128,128]{2,1,0:T(8,128)(2,1)S(1)}, u32[]{:S(2)}, u32[]{:S(2)}) collective-permute-start(bf16[2,128,128]{2,1,0:T(8,128)(2,1)S(1)} %get-tuple-element.57), channel_id=1, source_target_pairs={{0,3},{1,2},{2,1},{3,0},{4,7},{5,6},{6,5},{7,4},{8,11},{9,10},{10,... | collective-permute-start | bytes 196616 | tf_op jit(solution)/shard_map/ppermute | solution.py:33
  40.3 6.2 %collective-permute-start.13 = (bf16[2,128,128]{2,1,0:T(8,128)(2,1)S(1)}, bf16[2,128,128]{2,1,0:T(8,128)(2,1)S(1)}, u32[]{:S(2)}, u32[]{:S(2)}) collective-permute-start(bf16[2,128,128]{2,1,0:T(8,128)(2,1)S(1)} %get-tuple-element.61), channel_id=1, source_target_pairs={{0,4},{1,5},{2,6},{3,7},{4,0},{5,1},{6,2},{7,3},{8,12},{9,13},{10,... | collective-permute-start | bytes 196616 | tf_op jit(solution)/shard_map/ppermute | solution.py:33
  46.5 4.3 %collective-permute-start.14 = (bf16[2,128,128]{2,1,0:T(8,128)(2,1)S(1)}, bf16[2,128,128]{2,1,0:T(8,128)(2,1)S(1)}, u32[]{:S(2)}, u32[]{:S(2)}) collective-permute-start(bf16[2,128,128]{2,1,0:T(8,128)(2,1)S(1)} %finish.2.refs_0_.refs_2_), channel_id=1, source_target_pairs={{0,1},{1,0},{2,3},{3,2},{4,5},{5,4},{6,7},{7,6},{8,9},{9,8},{10,11... | collective-permute-start | bytes 196616 | tf_op jit(solution)/shard_map/ppermute | solution.py:33
  48.2 4.3 %collective-permute-start.15 = (bf16[2,128,128]{2,1,0:T(8,128)(2,1)S(1)}, bf16[2,128,128]{2,1,0:T(8,128)(2,1)S(1)}, u32[]{:S(2)}, u32[]{:S(2)}) collective-permute-start(bf16[2,128,128]{2,1,0:T(8,128)(2,1)S(1)} %finish.2.refs_0_.refs_2_), channel_id=1, source_target_pairs={{0,2},{1,3},{2,0},{3,1},{4,6},{5,7},{6,4},{7,5},{8,10},{9,11},{10,... | collective-permute-start | bytes 196616 | tf_op jit(solution)/shard_map/ppermute | solution.py:33
  48.2 5.2 %collective-permute-start.16 = (bf16[2,128,128]{2,1,0:T(8,128)(2,1)S(1)}, bf16[2,128,128]{2,1,0:T(8,128)(2,1)S(1)}, u32[]{:S(2)}, u32[]{:S(2)}) collective-permute-start(bf16[2,128,128]{2,1,0:T(8,128)(2,1)S(1)} %finish.2.refs_0_.refs_2_), channel_id=1, source_target_pairs={{0,3},{1,2},{2,1},{3,0},{4,7},{5,6},{6,5},{7,4},{8,11},{9,10},{10,... | collective-permute-start | bytes 196616 | tf_op jit(solution)/shard_map/ppermute | solution.py:33
  53.4 8.3 %collective-permute-start.20 = (bf16[8,128,128]{2,1,0:T(8,128)(2,1)S(1)}, bf16[8,128,128]{2,1,0:T(8,128)(2,1)S(1)}, u32[]{:S(2)}, u32[]{:S(2)}) collective-permute-start(bf16[8,128,128]{2,1,0:T(8,128)(2,1)S(1)} %stack.3.own_ref), channel_id=1, source_target_pairs={{8,0},{16,8},{24,16},{9,1},{17,9},{25,17},{10,2},{18,10},{26,18},{... | collective-permute-start | bytes 786440 | tf_op jit(solution)/shard_map/ppermute | solution.py:90
  58.1 5.0 %collective-permute-start.17 = (bf16[2,128,128]{2,1,0:T(8,128)(2,1)S(1)}, bf16[2,128,128]{2,1,0:T(8,128)(2,1)S(1)}, u32[]{:S(2)}, u32[]{:S(2)}) collective-permute-start(bf16[2,128,128]{2,1,0:T(8,128)(2,1)S(1)} %get-tuple-element.67), channel_id=1, source_target_pairs={{0,1},{1,0},{2,3},{3,2},{4,5},{5,4},{6,7},{7,6},{8,9},{9,8},{10,11... | collective-permute-start | bytes 196616 | tf_op jit(solution)/shard_map/ppermute | solution.py:33
  59.4 4.8 %collective-permute-start.18 = (bf16[2,128,128]{2,1,0:T(8,128)(2,1)S(1)}, bf16[2,128,128]{2,1,0:T(8,128)(2,1)S(1)}, u32[]{:S(2)}, u32[]{:S(2)}) collective-permute-start(bf16[2,128,128]{2,1,0:T(8,128)(2,1)S(1)} %get-tuple-element.68), channel_id=1, source_target_pairs={{0,2},{1,3},{2,0},{3,1},{4,6},{5,7},{6,4},{7,5},{8,10},{9,11},{10,... | collective-permute-start | bytes 196616 | tf_op jit(solution)/shard_map/ppermute | solution.py:33
  60.6 5.5 %collective-permute-start.19 = (bf16[2,128,128]{2,1,0:T(8,128)(2,1)S(1)}, bf16[2,128,128]{2,1,0:T(8,128)(2,1)S(1)}, u32[]{:S(2)}, u32[]{:S(2)}) collective-permute-start(bf16[2,128,128]{2,1,0:T(8,128)(2,1)S(1)} %get-tuple-element.69), channel_id=1, source_target_pairs={{0,3},{1,2},{2,1},{3,0},{4,7},{5,6},{6,5},{7,4},{8,11},{9,10},{10,... | collective-permute-start | bytes 196616 | tf_op jit(solution)/shard_map/ppermute | solution.py:33
  66.1 5.2 %collective-permute-start.21 = (bf16[1,128,128]{2,1,0:T(8,128)(2,1)S(1)}, bf16[1,128,128]{2,1,0:T(8,128)(2,1)S(1)}, u32[]{:S(2)}, u32[]{:S(2)}) collective-permute-start(bf16[1,128,128]{2,1,0:T(8,128)(2,1)S(1)} %get-tuple-element.72), channel_id=1, source_target_pairs={{0,4},{1,5},{2,6},{3,7},{4,0},{5,1},{6,2},{7,3},{8,12},{9,13},{10,... | collective-permute-start | bytes 98312 | tf_op jit(solution)/shard_map/ppermute | solution.py:33

commit v4 on v2

--- a/solution.py
+++ b/solution.py
@@ -134,7 +134,7 @@
 
         wide[pl.ds(s * npno, npno), :] = narrow[s].astype(F32).T.astype(BF16)
 
-    def body(i, carry):
+    def body(i):
         fetch(i).wait()
         for k in range(step):
             left = jnp.dot(wide[...], held[i * step + k], preferred_element_type=F32).astype(BF16)
@@ -151,9 +151,9 @@
                     tail[place, :, pl.ds((k % 2) * npno, npno)] = block
             if s == CAP - 1:
                 put(i).start()
-        return carry
-
-    lax.fori_loop(0, aux // step, body, 0)
+
+    for i in range(aux // step):
+        body(i)
     for i in range(aux // step):
         put(i).wait()
 

time: 72.2 us -> 73.1 us (1.012)
  Pallas kernels: 16.8 us -> 17.8 us
    pallas_call x1, Pallas kernels: 6.28 us -> 7.19 us  [project(): pl.pallas_call(kernel, in_specs=[smem_spec()] + [vmem_spec()] * given + [...]
  transfers between devices with their start and end apart: 22 -> 22, of which waited for: 12 -> 12; matrix products, arithmetic and copies ran while one was open for 3% -> 3% of each run, Pallas kernels for 22% -> 23%
where the time goes in v4:
time: 73.1 us; the launch traced here: 73 us
  starting transfers between devices  30 us (41%)
  waiting for transfers between devices  20.9 us (29%)
  Pallas kernels  17.8 us (24%)
  local copies, waits for them, and re-layouts  1.84 us (3%)
  other arithmetic  1.61 us (2%)
  between operations  0.82 us (1%)
    ppermute x20, starting transfers between devices, exchange(): return lax.ppermute(value, axis, [(d, d ^ offset) for d in range(count)])  27.5 us
    ppermute x20, waiting for transfers between devices, exchange(): return lax.ppermute(value, axis, [(d, d ^ offset) for d in range(count)])  20.9 us
    pallas_call x1, Pallas kernels, project(): pl.pallas_call(kernel, in_specs=[smem_spec()] + [vmem_spec()] * given + [...  7.19 us
    pallas_call x2, Pallas kernels, ladder(): pl.pallas_call(kernel, in_specs=[smem_spec()] * 2 + [vmem_spec()] * (give...  6.76 us
    pallas_call x2, Pallas kernels, coupling(): pl.pallas_call(coupling_kernel, in_specs=[smem_spec()] + [pl.BlockSpec()]...  2.79 us
    ppermute x2, starting transfers between devices, from_next(): return lax.ppermute(value, axis, [(d, d - 1) for d in range(1, count)])  2.58 us
    unnamed x7, local copies, waits for them, and re-layouts  1.6 us
  transfers between devices with their start and end apart: 22, of which 12 were waited for; matrix products, arithmetic and copies ran while one was open for 3% of the time, Pallas kernels for 23%

profile of v4, /device:TPU:0, one launch (start us, length us, event | category | flops | bytes accessed | tf_op | source)
XLA Modules:
  0.0 73.0 jit_solution(12017115548708104203)
XLA Ops:
  1.3 4.0 %collective-permute-start = (f32[1,128]{1,0:T(1,128)S(1)}, f32[1,128]{1,0:T(1,128)S(1)}, u32[]{:S(2)}, u32[]{:S(2)}) collective-permute-start(f32[1,128]{1,0:T(1,128)S(1)} %broadcast_add_fusion.refs_6_.refs_3_), channel_id=1, source_target_pairs={{0,4},{1,5},{2,6},{3,7},{4,0},{5,1},{6,2},{7,3},{8,12},{9,13},{10,... | collective-permute-start | bytes 1544 | tf_op jit(solution)/shard_map/ppermute | solution.py:33
  7.2 3.0 %collective-permute-start.2 = (bf16[1,128,128]{2,1,0:T(8,128)(2,1)}, bf16[1,128,128]{2,1,0:T(8,128)(2,1)S(1)}, u32[]{:S(2)}, u32[]{:S(2)}) collective-permute-start(bf16[1,128,128]{2,1,0:T(8,128)(2,1)} %param.9), channel_id=1, source_target_pairs={{0,4},{1,5},{2,6},{3,7},{4,0},{5,1},{6,2},{7,3},{8,12},{9,13},{10,... | collective-permute-start | bytes 98312 | tf_op jit(solution)/shard_map/ppermute | solution.py:33
  10.2 2.3 %collective-permute-done.1.other_ref = bf16[1,256,128]{2,1,0:T(8,128)(2,1)S(1)} collective-permute-done((bf16[1,256,128]{2,1,0:T(8,128)(2,1)}, bf16[1,256,128]{2,1,0:T(8,128)(2,1)S(1)}, u32[]{:S(2)}, u32[]{:S(2)}) %collective-permute-start.1) | collective-permute-done | bytes 65568 | tf_op jit(solution)/shard_map/ppermute | solution.py:33
  12.4 1.7 %collective-permute-start.6 = (bf16[2,256,128]{2,1,0:T(8,128)(2,1)S(1)}, bf16[2,256,128]{2,1,0:T(8,128)(2,1)S(1)}, u32[]{:S(2)}, u32[]{:S(2)}) collective-permute-start(bf16[2,256,128]{2,1,0:T(8,128)(2,1)S(1)} %join.1.refs_1_), channel_id=1, source_target_pairs={{0,1},{1,0},{2,3},{3,2},{4,5},{5,4},{6,7},{7,6},{8,9},{9,8},{10,11... | collective-permute-start | bytes 393224 | tf_op jit(solution)/shard_map/ppermute | solution.py:33
  14.3 1.7 %collective-permute-start.8 = (bf16[2,256,128]{2,1,0:T(8,128)(2,1)S(1)}, bf16[2,256,128]{2,1,0:T(8,128)(2,1)S(1)}, u32[]{:S(2)}, u32[]{:S(2)}) collective-permute-start(bf16[2,256,128]{2,1,0:T(8,128)(2,1)S(1)} %join.1.refs_1_), channel_id=1, source_target_pairs={{0,3},{1,2},{2,1},{3,0},{4,7},{5,6},{6,5},{7,4},{8,11},{9,10},{10,... | collective-permute-start | bytes 393224 | tf_op jit(solution)/shard_map/ppermute | solution.py:33
  16.8 1.7 %collective-permute-start.3 = (bf16[2,128,128]{2,1,0:T(8,128)(2,1)S(1)}, bf16[2,128,128]{2,1,0:T(8,128)(2,1)S(1)}, u32[]{:S(2)}, u32[]{:S(2)}) collective-permute-start(bf16[2,128,128]{2,1,0:T(8,128)(2,1)S(1)} %constant_dynamic-update-slice_fusion.refs_0_.refs_2_), channel_id=1, source_target_pairs={{0,1},{1,0},{2,3},{3,2},{4,5},{5,4},{6,7},{7,6},{8,9},{9,8},{10,11... | collective-permute-start | bytes 196616 | tf_op jit(solution)/shard_map/ppermute | solution.py:33
  18.8 1.7 %collective-permute-start.5 = (bf16[2,128,128]{2,1,0:T(8,128)(2,1)S(1)}, bf16[2,128,128]{2,1,0:T(8,128)(2,1)S(1)}, u32[]{:S(2)}, u32[]{:S(2)}) collective-permute-start(bf16[2,128,128]{2,1,0:T(8,128)(2,1)S(1)} %constant_dynamic-update-slice_fusion.refs_0_.refs_2_), channel_id=1, source_target_pairs={{0,3},{1,2},{2,1},{3,0},{4,7},{5,6},{6,5},{7,4},{8,11},{9,10},{10,... | collective-permute-start | bytes 196616 | tf_op jit(solution)/shard_map/ppermute | solution.py:33
  21.1 7.2 %project.1 = (bf16[2,16,128,256]{3,2,1,0:T(8,128)(2,1)S(1)}, bf16[16,128,256]{2,1,0:T(8,128)(2,1)}) custom-call(s32[3]{0:T(128)S(1)} %get-tuple-element.74.refs_0_, bf16[2,256,128]{2,1,0:T(8,128)(2,1)S(1)} %join.1.refs_1_, bf16[2,256,128]{2,1,0:T(8,128)(2,1)S(1)} %collective-permute-done.6.refs_2_, bf16[2,256,128]{2,1,0:T(8,128)(2,1)S(1)} %collective-permute-done.7.refs_3_, ...), custom_call_target="tpu_custom_call" | custom-call | flops 2415919104 | bytes 4194304 | tf_op jit(solution)/shard_map/project/pallas_call | solution.py:170
  28.4 1.3 %collective-permute-start.12 = (bf16[8,128,128]{2,1,0:T(8,128)(2,1)S(1)}, bf16[8,128,128]{2,1,0:T(8,128)(2,1)S(1)}, u32[]{:S(2)}, u32[]{:S(2)}) collective-permute-start(bf16[8,128,128]{2,1,0:T(8,128)(2,1)S(1)} %stack.2.own_ref), channel_id=1, source_target_pairs={{8,0},{16,8},{24,16},{9,1},{17,9},{25,17},{10,2},{18,10},{26,18},{... | collective-permute-start | bytes 786440 | tf_op jit(solution)/shard_map/ppermute | solution.py:90
  29.7 3.4 %ladder.2 = (bf16[2,128,128]{2,1,0:T(8,128)(2,1)S(1)}, bf16[2,128,128]{2,1,0:T(8,128)(2,1)S(1)}, bf16[2,128,128]{2,1,0:T(8,128)(2,1)S(1)}, bf16[2,128,128]{2,1,0:T(8,128)(2,1)S(1)}) custom-call(s32[3]{0:T(128)S(1)} %get-tuple-element.74.refs_0_, s32[3]{0:T(128)S(1)} %get-tuple-element.73.refs_1_, ...), custom_call_target="tpu_custom_call" | custom-call | bytes 12582912 | tf_op jit(solution)/shard_map/ladder/pallas_call | solution.py:246
  33.1 1.7 %collective-permute-start.9 = (bf16[2,128,128]{2,1,0:T(8,128)(2,1)S(1)}, bf16[2,128,128]{2,1,0:T(8,128)(2,1)S(1)}, u32[]{:S(2)}, u32[]{:S(2)}) collective-permute-start(bf16[2,128,128]{2,1,0:T(8,128)(2,1)S(1)} %get-tuple-element.55), channel_id=1, source_target_pairs={{0,1},{1,0},{2,3},{3,2},{4,5},{5,4},{6,7},{7,6},{8,9},{9,8},{10,11... | collective-permute-start | bytes 196616 | tf_op jit(solution)/shard_map/ppermute | solution.py:33
  34.8 0.9 %collective-permute-start.10 = (bf16[2,128,128]{2,1,0:T(8,128)(2,1)S(1)}, bf16[2,128,128]{2,1,0:T(8,128)(2,1)S(1)}, u32[]{:S(2)}, u32[]{:S(2)}) collective-permute-start(bf16[2,128,128]{2,1,0:T(8,128)(2,1)S(1)} %get-tuple-element.56), channel_id=1, source_target_pairs={{0,2},{1,3},{2,0},{3,1},{4,6},{5,7},{6,4},{7,5},{8,10},{9,11},{10,... | collective-permute-start | bytes 196616 | tf_op jit(solution)/shard_map/ppermute | solution.py:33
  35.6 1.0 %collective-permute-start.11 = (bf16[2,128,128]{2,1,0:T(8,128)(2,1)S(1)}, bf16[2,128,128]{2,1,0:T(8,128)(2,1)S(1)}, u32[]{:S(2)}, u32[]{:S(2)}) collective-permute-start(bf16[2,128,128]{2,1,0:T(8,128)(2,1)S(1)} %get-tuple-element.57), channel_id=1, source_target_pairs={{0,3},{1,2},{2,1},{3,0},{4,7},{5,6},{6,5},{7,4},{8,11},{9,10},{10,... | collective-permute-start | bytes 196616 | tf_op jit(solution)/shard_map/ppermute | solution.py:33
  36.9 1.4 %coupling.2.refs_4_ = f32[128,128]{1,0:T(8,128)S(1)} custom-call(s32[1,4]{1,0:T(1,128)S(1)} %copy-done.1, bf16[8,128,128]{2,1,0:T(8,128)(2,1)S(1)} %stack.2.own_ref, bf16[8,128,128]{2,1,0:T(8,128)(2,1)S(1)} %collective-permute-done.12.next_ref, bf16[1,4,128,128]{3,2,1,0:T(8,128)(2,1)} %inter_ref.3, f32[1,128,128]{2,1,0:T(8,128)} %ints_ref.3), custom_call_target="tpu_custom_call" | custom-call | flops 33554432 | tf_op jit(solution)/shard_map/coupling/pallas_call | solution.py:285
  38.3 1.4 %collective-permute-done.10.refs_2_ = bf16[2,128,128]{2,1,0:T(8,128)(2,1)S(1)} collective-permute-done((bf16[2,128,128]{2,1,0:T(8,128)(2,1)S(1)}, bf16[2,128,128]{2,1,0:T(8,128)(2,1)S(1)}, u32[]{:S(2)}, u32[]{:S(2)}) %collective-permute-start.10) | collective-permute-done | bytes 65568 | tf_op jit(solution)/shard_map/ppermute | solution.py:33
  39.7 1.4 %collective-permute-done.11.refs_3_ = bf16[2,128,128]{2,1,0:T(8,128)(2,1)S(1)} collective-permute-done((bf16[2,128,128]{2,1,0:T(8,128)(2,1)S(1)}, bf16[2,128,128]{2,1,0:T(8,128)(2,1)S(1)}, u32[]{:S(2)}, u32[]{:S(2)}) %collective-permute-start.11) | collective-permute-done | bytes 65568 | tf_op jit(solution)/shard_map/ppermute | solution.py:33
  41.2 1.0 %collective-permute-start.13 = (bf16[2,128,128]{2,1,0:T(8,128)(2,1)S(1)}, bf16[2,128,128]{2,1,0:T(8,128)(2,1)S(1)}, u32[]{:S(2)}, u32[]{:S(2)}) collective-permute-start(bf16[2,128,128]{2,1,0:T(8,128)(2,1)S(1)} %get-tuple-element.61), channel_id=1, source_target_pairs={{0,4},{1,5},{2,6},{3,7},{4,0},{5,1},{6,2},{7,3},{8,12},{9,13},{10,... | collective-permute-start | bytes 196616 | tf_op jit(solution)/shard_map/ppermute | solution.py:33
  42.2 5.1 %collective-permute-done.13.refs_1_ = bf16[2,128,128]{2,1,0:T(8,128)(2,1)S(1)} collective-permute-done((bf16[2,128,128]{2,1,0:T(8,128)(2,1)S(1)}, bf16[2,128,128]{2,1,0:T(8,128)(2,1)S(1)}, u32[]{:S(2)}, u32[]{:S(2)}) %collective-permute-start.13) | collective-permute-done | bytes 65568 | tf_op jit(solution)/shard_map/ppermute | solution.py:33
  47.5 1.6 %collective-permute-start.14 = (bf16[2,128,128]{2,1,0:T(8,128)(2,1)S(1)}, bf16[2,128,128]{2,1,0:T(8,128)(2,1)S(1)}, u32[]{:S(2)}, u32[]{:S(2)}) collective-permute-start(bf16[2,128,128]{2,1,0:T(8,128)(2,1)S(1)} %finish.2.refs_0_.refs_2_), channel_id=1, source_target_pairs={{0,1},{1,0},{2,3},{3,2},{4,5},{5,4},{6,7},{7,6},{8,9},{9,8},{10,11... | collective-permute-start | bytes 196616 | tf_op jit(solution)/shard_map/ppermute | solution.py:33
  49.1 1.9 %collective-permute-start.16 = (bf16[2,128,128]{2,1,0:T(8,128)(2,1)S(1)}, bf16[2,128,128]{2,1,0:T(8,128)(2,1)S(1)}, u32[]{:S(2)}, u32[]{:S(2)}) collective-permute-start(bf16[2,128,128]{2,1,0:T(8,128)(2,1)S(1)} %finish.2.refs_0_.refs_2_), channel_id=1, source_target_pairs={{0,3},{1,2},{2,1},{3,0},{4,7},{5,6},{6,5},{7,4},{8,11},{9,10},{10,... | collective-permute-start | bytes 196616 | tf_op jit(solution)/shard_map/ppermute | solution.py:33
  51.8 1.6 %collective-permute-done.15.refs_2_.refs_4_ = bf16[2,128,128]{2,1,0:T(8,128)(2,1)S(1)} collective-permute-done((bf16[2,128,128]{2,1,0:T(8,128)(2,1)S(1)}, bf16[2,128,128]{2,1,0:T(8,128)(2,1)S(1)}, u32[]{:S(2)}, u32[]{:S(2)}) %collective-permute-start.15) | collective-permute-done | bytes 65568 | tf_op jit(solution)/shard_map/ppermute | solution.py:33
  53.4 0.9 %collective-permute-done.16.refs_3_.refs_5_ = bf16[2,128,128]{2,1,0:T(8,128)(2,1)S(1)} collective-permute-done((bf16[2,128,128]{2,1,0:T(8,128)(2,1)S(1)}, bf16[2,128,128]{2,1,0:T(8,128)(2,1)S(1)}, u32[]{:S(2)}, u32[]{:S(2)}) %collective-permute-start.16) | collective-permute-done | bytes 65568 | tf_op jit(solution)/shard_map/ppermute | solution.py:33
  54.3 1.3 %collective-permute-start.20 = (bf16[8,128,128]{2,1,0:T(8,128)(2,1)S(1)}, bf16[8,128,128]{2,1,0:T(8,128)(2,1)S(1)}, u32[]{:S(2)}, u32[]{:S(2)}) collective-permute-start(bf16[8,128,128]{2,1,0:T(8,128)(2,1)S(1)} %stack.3.own_ref), channel_id=1, source_target_pairs={{8,0},{16,8},{24,16},{9,1},{17,9},{25,17},{10,2},{18,10},{26,18},{... | collective-permute-start | bytes 786440 | tf_op jit(solution)/shard_map/ppermute | solution.py:90
  55.6 3.4 %ladder.3 = (bf16[2,128,128]{2,1,0:T(8,128)(2,1)S(1)}, bf16[2,128,128]{2,1,0:T(8,128)(2,1)S(1)}, bf16[2,128,128]{2,1,0:T(8,128)(2,1)S(1)}, bf16[2,128,128]{2,1,0:T(8,128)(2,1)S(1)}) custom-call(s32[3]{0:T(128)S(1)} %get-tuple-element.74.refs_0_, s32[3]{0:T(128)S(1)} %get-tuple-element.73.refs_1_, bf16[2,128,128]{2,1,0:T(8,128)(2,1)S(1)} %finish.2.refs_0_.refs_2_, ...), custom_call_target="tpu_custom_call" | custom-call | bytes 12582912 | tf_op jit(solution)/shard_map/ladder/pallas_call | solution.py:246
  59.0 1.3 %collective-permute-start.17 = (bf16[2,128,128]{2,1,0:T(8,128)(2,1)S(1)}, bf16[2,128,128]{2,1,0:T(8,128)(2,1)S(1)}, u32[]{:S(2)}, u32[]{:S(2)}) collective-permute-start(bf16[2,128,128]{2,1,0:T(8,128)(2,1)S(1)} %get-tuple-element.67), channel_id=1, source_target_pairs={{0,1},{1,0},{2,3},{3,2},{4,5},{5,4},{6,7},{7,6},{8,9},{9,8},{10,11... | collective-permute-start | bytes 196616 | tf_op jit(solution)/shard_map/ppermute | solution.py:33
  60.3 1.2 %collective-permute-start.18 = (bf16[2,128,128]{2,1,0:T(8,128)(2,1)S(1)}, bf16[2,128,128]{2,1,0:T(8,128)(2,1)S(1)}, u32[]{:S(2)}, u32[]{:S(2)}) collective-permute-start(bf16[2,128,128]{2,1,0:T(8,128)(2,1)S(1)} %get-tuple-element.68), channel_id=1, source_target_pairs={{0,2},{1,3},{2,0},{3,1},{4,6},{5,7},{6,4},{7,5},{8,10},{9,11},{10,... | collective-permute-start | bytes 196616 | tf_op jit(solution)/shard_map/ppermute | solution.py:33
  61.5 1.0 %collective-permute-start.19 = (bf16[2,128,128]{2,1,0:T(8,128)(2,1)S(1)}, bf16[2,128,128]{2,1,0:T(8,128)(2,1)S(1)}, u32[]{:S(2)}, u32[]{:S(2)}) collective-permute-start(bf16[2,128,128]{2,1,0:T(8,128)(2,1)S(1)} %get-tuple-element.69), channel_id=1, source_target_pairs={{0,3},{1,2},{2,1},{3,0},{4,7},{5,6},{6,5},{7,4},{8,11},{9,10},{10,... | collective-permute-start | bytes 196616 | tf_op jit(solution)/shard_map/ppermute | solution.py:33
  62.5 1.4 %coupling.3.refs_4_ = f32[128,128]{1,0:T(8,128)S(1)} custom-call(s32[1,4]{1,0:T(1,128)S(1)} %copy-done.1, bf16[8,128,128]{2,1,0:T(8,128)(2,1)S(1)} %stack.3.own_ref, bf16[8,128,128]{2,1,0:T(8,128)(2,1)S(1)} %collective-permute-done.20.next_ref, bf16[1,4,128,128]{3,2,1,0:T(8,128)(2,1)} %inter_ref.3, f32[1,128,128]{2,1,0:T(8,128)} %ints_ref.3), custom_call_target="tpu_custom_call" | custom-call | flops 33554432 | tf_op jit(solution)/shard_map/coupling/pallas_call | solution.py:285
  63.9 1.2 %collective-permute-done.18.refs_2_ = bf16[2,128,128]{2,1,0:T(8,128)(2,1)S(1)} collective-permute-done((bf16[2,128,128]{2,1,0:T(8,128)(2,1)S(1)}, bf16[2,128,128]{2,1,0:T(8,128)(2,1)S(1)}, u32[]{:S(2)}, u32[]{:S(2)}) %collective-permute-start.18) | collective-permute-done | bytes 65568 | tf_op jit(solution)/shard_map/ppermute | solution.py:33
  65.1 1.8 %collective-permute-done.19.refs_3_ = bf16[2,128,128]{2,1,0:T(8,128)(2,1)S(1)} collective-permute-done((bf16[2,128,128]{2,1,0:T(8,128)(2,1)S(1)}, bf16[2,128,128]{2,1,0:T(8,128)(2,1)S(1)}, u32[]{:S(2)}, u32[]{:S(2)}) %collective-permute-start.19) | collective-permute-done | bytes 65568 | tf_op jit(solution)/shard_map/ppermute | solution.py:33
  67.0 1.7 %collective-permute-start.21 = (bf16[1,128,128]{2,1,0:T(8,128)(2,1)S(1)}, bf16[1,128,128]{2,1,0:T(8,128)(2,1)S(1)}, u32[]{:S(2)}, u32[]{:S(2)}) collective-permute-start(bf16[1,128,128]{2,1,0:T(8,128)(2,1)S(1)} %get-tuple-element.72), channel_id=1, source_target_pairs={{0,4},{1,5},{2,6},{3,7},{4,0},{5,1},{6,2},{7,3},{8,12},{9,13},{10,... | collective-permute-start | bytes 98312 | tf_op jit(solution)/shard_map/ppermute | solution.py:33
  68.7 3.6 %collective-permute-done.21.refs_1_ = bf16[1,128,128]{2,1,0:T(8,128)(2,1)S(1)} collective-permute-done((bf16[1,128,128]{2,1,0:T(8,128)(2,1)S(1)}, bf16[1,128,128]{2,1,0:T(8,128)(2,1)S(1)}, u32[]{:S(2)}, u32[]{:S(2)}) %collective-permute-start.21) | collective-permute-done | bytes 32800 | tf_op jit(solution)/shard_map/ppermute | solution.py:33
  (42 shorter events, 6.4 us)
Async XLA Ops:
  1.3 5.9 %collective-permute-start = (f32[1,128]{1,0:T(1,128)S(1)}, f32[1,128]{1,0:T(1,128)S(1)}, u32[]{:S(2)}, u32[]{:S(2)}) collective-permute-start(f32[1,128]{1,0:T(1,128)S(1)} %broadcast_add_fusion.refs_6_.refs_3_), channel_id=1, source_target_pairs={{0,4},{1,5},{2,6},{3,7},{4,0},{5,1},{6,2},{7,3},{8,12},{9,13},{10,... | collective-permute-start | bytes 1544 | tf_op jit(solution)/shard_map/ppermute | solution.py:33
  5.3 7.1 %collective-permute-start.1 = (bf16[1,256,128]{2,1,0:T(8,128)(2,1)}, bf16[1,256,128]{2,1,0:T(8,128)(2,1)S(1)}, u32[]{:S(2)}, u32[]{:S(2)}) collective-permute-start(bf16[1,256,128]{2,1,0:T(8,128)(2,1)} %value_ref.1), channel_id=1, source_target_pairs={{0,4},{1,5},{2,6},{3,7},{4,0},{5,1},{6,2},{7,3},{8,12},{9,13},{10,... | collective-permute-start | bytes 196616 | tf_op jit(solution)/shard_map/ppermute | solution.py:33
  6.3 0.8 %copy-start = (bf16[1,256,128]{2,1,0:T(8,128)(2,1)S(1)}, bf16[1,256,128]{2,1,0:T(8,128)(2,1)}, u32[]{:S(2)}) copy-start(bf16[1,256,128]{2,1,0:T(8,128)(2,1)} %value_ref.1) | copy-start | bytes 196612
  7.2 9.6 %collective-permute-start.2 = (bf16[1,128,128]{2,1,0:T(8,128)(2,1)}, bf16[1,128,128]{2,1,0:T(8,128)(2,1)S(1)}, u32[]{:S(2)}, u32[]{:S(2)}) collective-permute-start(bf16[1,128,128]{2,1,0:T(8,128)(2,1)} %param.9), channel_id=1, source_target_pairs={{0,4},{1,5},{2,6},{3,7},{4,0},{5,1},{6,2},{7,3},{8,12},{9,13},{10,... | collective-permute-start | bytes 98312 | tf_op jit(solution)/shard_map/ppermute | solution.py:33
  12.4 6.3 %collective-permute-start.6 = (bf16[2,256,128]{2,1,0:T(8,128)(2,1)S(1)}, bf16[2,256,128]{2,1,0:T(8,128)(2,1)S(1)}, u32[]{:S(2)}, u32[]{:S(2)}) collective-permute-start(bf16[2,256,128]{2,1,0:T(8,128)(2,1)S(1)} %join.1.refs_1_), channel_id=1, source_target_pairs={{0,1},{1,0},{2,3},{3,2},{4,5},{5,4},{6,7},{7,6},{8,9},{9,8},{10,11... | collective-permute-start | bytes 393224 | tf_op jit(solution)/shard_map/ppermute | solution.py:33
  14.1 6.4 %collective-permute-start.7 = (bf16[2,256,128]{2,1,0:T(8,128)(2,1)S(1)}, bf16[2,256,128]{2,1,0:T(8,128)(2,1)S(1)}, u32[]{:S(2)}, u32[]{:S(2)}) collective-permute-start(bf16[2,256,128]{2,1,0:T(8,128)(2,1)S(1)} %join.1.refs_1_), channel_id=1, source_target_pairs={{0,2},{1,3},{2,0},{3,1},{4,6},{5,7},{6,4},{7,5},{8,10},{9,11},{10,... | collective-permute-start | bytes 393224 | tf_op jit(solution)/shard_map/ppermute | solution.py:33
  14.3 6.9 %collective-permute-start.8 = (bf16[2,256,128]{2,1,0:T(8,128)(2,1)S(1)}, bf16[2,256,128]{2,1,0:T(8,128)(2,1)S(1)}, u32[]{:S(2)}, u32[]{:S(2)}) collective-permute-start(bf16[2,256,128]{2,1,0:T(8,128)(2,1)S(1)} %join.1.refs_1_), channel_id=1, source_target_pairs={{0,3},{1,2},{2,1},{3,0},{4,7},{5,6},{6,5},{7,4},{8,11},{9,10},{10,... | collective-permute-start | bytes 393224 | tf_op jit(solution)/shard_map/ppermute | solution.py:33
  16.8 11.5 %collective-permute-start.3 = (bf16[2,128,128]{2,1,0:T(8,128)(2,1)S(1)}, bf16[2,128,128]{2,1,0:T(8,128)(2,1)S(1)}, u32[]{:S(2)}, u32[]{:S(2)}) collective-permute-start(bf16[2,128,128]{2,1,0:T(8,128)(2,1)S(1)} %constant_dynamic-update-slice_fusion.refs_0_.refs_2_), channel_id=1, source_target_pairs={{0,1},{1,0},{2,3},{3,2},{4,5},{5,4},{6,7},{7,6},{8,9},{9,8},{10,11... | collective-permute-start | bytes 196616 | tf_op jit(solution)/shard_map/ppermute | solution.py:33
  18.5 9.9 %collective-permute-start.4 = (bf16[2,128,128]{2,1,0:T(8,128)(2,1)S(1)}, bf16[2,128,128]{2,1,0:T(8,128)(2,1)S(1)}, u32[]{:S(2)}, u32[]{:S(2)}) collective-permute-start(bf16[2,128,128]{2,1,0:T(8,128)(2,1)S(1)} %constant_dynamic-update-slice_fusion.refs_0_.refs_2_), channel_id=1, source_target_pairs={{0,2},{1,3},{2,0},{3,1},{4,6},{5,7},{6,4},{7,5},{8,10},{9,11},{10,... | collective-permute-start | bytes 196616 | tf_op jit(solution)/shard_map/ppermute | solution.py:33
  18.8 9.6 %collective-permute-start.5 = (bf16[2,128,128]{2,1,0:T(8,128)(2,1)S(1)}, bf16[2,128,128]{2,1,0:T(8,128)(2,1)S(1)}, u32[]{:S(2)}, u32[]{:S(2)}) collective-permute-start(bf16[2,128,128]{2,1,0:T(8,128)(2,1)S(1)} %constant_dynamic-update-slice_fusion.refs_0_.refs_2_), channel_id=1, source_target_pairs={{0,3},{1,2},{2,1},{3,0},{4,7},{5,6},{6,5},{7,4},{8,11},{9,10},{10,... | collective-permute-start | bytes 196616 | tf_op jit(solution)/shard_map/ppermute | solution.py:33
  21.1 15.5 %copy-start.2 = (f32[1,128]{1,0:T(1,128)S(1)}, f32[1,128]{1,0:T(1,128)}, u32[]{:S(2)}) copy-start(f32[1,128]{1,0:T(1,128)} %param.14) | copy-start | bytes 1540
  21.1 15.7 %copy-start.1 = (s32[1,4]{1,0:T(1,128)S(1)}, s32[1,4]{1,0:T(1,128)}, u32[]{:S(2)}) copy-start(s32[1,4]{1,0:T(1,128)} %near.3) | copy-start | bytes 52
  28.4 8.5 %collective-permute-start.12 = (bf16[8,128,128]{2,1,0:T(8,128)(2,1)S(1)}, bf16[8,128,128]{2,1,0:T(8,128)(2,1)S(1)}, u32[]{:S(2)}, u32[]{:S(2)}) collective-permute-start(bf16[8,128,128]{2,1,0:T(8,128)(2,1)S(1)} %stack.2.own_ref), channel_id=1, source_target_pairs={{8,0},{16,8},{24,16},{9,1},{17,9},{25,17},{10,2},{18,10},{26,18},{... | collective-permute-start | bytes 786440 | tf_op jit(solution)/shard_map/ppermute | solution.py:90
  33.1 5.2 %collective-permute-start.9 = (bf16[2,128,128]{2,1,0:T(8,128)(2,1)S(1)}, bf16[2,128,128]{2,1,0:T(8,128)(2,1)S(1)}, u32[]{:S(2)}, u32[]{:S(2)}) collective-permute-start(bf16[2,128,128]{2,1,0:T(8,128)(2,1)S(1)} %get-tuple-element.55), channel_id=1, source_target_pairs={{0,1},{1,0},{2,3},{3,2},{4,5},{5,4},{6,7},{7,6},{8,9},{9,8},{10,11... | collective-permute-start | bytes 196616 | tf_op jit(solution)/shard_map/ppermute | solution.py:33
  34.8 5.0 %collective-permute-start.10 = (bf16[2,128,128]{2,1,0:T(8,128)(2,1)S(1)}, bf16[2,128,128]{2,1,0:T(8,128)(2,1)S(1)}, u32[]{:S(2)}, u32[]{:S(2)}) collective-permute-start(bf16[2,128,128]{2,1,0:T(8,128)(2,1)S(1)} %get-tuple-element.56), channel_id=1, source_target_pairs={{0,2},{1,3},{2,0},{3,1},{4,6},{5,7},{6,4},{7,5},{8,10},{9,11},{10,... | collective-permute-start | bytes 196616 | tf_op jit(solution)/shard_map/ppermute | solution.py:33
  35.6 5.5 %collective-permute-start.11 = (bf16[2,128,128]{2,1,0:T(8,128)(2,1)S(1)}, bf16[2,128,128]{2,1,0:T(8,128)(2,1)S(1)}, u32[]{:S(2)}, u32[]{:S(2)}) collective-permute-start(bf16[2,128,128]{2,1,0:T(8,128)(2,1)S(1)} %get-tuple-element.57), channel_id=1, source_target_pairs={{0,3},{1,2},{2,1},{3,0},{4,7},{5,6},{6,5},{7,4},{8,11},{9,10},{10,... | collective-permute-start | bytes 196616 | tf_op jit(solution)/shard_map/ppermute | solution.py:33
  41.2 6.2 %collective-permute-start.13 = (bf16[2,128,128]{2,1,0:T(8,128)(2,1)S(1)}, bf16[2,128,128]{2,1,0:T(8,128)(2,1)S(1)}, u32[]{:S(2)}, u32[]{:S(2)}) collective-permute-start(bf16[2,128,128]{2,1,0:T(8,128)(2,1)S(1)} %get-tuple-element.61), channel_id=1, source_target_pairs={{0,4},{1,5},{2,6},{3,7},{4,0},{5,1},{6,2},{7,3},{8,12},{9,13},{10,... | collective-permute-start | bytes 196616 | tf_op jit(solution)/shard_map/ppermute | solution.py:33
  47.5 4.3 %collective-permute-start.14 = (bf16[2,128,128]{2,1,0:T(8,128)(2,1)S(1)}, bf16[2,128,128]{2,1,0:T(8,128)(2,1)S(1)}, u32[]{:S(2)}, u32[]{:S(2)}) collective-permute-start(bf16[2,128,128]{2,1,0:T(8,128)(2,1)S(1)} %finish.2.refs_0_.refs_2_), channel_id=1, source_target_pairs={{0,1},{1,0},{2,3},{3,2},{4,5},{5,4},{6,7},{7,6},{8,9},{9,8},{10,11... | collective-permute-start | bytes 196616 | tf_op jit(solution)/shard_map/ppermute | solution.py:33
  49.1 4.3 %collective-permute-start.15 = (bf16[2,128,128]{2,1,0:T(8,128)(2,1)S(1)}, bf16[2,128,128]{2,1,0:T(8,128)(2,1)S(1)}, u32[]{:S(2)}, u32[]{:S(2)}) collective-permute-start(bf16[2,128,128]{2,1,0:T(8,128)(2,1)S(1)} %finish.2.refs_0_.refs_2_), channel_id=1, source_target_pairs={{0,2},{1,3},{2,0},{3,1},{4,6},{5,7},{6,4},{7,5},{8,10},{9,11},{10,... | collective-permute-start | bytes 196616 | tf_op jit(solution)/shard_map/ppermute | solution.py:33
  49.1 5.2 %collective-permute-start.16 = (bf16[2,128,128]{2,1,0:T(8,128)(2,1)S(1)}, bf16[2,128,128]{2,1,0:T(8,128)(2,1)S(1)}, u32[]{:S(2)}, u32[]{:S(2)}) collective-permute-start(bf16[2,128,128]{2,1,0:T(8,128)(2,1)S(1)} %finish.2.refs_0_.refs_2_), channel_id=1, source_target_pairs={{0,3},{1,2},{2,1},{3,0},{4,7},{5,6},{6,5},{7,4},{8,11},{9,10},{10,... | collective-permute-start | bytes 196616 | tf_op jit(solution)/shard_map/ppermute | solution.py:33
  54.3 8.2 %collective-permute-start.20 = (bf16[8,128,128]{2,1,0:T(8,128)(2,1)S(1)}, bf16[8,128,128]{2,1,0:T(8,128)(2,1)S(1)}, u32[]{:S(2)}, u32[]{:S(2)}) collective-permute-start(bf16[8,128,128]{2,1,0:T(8,128)(2,1)S(1)} %stack.3.own_ref), channel_id=1, source_target_pairs={{8,0},{16,8},{24,16},{9,1},{17,9},{25,17},{10,2},{18,10},{26,18},{... | collective-permute-start | bytes 786440 | tf_op jit(solution)/shard_map/ppermute | solution.py:90
  59.0 5.0 %collective-permute-start.17 = (bf16[2,128,128]{2,1,0:T(8,128)(2,1)S(1)}, bf16[2,128,128]{2,1,0:T(8,128)(2,1)S(1)}, u32[]{:S(2)}, u32[]{:S(2)}) collective-permute-start(bf16[2,128,128]{2,1,0:T(8,128)(2,1)S(1)} %get-tuple-element.67), channel_id=1, source_target_pairs={{0,1},{1,0},{2,3},{3,2},{4,5},{5,4},{6,7},{7,6},{8,9},{9,8},{10,11... | collective-permute-start | bytes 196616 | tf_op jit(solution)/shard_map/ppermute | solution.py:33
  60.3 4.8 %collective-permute-start.18 = (bf16[2,128,128]{2,1,0:T(8,128)(2,1)S(1)}, bf16[2,128,128]{2,1,0:T(8,128)(2,1)S(1)}, u32[]{:S(2)}, u32[]{:S(2)}) collective-permute-start(bf16[2,128,128]{2,1,0:T(8,128)(2,1)S(1)} %get-tuple-element.68), channel_id=1, source_target_pairs={{0,2},{1,3},{2,0},{3,1},{4,6},{5,7},{6,4},{7,5},{8,10},{9,11},{10,... | collective-permute-start | bytes 196616 | tf_op jit(solution)/shard_map/ppermute | solution.py:33
  61.5 5.5 %collective-permute-start.19 = (bf16[2,128,128]{2,1,0:T(8,128)(2,1)S(1)}, bf16[2,128,128]{2,1,0:T(8,128)(2,1)S(1)}, u32[]{:S(2)}, u32[]{:S(2)}) collective-permute-start(bf16[2,128,128]{2,1,0:T(8,128)(2,1)S(1)} %get-tuple-element.69), channel_id=1, source_target_pairs={{0,3},{1,2},{2,1},{3,0},{4,7},{5,6},{6,5},{7,4},{8,11},{9,10},{10,... | collective-permute-start | bytes 196616 | tf_op jit(solution)/shard_map/ppermute | solution.py:33
  67.0 5.2 %collective-permute-start.21 = (bf16[1,128,128]{2,1,0:T(8,128)(2,1)S(1)}, bf16[1,128,128]{2,1,0:T(8,128)(2,1)S(1)}, u32[]{:S(2)}, u32[]{:S(2)}) collective-permute-start(bf16[1,128,128]{2,1,0:T(8,128)(2,1)S(1)} %get-tuple-element.72), channel_id=1, source_target_pairs={{0,4},{1,5},{2,6},{3,7},{4,0},{5,1},{6,2},{7,3},{8,12},{9,13},{10,... | collective-permute-start | bytes 98312 | tf_op jit(solution)/shard_map/ppermute | solution.py:33

commit v5 on v3

--- a/solution.py
+++ b/solution.py
@@ -158,7 +158,7 @@
         put(i).wait()
 
 
-def project(slots, group_bases, factor_block, step=8):
+def project(slots, group_bases, factor_block, step=4):
     aux, width, _ = factor_block.shape
     given = len(group_bases)
     npno = group_bases[0].shape[2]
@@ -217,19 +217,21 @@
             source = tail
         else:
             source = proj_ref.at[s]
-        total = jnp.zeros((npno, npno), F32)
         chunk = min(4, half)
-        for c in range(0, half, chunk):
-            part = pl.ds(c * npno, chunk * npno)
-            flat = source[pl.ds(c, chunk)].reshape(chunk * npno, 2 * npno)
-            mixed[part, :] = jnp.dot(flat, twice[...], preferred_element_type=F32).astype(BF16)
-            for m in range(c, c + chunk):
+
+        def body(c, total):
+            flat = source[pl.ds(c * chunk, chunk)].reshape(chunk * npno, 2 * npno)
+            mixed[...] = jnp.dot(flat, twice[...], preferred_element_type=F32).astype(BF16)
+            for m in range(chunk):
                 total = total + lax.dot_general(
                     mixed[pl.ds(m * npno, npno), :],
-                    source[m],
+                    source[c * chunk + m],
                     CONTRACT_LAST,
                     preferred_element_type=F32,
                 )
+            return total
+
+        total = lax.fori_loop(0, half // chunk, body, jnp.zeros((npno, npno), F32))
         narrow = total.astype(BF16)
         for j in range(given):
 
@@ -255,7 +257,7 @@
         out_shape=[pltpu.VMEM((2, npno, npno), BF16)] * given,
         scratch_shapes=[
             pltpu.VMEM((2 * npno, 2 * npno), BF16),
-            pltpu.VMEM((half * npno, 2 * npno), BF16),
+            pltpu.VMEM((min(4, half) * npno, 2 * npno), BF16),
             pltpu.VMEM(tail.shape, BF16),
             pltpu.SemaphoreType.DMA,
         ],

time: 72.4 us -> 78.5 us (1.084)
  Pallas kernels: 16.9 us -> 23.2 us
    pallas_call x2, Pallas kernels: 6.78 us -> 11.5 us  [ladder(): pl.pallas_call(kernel, in_specs=[smem_spec()] * 2 + [vmem_spec()] * (give...]
    pallas_call x1, Pallas kernels: 6.28 us -> 7.9 us  [project(): pl.pallas_call(kernel, in_specs=[smem_spec()] + [vmem_spec()] * given + [...]
  transfers between devices with their start and end apart: 22 -> 22, of which waited for: 12 -> 12; matrix products, arithmetic and copies ran while one was open for 3% -> 2% of each run, Pallas kernels for 22% -> 28%
where the time goes in v5:
time: 78.5 us; the launch traced here: 78.4 us
  starting transfers between devices  30 us (38%)
  Pallas kernels  23.2 us (30%)
  waiting for transfers between devices  20.9 us (27%)
  local copies, waits for them, and re-layouts  1.84 us (2%)
  other arithmetic  1.61 us (2%)
  between operations  0.82 us (1%)
    ppermute x20, starting transfers between devices, exchange(): return lax.ppermute(value, axis, [(d, d ^ offset) for d in range(count)])  27.4 us
    ppermute x20, waiting for transfers between devices, exchange(): return lax.ppermute(value, axis, [(d, d ^ offset) for d in range(count)])  20.9 us
    pallas_call x2, Pallas kernels, ladder(): pl.pallas_call(kernel, in_specs=[smem_spec()] * 2 + [vmem_spec()] * (give...  11.5 us
    pallas_call x1, Pallas kernels, project(): pl.pallas_call(kernel, in_specs=[smem_spec()] + [vmem_spec()] * given + [...  7.9 us
    pallas_call x2, Pallas kernels, coupling(): pl.pallas_call(coupling_kernel, in_specs=[smem_spec()] + [pl.BlockSpec()]...  2.79 us
    ppermute x2, starting transfers between devices, from_next(): return lax.ppermute(value, axis, [(d, d - 1) for d in range(1, count)])  2.58 us
    unnamed x7, local copies, waits for them, and re-layouts  1.6 us
  transfers between devices with their start and end apart: 22, of which 12 were waited for; matrix products, arithmetic and copies ran while one was open for 2% of the time, Pallas kernels for 28%

profile of v5, /device:TPU:0, one launch (start us, length us, event | category | flops | bytes accessed | tf_op | source)
XLA Modules:
  0.0 78.4 jit_solution(8622149094503940410)
XLA Ops:
  1.3 4.0 %collective-permute-start = (f32[1,128]{1,0:T(1,128)S(1)}, f32[1,128]{1,0:T(1,128)S(1)}, u32[]{:S(2)}, u32[]{:S(2)}) collective-permute-start(f32[1,128]{1,0:T(1,128)S(1)} %broadcast_add_fusion.refs_6_.refs_3_), channel_id=1, source_target_pairs={{0,4},{1,5},{2,6},{3,7},{4,0},{5,1},{6,2},{7,3},{8,12},{9,13},{10,... | collective-permute-start | bytes 1544 | tf_op jit(solution)/shard_map/ppermute | solution.py:33
  7.2 3.0 %collective-permute-start.2 = (bf16[1,128,128]{2,1,0:T(8,128)(2,1)}, bf16[1,128,128]{2,1,0:T(8,128)(2,1)S(1)}, u32[]{:S(2)}, u32[]{:S(2)}) collective-permute-start(bf16[1,128,128]{2,1,0:T(8,128)(2,1)} %param.9), channel_id=1, source_target_pairs={{0,4},{1,5},{2,6},{3,7},{4,0},{5,1},{6,2},{7,3},{8,12},{9,13},{10,... | collective-permute-start | bytes 98312 | tf_op jit(solution)/shard_map/ppermute | solution.py:33
  10.2 2.3 %collective-permute-done.1.other_ref = bf16[1,256,128]{2,1,0:T(8,128)(2,1)S(1)} collective-permute-done((bf16[1,256,128]{2,1,0:T(8,128)(2,1)}, bf16[1,256,128]{2,1,0:T(8,128)(2,1)S(1)}, u32[]{:S(2)}, u32[]{:S(2)}) %collective-permute-start.1) | collective-permute-done | bytes 65568 | tf_op jit(solution)/shard_map/ppermute | solution.py:33
  12.4 1.7 %collective-permute-start.6 = (bf16[2,256,128]{2,1,0:T(8,128)(2,1)S(1)}, bf16[2,256,128]{2,1,0:T(8,128)(2,1)S(1)}, u32[]{:S(2)}, u32[]{:S(2)}) collective-permute-start(bf16[2,256,128]{2,1,0:T(8,128)(2,1)S(1)} %join.1.refs_1_), channel_id=1, source_target_pairs={{0,1},{1,0},{2,3},{3,2},{4,5},{5,4},{6,7},{7,6},{8,9},{9,8},{10,11... | collective-permute-start | bytes 393224 | tf_op jit(solution)/shard_map/ppermute | solution.py:33
  14.3 1.7 %collective-permute-start.8 = (bf16[2,256,128]{2,1,0:T(8,128)(2,1)S(1)}, bf16[2,256,128]{2,1,0:T(8,128)(2,1)S(1)}, u32[]{:S(2)}, u32[]{:S(2)}) collective-permute-start(bf16[2,256,128]{2,1,0:T(8,128)(2,1)S(1)} %join.1.refs_1_), channel_id=1, source_target_pairs={{0,3},{1,2},{2,1},{3,0},{4,7},{5,6},{6,5},{7,4},{8,11},{9,10},{10,... | collective-permute-start | bytes 393224 | tf_op jit(solution)/shard_map/ppermute | solution.py:33
  16.8 1.7 %collective-permute-start.3 = (bf16[2,128,128]{2,1,0:T(8,128)(2,1)S(1)}, bf16[2,128,128]{2,1,0:T(8,128)(2,1)S(1)}, u32[]{:S(2)}, u32[]{:S(2)}) collective-permute-start(bf16[2,128,128]{2,1,0:T(8,128)(2,1)S(1)} %constant_dynamic-update-slice_fusion.refs_0_.refs_2_), channel_id=1, source_target_pairs={{0,1},{1,0},{2,3},{3,2},{4,5},{5,4},{6,7},{7,6},{8,9},{9,8},{10,11... | collective-permute-start | bytes 196616 | tf_op jit(solution)/shard_map/ppermute | solution.py:33
  18.8 1.7 %collective-permute-start.5 = (bf16[2,128,128]{2,1,0:T(8,128)(2,1)S(1)}, bf16[2,128,128]{2,1,0:T(8,128)(2,1)S(1)}, u32[]{:S(2)}, u32[]{:S(2)}) collective-permute-start(bf16[2,128,128]{2,1,0:T(8,128)(2,1)S(1)} %constant_dynamic-update-slice_fusion.refs_0_.refs_2_), channel_id=1, source_target_pairs={{0,3},{1,2},{2,1},{3,0},{4,7},{5,6},{6,5},{7,4},{8,11},{9,10},{10,... | collective-permute-start | bytes 196616 | tf_op jit(solution)/shard_map/ppermute | solution.py:33
  21.1 7.9 %project.1 = (bf16[2,16,128,256]{3,2,1,0:T(8,128)(2,1)S(1)}, bf16[16,128,256]{2,1,0:T(8,128)(2,1)}) custom-call(s32[3]{0:T(128)S(1)} %get-tuple-element.74.refs_0_, bf16[2,256,128]{2,1,0:T(8,128)(2,1)S(1)} %join.1.refs_1_, bf16[2,256,128]{2,1,0:T(8,128)(2,1)S(1)} %collective-permute-done.6.refs_2_, bf16[2,256,128]{2,1,0:T(8,128)(2,1)S(1)} %collective-permute-done.7.refs_3_, ...), custom_call_target="tpu_custom_call" | custom-call | flops 2415919104 | bytes 4194304 | tf_op jit(solution)/shard_map/project/pallas_call | solution.py:170
  29.1 1.3 %collective-permute-start.12 = (bf16[8,128,128]{2,1,0:T(8,128)(2,1)S(1)}, bf16[8,128,128]{2,1,0:T(8,128)(2,1)S(1)}, u32[]{:S(2)}, u32[]{:S(2)}) collective-permute-start(bf16[8,128,128]{2,1,0:T(8,128)(2,1)S(1)} %stack.2.own_ref), channel_id=1, source_target_pairs={{8,0},{16,8},{24,16},{9,1},{17,9},{25,17},{10,2},{18,10},{26,18},{... | collective-permute-start | bytes 786440 | tf_op jit(solution)/shard_map/ppermute | solution.py:90
  30.4 5.7 %ladder.2 = (bf16[2,128,128]{2,1,0:T(8,128)(2,1)S(1)}, bf16[2,128,128]{2,1,0:T(8,128)(2,1)S(1)}, bf16[2,128,128]{2,1,0:T(8,128)(2,1)S(1)}, bf16[2,128,128]{2,1,0:T(8,128)(2,1)S(1)}) custom-call(s32[3]{0:T(128)S(1)} %get-tuple-element.74.refs_0_, s32[3]{0:T(128)S(1)} %get-tuple-element.73.refs_1_, ...), custom_call_target="tpu_custom_call" | custom-call | bytes 12582912 | tf_op jit(solution)/shard_map/ladder/pallas_call | solution.py:251
  36.1 1.7 %collective-permute-start.9 = (bf16[2,128,128]{2,1,0:T(8,128)(2,1)S(1)}, bf16[2,128,128]{2,1,0:T(8,128)(2,1)S(1)}, u32[]{:S(2)}, u32[]{:S(2)}) collective-permute-start(bf16[2,128,128]{2,1,0:T(8,128)(2,1)S(1)} %get-tuple-element.55), channel_id=1, source_target_pairs={{0,1},{1,0},{2,3},{3,2},{4,5},{5,4},{6,7},{7,6},{8,9},{9,8},{10,11... | collective-permute-start | bytes 196616 | tf_op jit(solution)/shard_map/ppermute | solution.py:33
  37.8 0.9 %collective-permute-start.10 = (bf16[2,128,128]{2,1,0:T(8,128)(2,1)S(1)}, bf16[2,128,128]{2,1,0:T(8,128)(2,1)S(1)}, u32[]{:S(2)}, u32[]{:S(2)}) collective-permute-start(bf16[2,128,128]{2,1,0:T(8,128)(2,1)S(1)} %get-tuple-element.56), channel_id=1, source_target_pairs={{0,2},{1,3},{2,0},{3,1},{4,6},{5,7},{6,4},{7,5},{8,10},{9,11},{10,... | collective-permute-start | bytes 196616 | tf_op jit(solution)/shard_map/ppermute | solution.py:33
  38.7 1.0 %collective-permute-start.11 = (bf16[2,128,128]{2,1,0:T(8,128)(2,1)S(1)}, bf16[2,128,128]{2,1,0:T(8,128)(2,1)S(1)}, u32[]{:S(2)}, u32[]{:S(2)}) collective-permute-start(bf16[2,128,128]{2,1,0:T(8,128)(2,1)S(1)} %get-tuple-element.57), channel_id=1, source_target_pairs={{0,3},{1,2},{2,1},{3,0},{4,7},{5,6},{6,5},{7,4},{8,11},{9,10},{10,... | collective-permute-start | bytes 196616 | tf_op jit(solution)/shard_map/ppermute | solution.py:33
  39.9 1.4 %coupling.2.refs_4_ = f32[128,128]{1,0:T(8,128)S(1)} custom-call(s32[1,4]{1,0:T(1,128)S(1)} %copy-done.1, bf16[8,128,128]{2,1,0:T(8,128)(2,1)S(1)} %stack.2.own_ref, bf16[8,128,128]{2,1,0:T(8,128)(2,1)S(1)} %collective-permute-done.12.next_ref, bf16[1,4,128,128]{3,2,1,0:T(8,128)(2,1)} %inter_ref.3, f32[1,128,128]{2,1,0:T(8,128)} %ints_ref.3), custom_call_target="tpu_custom_call" | custom-call | flops 33554432 | tf_op jit(solution)/shard_map/coupling/pallas_call | solution.py:290
  41.3 1.4 %collective-permute-done.10.refs_2_ = bf16[2,128,128]{2,1,0:T(8,128)(2,1)S(1)} collective-permute-done((bf16[2,128,128]{2,1,0:T(8,128)(2,1)S(1)}, bf16[2,128,128]{2,1,0:T(8,128)(2,1)S(1)}, u32[]{:S(2)}, u32[]{:S(2)}) %collective-permute-start.10) | collective-permute-done | bytes 65568 | tf_op jit(solution)/shard_map/ppermute | solution.py:33
  42.8 1.4 %collective-permute-done.11.refs_3_ = bf16[2,128,128]{2,1,0:T(8,128)(2,1)S(1)} collective-permute-done((bf16[2,128,128]{2,1,0:T(8,128)(2,1)S(1)}, bf16[2,128,128]{2,1,0:T(8,128)(2,1)S(1)}, u32[]{:S(2)}, u32[]{:S(2)}) %collective-permute-start.11) | collective-permute-done | bytes 65568 | tf_op jit(solution)/shard_map/ppermute | solution.py:33
  44.3 1.0 %collective-permute-start.13 = (bf16[2,128,128]{2,1,0:T(8,128)(2,1)S(1)}, bf16[2,128,128]{2,1,0:T(8,128)(2,1)S(1)}, u32[]{:S(2)}, u32[]{:S(2)}) collective-permute-start(bf16[2,128,128]{2,1,0:T(8,128)(2,1)S(1)} %get-tuple-element.61), channel_id=1, source_target_pairs={{0,4},{1,5},{2,6},{3,7},{4,0},{5,1},{6,2},{7,3},{8,12},{9,13},{10,... | collective-permute-start | bytes 196616 | tf_op jit(solution)/shard_map/ppermute | solution.py:33
  45.3 5.1 %collective-permute-done.13.refs_1_ = bf16[2,128,128]{2,1,0:T(8,128)(2,1)S(1)} collective-permute-done((bf16[2,128,128]{2,1,0:T(8,128)(2,1)S(1)}, bf16[2,128,128]{2,1,0:T(8,128)(2,1)S(1)}, u32[]{:S(2)}, u32[]{:S(2)}) %collective-permute-start.13) | collective-permute-done | bytes 65568 | tf_op jit(solution)/shard_map/ppermute | solution.py:33
  50.5 1.6 %collective-permute-start.14 = (bf16[2,128,128]{2,1,0:T(8,128)(2,1)S(1)}, bf16[2,128,128]{2,1,0:T(8,128)(2,1)S(1)}, u32[]{:S(2)}, u32[]{:S(2)}) collective-permute-start(bf16[2,128,128]{2,1,0:T(8,128)(2,1)S(1)} %finish.2.refs_0_.refs_2_), channel_id=1, source_target_pairs={{0,1},{1,0},{2,3},{3,2},{4,5},{5,4},{6,7},{7,6},{8,9},{9,8},{10,11... | collective-permute-start | bytes 196616 | tf_op jit(solution)/shard_map/ppermute | solution.py:33
  52.2 1.9 %collective-permute-start.16 = (bf16[2,128,128]{2,1,0:T(8,128)(2,1)S(1)}, bf16[2,128,128]{2,1,0:T(8,128)(2,1)S(1)}, u32[]{:S(2)}, u32[]{:S(2)}) collective-permute-start(bf16[2,128,128]{2,1,0:T(8,128)(2,1)S(1)} %finish.2.refs_0_.refs_2_), channel_id=1, source_target_pairs={{0,3},{1,2},{2,1},{3,0},{4,7},{5,6},{6,5},{7,4},{8,11},{9,10},{10,... | collective-permute-start | bytes 196616 | tf_op jit(solution)/shard_map/ppermute | solution.py:33
  54.8 1.6 %collective-permute-done.15.refs_2_.refs_4_ = bf16[2,128,128]{2,1,0:T(8,128)(2,1)S(1)} collective-permute-done((bf16[2,128,128]{2,1,0:T(8,128)(2,1)S(1)}, bf16[2,128,128]{2,1,0:T(8,128)(2,1)S(1)}, u32[]{:S(2)}, u32[]{:S(2)}) %collective-permute-start.15) | collective-permute-done | bytes 65568 | tf_op jit(solution)/shard_map/ppermute | solution.py:33
  56.4 0.9 %collective-permute-done.16.refs_3_.refs_5_ = bf16[2,128,128]{2,1,0:T(8,128)(2,1)S(1)} collective-permute-done((bf16[2,128,128]{2,1,0:T(8,128)(2,1)S(1)}, bf16[2,128,128]{2,1,0:T(8,128)(2,1)S(1)}, u32[]{:S(2)}, u32[]{:S(2)}) %collective-permute-start.16) | collective-permute-done | bytes 65568 | tf_op jit(solution)/shard_map/ppermute | solution.py:33
  57.3 1.3 %collective-permute-start.20 = (bf16[8,128,128]{2,1,0:T(8,128)(2,1)S(1)}, bf16[8,128,128]{2,1,0:T(8,128)(2,1)S(1)}, u32[]{:S(2)}, u32[]{:S(2)}) collective-permute-start(bf16[8,128,128]{2,1,0:T(8,128)(2,1)S(1)} %stack.3.own_ref), channel_id=1, source_target_pairs={{8,0},{16,8},{24,16},{9,1},{17,9},{25,17},{10,2},{18,10},{26,18},{... | collective-permute-start | bytes 786440 | tf_op jit(solution)/shard_map/ppermute | solution.py:90
  58.6 5.7 %ladder.3 = (bf16[2,128,128]{2,1,0:T(8,128)(2,1)S(1)}, bf16[2,128,128]{2,1,0:T(8,128)(2,1)S(1)}, bf16[2,128,128]{2,1,0:T(8,128)(2,1)S(1)}, bf16[2,128,128]{2,1,0:T(8,128)(2,1)S(1)}) custom-call(s32[3]{0:T(128)S(1)} %get-tuple-element.74.refs_0_, s32[3]{0:T(128)S(1)} %get-tuple-element.73.refs_1_, bf16[2,128,128]{2,1,0:T(8,128)(2,1)S(1)} %finish.2.refs_0_.refs_2_, ...), custom_call_target="tpu_custom_call" | custom-call | bytes 12582912 | tf_op jit(solution)/shard_map/ladder/pallas_call | solution.py:251
  64.4 1.3 %collective-permute-start.17 = (bf16[2,128,128]{2,1,0:T(8,128)(2,1)S(1)}, bf16[2,128,128]{2,1,0:T(8,128)(2,1)S(1)}, u32[]{:S(2)}, u32[]{:S(2)}) collective-permute-start(bf16[2,128,128]{2,1,0:T(8,128)(2,1)S(1)} %get-tuple-element.67), channel_id=1, source_target_pairs={{0,1},{1,0},{2,3},{3,2},{4,5},{5,4},{6,7},{7,6},{8,9},{9,8},{10,11... | collective-permute-start | bytes 196616 | tf_op jit(solution)/shard_map/ppermute | solution.py:33
  65.7 1.2 %collective-permute-start.18 = (bf16[2,128,128]{2,1,0:T(8,128)(2,1)S(1)}, bf16[2,128,128]{2,1,0:T(8,128)(2,1)S(1)}, u32[]{:S(2)}, u32[]{:S(2)}) collective-permute-start(bf16[2,128,128]{2,1,0:T(8,128)(2,1)S(1)} %get-tuple-element.68), channel_id=1, source_target_pairs={{0,2},{1,3},{2,0},{3,1},{4,6},{5,7},{6,4},{7,5},{8,10},{9,11},{10,... | collective-permute-start | bytes 196616 | tf_op jit(solution)/shard_map/ppermute | solution.py:33
  66.9 1.0 %collective-permute-start.19 = (bf16[2,128,128]{2,1,0:T(8,128)(2,1)S(1)}, bf16[2,128,128]{2,1,0:T(8,128)(2,1)S(1)}, u32[]{:S(2)}, u32[]{:S(2)}) collective-permute-start(bf16[2,128,128]{2,1,0:T(8,128)(2,1)S(1)} %get-tuple-element.69), channel_id=1, source_target_pairs={{0,3},{1,2},{2,1},{3,0},{4,7},{5,6},{6,5},{7,4},{8,11},{9,10},{10,... | collective-permute-start | bytes 196616 | tf_op jit(solution)/shard_map/ppermute | solution.py:33
  67.9 1.4 %coupling.3.refs_4_ = f32[128,128]{1,0:T(8,128)S(1)} custom-call(s32[1,4]{1,0:T(1,128)S(1)} %copy-done.1, bf16[8,128,128]{2,1,0:T(8,128)(2,1)S(1)} %stack.3.own_ref, bf16[8,128,128]{2,1,0:T(8,128)(2,1)S(1)} %collective-permute-done.20.next_ref, bf16[1,4,128,128]{3,2,1,0:T(8,128)(2,1)} %inter_ref.3, f32[1,128,128]{2,1,0:T(8,128)} %ints_ref.3), custom_call_target="tpu_custom_call" | custom-call | flops 33554432 | tf_op jit(solution)/shard_map/coupling/pallas_call | solution.py:290
  69.4 1.2 %collective-permute-done.18.refs_2_ = bf16[2,128,128]{2,1,0:T(8,128)(2,1)S(1)} collective-permute-done((bf16[2,128,128]{2,1,0:T(8,128)(2,1)S(1)}, bf16[2,128,128]{2,1,0:T(8,128)(2,1)S(1)}, u32[]{:S(2)}, u32[]{:S(2)}) %collective-permute-start.18) | collective-permute-done | bytes 65568 | tf_op jit(solution)/shard_map/ppermute | solution.py:33
  70.5 1.9 %collective-permute-done.19.refs_3_ = bf16[2,128,128]{2,1,0:T(8,128)(2,1)S(1)} collective-permute-done((bf16[2,128,128]{2,1,0:T(8,128)(2,1)S(1)}, bf16[2,128,128]{2,1,0:T(8,128)(2,1)S(1)}, u32[]{:S(2)}, u32[]{:S(2)}) %collective-permute-start.19) | collective-permute-done | bytes 65568 | tf_op jit(solution)/shard_map/ppermute | solution.py:33
  72.4 1.6 %collective-permute-start.21 = (bf16[1,128,128]{2,1,0:T(8,128)(2,1)S(1)}, bf16[1,128,128]{2,1,0:T(8,128)(2,1)S(1)}, u32[]{:S(2)}, u32[]{:S(2)}) collective-permute-start(bf16[1,128,128]{2,1,0:T(8,128)(2,1)S(1)} %get-tuple-element.72), channel_id=1, source_target_pairs={{0,4},{1,5},{2,6},{3,7},{4,0},{5,1},{6,2},{7,3},{8,12},{9,13},{10,... | collective-permute-start | bytes 98312 | tf_op jit(solution)/shard_map/ppermute | solution.py:33
  74.1 3.6 %collective-permute-done.21.refs_1_ = bf16[1,128,128]{2,1,0:T(8,128)(2,1)S(1)} collective-permute-done((bf16[1,128,128]{2,1,0:T(8,128)(2,1)S(1)}, bf16[1,128,128]{2,1,0:T(8,128)(2,1)S(1)}, u32[]{:S(2)}, u32[]{:S(2)}) %collective-permute-start.21) | collective-permute-done | bytes 32800 | tf_op jit(solution)/shard_map/ppermute | solution.py:33
  (42 shorter events, 6.4 us)
Async XLA Ops:
  1.3 5.9 %collective-permute-start = (f32[1,128]{1,0:T(1,128)S(1)}, f32[1,128]{1,0:T(1,128)S(1)}, u32[]{:S(2)}, u32[]{:S(2)}) collective-permute-start(f32[1,128]{1,0:T(1,128)S(1)} %broadcast_add_fusion.refs_6_.refs_3_), channel_id=1, source_target_pairs={{0,4},{1,5},{2,6},{3,7},{4,0},{5,1},{6,2},{7,3},{8,12},{9,13},{10,... | collective-permute-start | bytes 1544 | tf_op jit(solution)/shard_map/ppermute | solution.py:33
  5.3 7.1 %collective-permute-start.1 = (bf16[1,256,128]{2,1,0:T(8,128)(2,1)}, bf16[1,256,128]{2,1,0:T(8,128)(2,1)S(1)}, u32[]{:S(2)}, u32[]{:S(2)}) collective-permute-start(bf16[1,256,128]{2,1,0:T(8,128)(2,1)} %value_ref.1), channel_id=1, source_target_pairs={{0,4},{1,5},{2,6},{3,7},{4,0},{5,1},{6,2},{7,3},{8,12},{9,13},{10,... | collective-permute-start | bytes 196616 | tf_op jit(solution)/shard_map/ppermute | solution.py:33
  6.3 0.8 %copy-start = (bf16[1,256,128]{2,1,0:T(8,128)(2,1)S(1)}, bf16[1,256,128]{2,1,0:T(8,128)(2,1)}, u32[]{:S(2)}) copy-start(bf16[1,256,128]{2,1,0:T(8,128)(2,1)} %value_ref.1) | copy-start | bytes 196612
  7.2 9.6 %collective-permute-start.2 = (bf16[1,128,128]{2,1,0:T(8,128)(2,1)}, bf16[1,128,128]{2,1,0:T(8,128)(2,1)S(1)}, u32[]{:S(2)}, u32[]{:S(2)}) collective-permute-start(bf16[1,128,128]{2,1,0:T(8,128)(2,1)} %param.9), channel_id=1, source_target_pairs={{0,4},{1,5},{2,6},{3,7},{4,0},{5,1},{6,2},{7,3},{8,12},{9,13},{10,... | collective-permute-start | bytes 98312 | tf_op jit(solution)/shard_map/ppermute | solution.py:33
  12.4 6.3 %collective-permute-start.6 = (bf16[2,256,128]{2,1,0:T(8,128)(2,1)S(1)}, bf16[2,256,128]{2,1,0:T(8,128)(2,1)S(1)}, u32[]{:S(2)}, u32[]{:S(2)}) collective-permute-start(bf16[2,256,128]{2,1,0:T(8,128)(2,1)S(1)} %join.1.refs_1_), channel_id=1, source_target_pairs={{0,1},{1,0},{2,3},{3,2},{4,5},{5,4},{6,7},{7,6},{8,9},{9,8},{10,11... | collective-permute-start | bytes 393224 | tf_op jit(solution)/shard_map/ppermute | solution.py:33
  14.1 6.4 %collective-permute-start.7 = (bf16[2,256,128]{2,1,0:T(8,128)(2,1)S(1)}, bf16[2,256,128]{2,1,0:T(8,128)(2,1)S(1)}, u32[]{:S(2)}, u32[]{:S(2)}) collective-permute-start(bf16[2,256,128]{2,1,0:T(8,128)(2,1)S(1)} %join.1.refs_1_), channel_id=1, source_target_pairs={{0,2},{1,3},{2,0},{3,1},{4,6},{5,7},{6,4},{7,5},{8,10},{9,11},{10,... | collective-permute-start | bytes 393224 | tf_op jit(solution)/shard_map/ppermute | solution.py:33
  14.3 6.9 %collective-permute-start.8 = (bf16[2,256,128]{2,1,0:T(8,128)(2,1)S(1)}, bf16[2,256,128]{2,1,0:T(8,128)(2,1)S(1)}, u32[]{:S(2)}, u32[]{:S(2)}) collective-permute-start(bf16[2,256,128]{2,1,0:T(8,128)(2,1)S(1)} %join.1.refs_1_), channel_id=1, source_target_pairs={{0,3},{1,2},{2,1},{3,0},{4,7},{5,6},{6,5},{7,4},{8,11},{9,10},{10,... | collective-permute-start | bytes 393224 | tf_op jit(solution)/shard_map/ppermute | solution.py:33
  16.8 12.3 %collective-permute-start.3 = (bf16[2,128,128]{2,1,0:T(8,128)(2,1)S(1)}, bf16[2,128,128]{2,1,0:T(8,128)(2,1)S(1)}, u32[]{:S(2)}, u32[]{:S(2)}) collective-permute-start(bf16[2,128,128]{2,1,0:T(8,128)(2,1)S(1)} %constant_dynamic-update-slice_fusion.refs_0_.refs_2_), channel_id=1, source_target_pairs={{0,1},{1,0},{2,3},{3,2},{4,5},{5,4},{6,7},{7,6},{8,9},{9,8},{10,11... | collective-permute-start | bytes 196616 | tf_op jit(solution)/shard_map/ppermute | solution.py:33
  18.5 10.6 %collective-permute-start.4 = (bf16[2,128,128]{2,1,0:T(8,128)(2,1)S(1)}, bf16[2,128,128]{2,1,0:T(8,128)(2,1)S(1)}, u32[]{:S(2)}, u32[]{:S(2)}) collective-permute-start(bf16[2,128,128]{2,1,0:T(8,128)(2,1)S(1)} %constant_dynamic-update-slice_fusion.refs_0_.refs_2_), channel_id=1, source_target_pairs={{0,2},{1,3},{2,0},{3,1},{4,6},{5,7},{6,4},{7,5},{8,10},{9,11},{10,... | collective-permute-start | bytes 196616 | tf_op jit(solution)/shard_map/ppermute | solution.py:33
  18.8 10.3 %collective-permute-start.5 = (bf16[2,128,128]{2,1,0:T(8,128)(2,1)S(1)}, bf16[2,128,128]{2,1,0:T(8,128)(2,1)S(1)}, u32[]{:S(2)}, u32[]{:S(2)}) collective-permute-start(bf16[2,128,128]{2,1,0:T(8,128)(2,1)S(1)} %constant_dynamic-update-slice_fusion.refs_0_.refs_2_), channel_id=1, source_target_pairs={{0,3},{1,2},{2,1},{3,0},{4,7},{5,6},{6,5},{7,4},{8,11},{9,10},{10,... | collective-permute-start | bytes 196616 | tf_op jit(solution)/shard_map/ppermute | solution.py:33
  21.1 18.6 %copy-start.2 = (f32[1,128]{1,0:T(1,128)S(1)}, f32[1,128]{1,0:T(1,128)}, u32[]{:S(2)}) copy-start(f32[1,128]{1,0:T(1,128)} %param.14) | copy-start | bytes 1540
  21.1 18.8 %copy-start.1 = (s32[1,4]{1,0:T(1,128)S(1)}, s32[1,4]{1,0:T(1,128)}, u32[]{:S(2)}) copy-start(s32[1,4]{1,0:T(1,128)} %near.3) | copy-start | bytes 52
  29.1 10.8 %collective-permute-start.12 = (bf16[8,128,128]{2,1,0:T(8,128)(2,1)S(1)}, bf16[8,128,128]{2,1,0:T(8,128)(2,1)S(1)}, u32[]{:S(2)}, u32[]{:S(2)}) collective-permute-start(bf16[8,128,128]{2,1,0:T(8,128)(2,1)S(1)} %stack.2.own_ref), channel_id=1, source_target_pairs={{8,0},{16,8},{24,16},{9,1},{17,9},{25,17},{10,2},{18,10},{26,18},{... | collective-permute-start | bytes 786440 | tf_op jit(solution)/shard_map/ppermute | solution.py:90
  36.1 5.2 %collective-permute-start.9 = (bf16[2,128,128]{2,1,0:T(8,128)(2,1)S(1)}, bf16[2,128,128]{2,1,0:T(8,128)(2,1)S(1)}, u32[]{:S(2)}, u32[]{:S(2)}) collective-permute-start(bf16[2,128,128]{2,1,0:T(8,128)(2,1)S(1)} %get-tuple-element.55), channel_id=1, source_target_pairs={{0,1},{1,0},{2,3},{3,2},{4,5},{5,4},{6,7},{7,6},{8,9},{9,8},{10,11... | collective-permute-start | bytes 196616 | tf_op jit(solution)/shard_map/ppermute | solution.py:33
  37.8 5.0 %collective-permute-start.10 = (bf16[2,128,128]{2,1,0:T(8,128)(2,1)S(1)}, bf16[2,128,128]{2,1,0:T(8,128)(2,1)S(1)}, u32[]{:S(2)}, u32[]{:S(2)}) collective-permute-start(bf16[2,128,128]{2,1,0:T(8,128)(2,1)S(1)} %get-tuple-element.56), channel_id=1, source_target_pairs={{0,2},{1,3},{2,0},{3,1},{4,6},{5,7},{6,4},{7,5},{8,10},{9,11},{10,... | collective-permute-start | bytes 196616 | tf_op jit(solution)/shard_map/ppermute | solution.py:33
  38.7 5.5 %collective-permute-start.11 = (bf16[2,128,128]{2,1,0:T(8,128)(2,1)S(1)}, bf16[2,128,128]{2,1,0:T(8,128)(2,1)S(1)}, u32[]{:S(2)}, u32[]{:S(2)}) collective-permute-start(bf16[2,128,128]{2,1,0:T(8,128)(2,1)S(1)} %get-tuple-element.57), channel_id=1, source_target_pairs={{0,3},{1,2},{2,1},{3,0},{4,7},{5,6},{6,5},{7,4},{8,11},{9,10},{10,... | collective-permute-start | bytes 196616 | tf_op jit(solution)/shard_map/ppermute | solution.py:33
  44.3 6.2 %collective-permute-start.13 = (bf16[2,128,128]{2,1,0:T(8,128)(2,1)S(1)}, bf16[2,128,128]{2,1,0:T(8,128)(2,1)S(1)}, u32[]{:S(2)}, u32[]{:S(2)}) collective-permute-start(bf16[2,128,128]{2,1,0:T(8,128)(2,1)S(1)} %get-tuple-element.61), channel_id=1, source_target_pairs={{0,4},{1,5},{2,6},{3,7},{4,0},{5,1},{6,2},{7,3},{8,12},{9,13},{10,... | collective-permute-start | bytes 196616 | tf_op jit(solution)/shard_map/ppermute | solution.py:33
  50.5 4.3 %collective-permute-start.14 = (bf16[2,128,128]{2,1,0:T(8,128)(2,1)S(1)}, bf16[2,128,128]{2,1,0:T(8,128)(2,1)S(1)}, u32[]{:S(2)}, u32[]{:S(2)}) collective-permute-start(bf16[2,128,128]{2,1,0:T(8,128)(2,1)S(1)} %finish.2.refs_0_.refs_2_), channel_id=1, source_target_pairs={{0,1},{1,0},{2,3},{3,2},{4,5},{5,4},{6,7},{7,6},{8,9},{9,8},{10,11... | collective-permute-start | bytes 196616 | tf_op jit(solution)/shard_map/ppermute | solution.py:33
  52.1 4.3 %collective-permute-start.15 = (bf16[2,128,128]{2,1,0:T(8,128)(2,1)S(1)}, bf16[2,128,128]{2,1,0:T(8,128)(2,1)S(1)}, u32[]{:S(2)}, u32[]{:S(2)}) collective-permute-start(bf16[2,128,128]{2,1,0:T(8,128)(2,1)S(1)} %finish.2.refs_0_.refs_2_), channel_id=1, source_target_pairs={{0,2},{1,3},{2,0},{3,1},{4,6},{5,7},{6,4},{7,5},{8,10},{9,11},{10,... | collective-permute-start | bytes 196616 | tf_op jit(solution)/shard_map/ppermute | solution.py:33
  52.2 5.2 %collective-permute-start.16 = (bf16[2,128,128]{2,1,0:T(8,128)(2,1)S(1)}, bf16[2,128,128]{2,1,0:T(8,128)(2,1)S(1)}, u32[]{:S(2)}, u32[]{:S(2)}) collective-permute-start(bf16[2,128,128]{2,1,0:T(8,128)(2,1)S(1)} %finish.2.refs_0_.refs_2_), channel_id=1, source_target_pairs={{0,3},{1,2},{2,1},{3,0},{4,7},{5,6},{6,5},{7,4},{8,11},{9,10},{10,... | collective-permute-start | bytes 196616 | tf_op jit(solution)/shard_map/ppermute | solution.py:33
  57.3 10.6 %collective-permute-start.20 = (bf16[8,128,128]{2,1,0:T(8,128)(2,1)S(1)}, bf16[8,128,128]{2,1,0:T(8,128)(2,1)S(1)}, u32[]{:S(2)}, u32[]{:S(2)}) collective-permute-start(bf16[8,128,128]{2,1,0:T(8,128)(2,1)S(1)} %stack.3.own_ref), channel_id=1, source_target_pairs={{8,0},{16,8},{24,16},{9,1},{17,9},{25,17},{10,2},{18,10},{26,18},{... | collective-permute-start | bytes 786440 | tf_op jit(solution)/shard_map/ppermute | solution.py:90
  64.4 5.0 %collective-permute-start.17 = (bf16[2,128,128]{2,1,0:T(8,128)(2,1)S(1)}, bf16[2,128,128]{2,1,0:T(8,128)(2,1)S(1)}, u32[]{:S(2)}, u32[]{:S(2)}) collective-permute-start(bf16[2,128,128]{2,1,0:T(8,128)(2,1)S(1)} %get-tuple-element.67), channel_id=1, source_target_pairs={{0,1},{1,0},{2,3},{3,2},{4,5},{5,4},{6,7},{7,6},{8,9},{9,8},{10,11... | collective-permute-start | bytes 196616 | tf_op jit(solution)/shard_map/ppermute | solution.py:33
  65.7 4.8 %collective-permute-start.18 = (bf16[2,128,128]{2,1,0:T(8,128)(2,1)S(1)}, bf16[2,128,128]{2,1,0:T(8,128)(2,1)S(1)}, u32[]{:S(2)}, u32[]{:S(2)}) collective-permute-start(bf16[2,128,128]{2,1,0:T(8,128)(2,1)S(1)} %get-tuple-element.68), channel_id=1, source_target_pairs={{0,2},{1,3},{2,0},{3,1},{4,6},{5,7},{6,4},{7,5},{8,10},{9,11},{10,... | collective-permute-start | bytes 196616 | tf_op jit(solution)/shard_map/ppermute | solution.py:33
  66.9 5.5 %collective-permute-start.19 = (bf16[2,128,128]{2,1,0:T(8,128)(2,1)S(1)}, bf16[2,128,128]{2,1,0:T(8,128)(2,1)S(1)}, u32[]{:S(2)}, u32[]{:S(2)}) collective-permute-start(bf16[2,128,128]{2,1,0:T(8,128)(2,1)S(1)} %get-tuple-element.69), channel_id=1, source_target_pairs={{0,3},{1,2},{2,1},{3,0},{4,7},{5,6},{6,5},{7,4},{8,11},{9,10},{10,... | collective-permute-start | bytes 196616 | tf_op jit(solution)/shard_map/ppermute | solution.py:33
  72.4 5.2 %collective-permute-start.21 = (bf16[1,128,128]{2,1,0:T(8,128)(2,1)S(1)}, bf16[1,128,128]{2,1,0:T(8,128)(2,1)S(1)}, u32[]{:S(2)}, u32[]{:S(2)}) collective-permute-start(bf16[1,128,128]{2,1,0:T(8,128)(2,1)S(1)} %get-tuple-element.72), channel_id=1, source_target_pairs={{0,4},{1,5},{2,6},{3,7},{4,0},{5,1},{6,2},{7,3},{8,12},{9,13},{10,... | collective-permute-start | bytes 98312 | tf_op jit(solution)/shard_map/ppermute | solution.py:33
